TPU v7x, 32 devices: a whole 2x2x4 slice. The times are simulated.
32 devices in a mesh: pages: 4 (over y, x), blk: 8 (over z, core).
Axes of the slice: x: 2, y: 2, z: 4, core: 2. Of those that a mesh axis runs over, the one named last changes fastest.
Arguments:
- new_hidden: bfloat16 [32, 6144], P('pages', 'blk'), may hold values from -6 to 6
- attn_gain: float32 [6144], replicated, may hold values from 0.1 to 1.9
- mlp_gain: float32 [6144], replicated, may hold values from 0.1 to 1.9
- qkv_weight: bfloat16 [6144, 18432], P(None, 'blk'), may hold values from -0.078125 to 0.078125
- dense_weight: bfloat16 [6144, 6144], P('blk'), may hold values from -0.078125 to 0.078125
- in_weight: bfloat16 [6144, 24576], P(None, ('pages', 'blk')), may hold values from -0.078125 to 0.078125
- out_weight: bfloat16 [24576, 6144], P(('pages', 'blk')), may hold values from -0.078125 to 0.078125
- page_store: bfloat16 [384, 16, 12288], P(('pages', 'blk')), may hold values from -420 to 420
- held_states: bfloat16 [32, 8, 6144], P(('pages', 'blk')), may hold values from -6 to 6
- fold_weights: float32 [8, 16], replicated, may hold values from 0.02 to 0.14
- page_table: int32 [32, 12], replicated, may hold values from 0 to 383, as said below
- lengths: int32 [32], P('pages'), may hold values from 81 to 192, as said below
- keep_slots: int32 [32, 5], P('pages'), may hold values from 0 to 11, as said below
- fold_index: int32 [32, 12], P('pages'), may hold values from 0 to 7
- recompute_list: int32 [32, 8], P('pages'), may hold values from 0 to 79, as said below
Outputs:
- update: bfloat16 [32, 6144], P('pages', 'blk')
- folded: bfloat16 [32, 12, 12288], P('pages', None, 'blk')
Inputs may be any that keep to these rules, and one draw needn't show every extreme that they name: `page_table`: every page id appears exactly once; the device of index s along pages+blk holds pages s*12 to s*12 + 11, and exactly 3 of them belong to requests of each group of 8 consecutive requests. `lengths`: one request in every draw holds 192 tokens. `keep_slots`: A request's kept slots are distinct, ascending, and all below lengths // 16. `recompute_list`: A request's entries are distinct and ascending.
All inputs are finite; a program needn't handle non-finite values.
Results may differ from a plain program's by a relative error of at most 0.024.
Values may be sent and summed in bfloat16 or wider, within the bound.
No kernel may reach another device: no remote copies, remote signals or barrier semaphores. Data moves between devices by JAX's collectives and lax.ppermute only.
A program may use at most 192 MiB of HBM per device.

v0:
```python
import math

import jax
import jax.numpy as jnp
from jax import lax
from jax.sharding import PartitionSpec as P

D = 6144
H = 64
HD = 96
ROT = 24
PAGE = 16
PPR = 12
KP = 5
NREC = 8
NF = 8


EPSILON = 1e-05
ROT_BASE = 10000.0


def layer_norm(values, scale_gain):
    values = values.astype(jnp.float32)
    centered = values - jnp.mean(values, axis=-1, keepdims=True)
    spread = jnp.mean(centered * centered, axis=-1, keepdims=True)
    return centered * lax.rsqrt(spread + EPSILON) * scale_gain


def rotate(values, positions):
    half_rot = ROT // 2
    frequency = ROT_BASE ** (-2.0 * jnp.arange(half_rot, dtype=jnp.float32) / ROT)
    angles = positions.astype(jnp.float32)[..., None] * frequency
    cos_part = jnp.cos(angles)
    sin_part = jnp.sin(angles)
    lower_part = values[..., :half_rot]
    upper_part = values[..., half_rot:ROT]
    return jnp.concatenate(
        [
            lower_part * cos_part - upper_part * sin_part,
            upper_part * cos_part + lower_part * sin_part,
            values[..., ROT:],
        ],
        axis=-1,
    )


def on_device(
    new_hidden,
    attn_gain,
    mlp_gain,
    qkv_weight,
    dense_weight,
    in_weight,
    out_weight,
    page_store,
    held_states,
    fold_weights,
    page_table,
    lengths,
    keep_slots,
    fold_index,
    recompute_list,
):
    n_pages = lax.axis_size("pages")
    n_blk = lax.axis_size("blk")
    group = lax.axis_index("pages")
    device = lax.axis_index(("pages", "blk"))
    n_devices = n_pages * n_blk
    group_rows = lengths.shape[0]
    every_count = page_table.shape[0]
    heads = H // n_blk
    width = heads * 2 * HD
    pages_dev = page_store.shape[0]
    per_group = pages_dev // n_pages
    kept_count = KP * PAGE
    scale = 1.0 / math.sqrt(HD)
    whole = lax.all_gather(new_hidden, "blk", axis=1, tiled=True)
    normed_attn = layer_norm(whole, attn_gain).astype(jnp.bfloat16)
    normed_mlp = layer_norm(whole, mlp_gain).astype(jnp.bfloat16)
    every_row = lax.all_gather(normed_mlp, "pages", axis=0, tiled=True)
    key_weight = qkv_weight.reshape(D, heads, 3, HD)[:, :, 1, :].reshape(D, heads * HD)
    piece = lax.all_gather(held_states, "blk", axis=0, tiled=True)
    count = piece.shape[0]
    normed = layer_norm(piece.reshape(count * NREC, D), attn_gain).astype(jnp.bfloat16)
    fresh_keys = jnp.dot(normed, key_weight, preferred_element_type=jnp.float32).reshape(
        count, NREC, heads * HD
    )
    rec_slot = jnp.take_along_axis(keep_slots, recompute_list // PAGE, axis=1)
    rec_pos = rec_slot * PAGE + recompute_list % PAGE
    fresh_keys = rotate(
        fresh_keys.reshape(group_rows, NREC, heads, HD), rec_pos[:, :, None]
    ).astype(jnp.bfloat16)
    projected = jnp.dot(normed_attn, qkv_weight, preferred_element_type=jnp.float32).reshape(
        group_rows, heads, 3, HD
    )
    new_pos = lengths[:, None]
    query = rotate(projected[:, :, 0], new_pos).astype(jnp.bfloat16)
    new_key = rotate(projected[:, :, 1], new_pos).astype(jnp.bfloat16)
    new_value = projected[:, :, 2].astype(jnp.bfloat16)
    own_score = jnp.sum(query.astype(jnp.float32) * new_key.astype(jnp.float32), axis=-1) * scale
    slot_total = every_count * PPR
    flat_table = page_table.reshape(-1)
    slot_numbers = jnp.arange(slot_total, dtype=jnp.int32)
    owner_request = jnp.zeros((slot_total,), jnp.int32).at[flat_table].set(slot_numbers // PPR)
    owner_group = (owner_request // group_rows).reshape(n_devices, pages_dev)
    local_index = jnp.arange(pages_dev, dtype=jnp.int32)
    my_groups = lax.dynamic_index_in_dim(owner_group, device, 0, keepdims=False)
    in_group = (owner_group == group).astype(jnp.int32)
    rank = jnp.cumsum(in_group, axis=1) - in_group
    my_table = lax.dynamic_slice_in_dim(page_table, group * group_rows, group_rows, 0)
    place = my_table // pages_dev * per_group + rank.reshape(-1)[my_table]
    slot_ids = jnp.arange(PPR, dtype=jnp.int32)
    token_ids = jnp.arange(PAGE, dtype=jnp.int32)
    fold_choices = jnp.arange(NF, dtype=jnp.int32)
    send_order = jnp.argsort(my_groups * pages_dev + local_index)
    outgoing = page_store[send_order].reshape(n_pages, per_group, PAGE, n_blk, width)
    outgoing = jnp.transpose(outgoing, (0, 3, 1, 2, 4))
    incoming = lax.all_to_all(
        outgoing.reshape(n_devices, per_group, PAGE, width),
        ("pages", "blk"),
        split_axis=0,
        concat_axis=0,
        tiled=True,
    )
    incoming = incoming.reshape(n_devices * per_group, PAGE, width)
    arrived = incoming[place.reshape(-1)].reshape(group_rows, PPR, PAGE, width)
    is_kept = jnp.any(keep_slots[:, :, None] == slot_ids[None, None, :], axis=1)
    dropped = jnp.logical_and(jnp.logical_not(is_kept), slot_ids[None, :] * PAGE < lengths[:, None])
    live = slot_ids[None, :, None] * PAGE + token_ids[None, None, :] < lengths[:, None, None]
    choose = (fold_index[:, :, None] == fold_choices[None, None, :]).astype(jnp.float32)
    weight_rows = jnp.einsum("rjf,ft->rjt", choose, fold_weights, precision=lax.Precision.HIGHEST)
    weight_rows = jnp.where(jnp.logical_and(live, dropped[:, :, None]), weight_rows, 0.0)
    folded = jnp.einsum(
        "rjt,rjtc->rjc", weight_rows, arrived.astype(jnp.float32), precision=lax.Precision.HIGHEST
    ).astype(jnp.bfloat16)
    kept_index = (jnp.arange(group_rows, dtype=jnp.int32)[:, None] * PPR + keep_slots).reshape(-1)
    kept = arrived.reshape(group_rows * PPR, PAGE, width)[kept_index].reshape(
        group_rows, kept_count, heads, 2, HD
    )
    hits = recompute_list[:, :, None] == jnp.arange(kept_count, dtype=jnp.int32)[None, None, :]
    placed = jnp.einsum(
        "rnk,rnhd->rkhd", hits.astype(jnp.bfloat16), fresh_keys, preferred_element_type=jnp.float32
    ).astype(jnp.bfloat16)
    touched = jnp.any(hits, axis=1)
    keys = jnp.where(touched[:, :, None, None], placed, kept[:, :, :, 0])
    values = kept[:, :, :, 1]
    fold_pairs = folded.reshape(group_rows, PPR, heads, 2, HD)
    kept_scores = (
        jnp.einsum("rhd,rkhd->rhk", query, keys, preferred_element_type=jnp.float32) * scale
    )
    fold_scores = (
        jnp.einsum(
            "rhd,rjhd->rhj", query, fold_pairs[:, :, :, 0], preferred_element_type=jnp.float32
        )
        * scale
    )
    fold_scores = jnp.where(dropped[:, None, :], fold_scores, -1e30)
    top = jnp.maximum(
        jnp.maximum(jnp.max(kept_scores, axis=-1), jnp.max(fold_scores, axis=-1)), own_score
    )
    kept_exp = jnp.exp(kept_scores - top[..., None])
    fold_exp = jnp.exp(fold_scores - top[..., None])
    own_exp = jnp.exp(own_score - top)
    total = jnp.sum(kept_exp, axis=-1) + jnp.sum(fold_exp, axis=-1) + own_exp
    kept_prob = (kept_exp / total[..., None]).astype(jnp.bfloat16)
    fold_prob = (fold_exp / total[..., None]).astype(jnp.bfloat16)
    own_prob = (own_exp / total).astype(jnp.bfloat16)
    mixed = jnp.einsum("rhk,rkhd->rhd", kept_prob, values, preferred_element_type=jnp.float32)
    mixed = mixed + jnp.einsum(
        "rhj,rjhd->rhd", fold_prob, fold_pairs[:, :, :, 1], preferred_element_type=jnp.float32
    )
    mixed = mixed + own_prob.astype(jnp.float32)[..., None] * new_value.astype(jnp.float32)
    attended = mixed.reshape(group_rows, heads * HD).astype(jnp.bfloat16)
    attn_part = jnp.dot(attended, dense_weight, preferred_element_type=jnp.float32)
    activated = jax.nn.gelu(
        jnp.dot(every_row, in_weight, preferred_element_type=jnp.float32), approximate=False
    ).astype(jnp.bfloat16)
    mlp_part = jnp.dot(activated, out_weight, preferred_element_type=jnp.float32)
    row_share = lax.psum_scatter(
        mlp_part.astype(jnp.bfloat16), "pages", scatter_dimension=0, tiled=True
    ).astype(jnp.float32)
    summed = lax.psum_scatter(
        (row_share + attn_part).astype(jnp.bfloat16), "blk", scatter_dimension=1, tiled=True
    )
    return (summed, folded)


def solution(mesh):
    in_specs = (
        P("pages", "blk"),
        P(),
        P(),
        P(None, "blk"),
        P("blk", None),
        P(None, ("pages", "blk")),
        P(("pages", "blk"), None),
        P(("pages", "blk"), None, None),
        P(("pages", "blk"), None, None),
        P(),
        P(),
        P("pages"),
        P("pages", None),
        P("pages", None),
        P("pages", None),
    )
    out_specs = (P("pages", "blk"), P("pages", None, "blk"))
    return jax.shard_map(
        on_device, mesh=mesh, in_specs=in_specs, out_specs=out_specs, check_vma=False
    )
```

profile of v0, /device:TPU:0, one launch (start us, length us, event | category | flops | bytes accessed | tf_op | source)
XLA Modules:
  0.0 322.9 jit_solution(10986200738607406724)
XLA Ops:
  7.2 0.8 copy.42
  8.1 2.9 scatter_custom_fusion
  11.2 1.2 sort.17
  12.4 5.5 %gather_fusion = bf16[12,16,12288]{2,1,0:T(8,128)(2,1)} fusion(bf16[12,16,12288]{2,1,0:T(8,128)(2,1)} %param.22, s32[1024]{0:T(1024)S(1)} %pad_clamp_fusion.3), kind=kCustom, calls=%fused_computation | custom fusion | bytes 9437232 | tf_op jit(solution)/shard_map/gather | solution.py:117
  17.9 4.2 %copy.68 = bf16[24,8,8,1536]{3,2,1,0:T(8,128)(2,1)S(1)} copy(bf16[24,8,8,1536]{3,1,2,0:T(8,128)(2,1)} %bitcast.97) | data formatting | bytes 9437184
  22.2 3.7 %copy.43 = bf16[4,8,3,16,1536]{4,3,2,1,0:T(8,128)(2,1)} copy(bf16[4,8,3,16,1536]{4,1,3,2,0:T(8,128)(2,1)S(1)} %bitcast.98) | data formatting | bytes 9437184 | tf_op jit(solution)/shard_map/transpose | solution.py:118
  25.9 7.4 %all-to-all-start = ((bf16[32,3,16,1536]{3,2,1,0:T(8,128)(2,1)}), bf16[32,3,16,1536]{3,2,1,0:T(8,128)(2,1)}, u32[]{:S(2)}, u32[]{:S(2)}) async-start(bf16[32,3,16,1536]{3,2,1,0:T(8,128)(2,1)} %bitcast.96), calls=%async_computation | async-start | bytes 9437184 | tf_op jit(solution)/shard_map/all_to_all | solution.py:119
  33.4 111.0 %all_gather.9 = bf16[8,6144]{1,0:T(8,128)(2,1)S(1)} all-gather(bf16[8,768]{1,0:T(8,128)(2,1)S(1)} %copy-done.7), channel_id=1, replica_groups=mesh['pages'=4,'blk'=8] {'blk'}, dimensions={1}, use_global_device_ids=true | all-gather | bytes 110592 | tf_op jit(solution)/shard_map/all_gather | solution.py:78
  144.9 9.7 %all_gather.10 = bf16[32,6144]{1,0:T(8,128)(2,1)S(1)} all-gather(bf16[8,6144]{1,0:T(8,128)(2,1)S(1)} %fusion.31), channel_id=1, replica_groups=mesh['pages'=4,'blk'=8] {'pages'}, dimensions={0}, use_global_device_ids=true | all-gather | bytes 491520 | tf_op jit(solution)/shard_map/all_gather | solution.py:81
  154.6 11.1 %convolution_convert_fusion = bf16[32,6144]{1,0:T(8,128)(2,1)} fusion(bf16[768,6144]{1,0:T(8,128)(2,1)} %param.21, bf16[32,6144]{1,0:T(8,128)(2,1)S(1)} %all_gather.10, bf16[6144,768]{1,0:T(8,128)(2,1)} %param.20), kind=kOutput, calls=%fused_computation.8 | convolution fusion | flops 605773824 | bytes 19660800 | tf_op jit(solution)/shard_map/dot_general | solution.py:179
  166.3 0.7 gather_fusion.4
  167.5 1.3 gather_fusion.1
  169.0 36.7 %copy.41 = bf16[6144,2304]{0,1:T(8,128)(2,1)} copy(bf16[6144,2304]{1,0:T(8,128)(2,1)} %param.18) | data formatting | bytes 56623104 | tf_op args[3]
  205.7 11.1 %fusion.47 = f32[8,2304]{1,0:T(8,128)S(1)} fusion(bf16[6144,2304]{1,0:T(8,128)(2,1)} %param.18, bf16[8,6144]{1,0:T(8,128)(2,1)S(1)} %all_gather.9, f32[6144]{0:T(1024)S(1)} %copy-done.4, f32[8]{0:T(128)S(1)} %add_rsqrt_fusion.1, f32[8]{0:T(128)S(1)} %broadcast_multiply_fusion.1), kind=kOutput, calls=%fused_computation.61 | convolution fusion | flops 226738176 | bytes 28508224 | tf_op jit(solution)/shard_map/dot_general | solution.py:94
  217.2 15.7 %all_gather.11 = bf16[8,8,6144]{2,1,0:T(8,128)(2,1)S(1)} all-gather(bf16[1,8,6144]{2,1,0:T(8,128)(2,1)S(1)} %copy-done.3), channel_id=1, replica_groups=mesh['pages'=4,'blk'=8] {'blk'}, dimensions={0}, use_global_device_ids=true | all-gather | bytes 884736 | tf_op jit(solution)/shard_map/all_gather | solution.py:83
  233.1 0.4 fusion.4
  233.5 6.1 %fusion = f32[8,8,8,96]{3,1,2,0:T(8,128)S(1)} fusion(bf16[6144,8,3,96]{0,3,2,1:T(8,128)(2,1)} %bitcast.95, bf16[8,8,6144]{2,1,0:T(8,128)(2,1)S(1)} %all_gather.11, f32[6144]{0:T(1024)S(1)} %copy-done.4, f32[8,8]{1,0:T(8,128)S(1)} %add_rsqrt_fusion, f32[8,8]{1,0:T(8,128)S(1)} %broadcast_multiply_fusion), kind=kOutput, calls=%fused_computation.7 | convolution fusion | flops 605945856 | bytes 10445312 | tf_op jit(solution)/shard_map/dot_general | solution.py:86
  239.7 0.6 dynamic-slice
  242.4 0.9 subtract_convert_fusion
  243.2 5.5 %gather_fusion.2 = bf16[96,16,1536]{2,1,0:T(8,128)(2,1)} fusion(bf16[96,16,1536]{2,1,0:T(8,128)(2,1)} %bitcast.15, s32[1024]{0:T(1024)S(1)} %pad_clamp_fusion.1), kind=kCustom, calls=%fused_computation.2 | custom fusion | bytes 9437568 | tf_op jit(solution)/shard_map/gather | solution.py:127
  248.7 4.4 %fusion.60 = bf16[8,12,1,1536]{3,2,1,0:T(2,128)(2,1)S(1)} fusion(bf16[8,12,16,1536]{3,2,1,0:T(8,128)(2,1)} %bitcast.94, f32[8,12,16,1]{2,1,0,3:T(8,128)S(1)} %fusion.15), kind=kOutput, calls=%fused_computation.80 | convolution fusion | flops 28311552 | bytes 5019648 | tf_op jit(solution)/shard_map/rjt,rjtc->rjc/dot_general | solution.py:134
  253.4 0.3 reshape.423
  253.7 0.8 fusion.163
  254.5 0.3 fusion.24
  254.9 4.4 %gather_fusion.3 = bf16[40,16,1536]{2,1,0:T(8,128)(2,1)} fusion(bf16[96,16,1536]{2,1,0:T(8,128)(2,1)} %gather_fusion.2, s32[1024]{0:T(1024)S(1)} %pad_clamp_fusion), kind=kCustom, calls=%fused_computation.3 | custom fusion | bytes 3932320 | tf_op jit(solution)/shard_map/gather | solution.py:138
  259.3 8.4 %reshape.421 = bf16[8,80,8,2,96]{4,3,2,1,0:T(2,128)(2,1)S(1)} reshape(bf16[40,16,1536]{2,1,0:T(8,128)(2,1)} %gather_fusion.3) | data formatting | bytes 3932160 | tf_op jit(solution)/shard_map/reshape | solution.py:138
  267.8 5.8 %fusion.162 = (bf16[8,80,8,1,96]{4,3,2,1,0:T(2,128)(2,1)}, bf16[8,80,8,1,96]{4,3,2,1,0:T(2,128)(2,1)}) fusion(bf16[8,80,8,2,96]{4,3,2,1,0:T(2,128)(2,1)S(1)} %reshape.421), kind=kLoop, calls=%fused_computation.247 | loop fusion | bytes 3932160 | tf_op jit(solution)/shard_map/slice | solution.py:146
  273.5 3.6 %fusion.8 = f32[8,8,1,80]{3,2,1,0:T(1,128)S(1)} fusion(bf16[8,80,8,1,96]{4,3,2,1,0:T(2,128)(2,1)} %get-tuple-element.6, pred[8,80]{1,0:T(8,128)(4,1)S(1)} %fusion.96, bf16[8,8,8,72]{3,1,2,0:T(8,128)(2,1)S(1)} %slice.119, bf16[8,8,8,12]{3,1,2,0:T(8,128)(2,1)} %get-tuple-element.11, bf16[8,8,8,12]{3,1,2,0:T(8,128)(2,1)} %get-tuple-element.10, ...), kind=kOutput, calls=%fused_computation.20 | convolution fusion | flops 10130432 | bytes 1115008 | tf_op jit(solution)/shard_map/rhd,rkhd->rhk/dot_general | solution.py:150
  277.8 2.2 fusion.9
  280.0 0.3 fusion.21
  280.5 5.6 %fusion.1 = bf16[8,6144]{1,0:T(8,128)(2,1)} fusion(bf16[8,768]{1,0:T(8,128)(2,1)S(1)} %convert_element_type.122, bf16[768,6144]{1,0:T(8,128)(2,1)} %param.19, bf16[32,6144]{1,0:T(8,128)(2,1)} %all-reduce.3.cloned.1.call-done, u32[]{:T(128)S(6)} %multiply.38), kind=kOutput, calls=%fused_computation.10 | convolution fusion | flops 75644928 | bytes 9646084 | tf_op jit(solution)/shard_map/dot_general | solution.py:175
  286.2 29.9 %reduce-scatter.2.cloned.1.call-done = bf16[8,768]{1,0:T(8,128)(2,1)} async-done(((bf16[8,6144]{1,0:T(8,128)(2,1)}), bf16[8,768]{1,0:T(8,128)(2,1)}) %reduce-scatter.2.cloned.1.call-update) | async-done | bytes 12304 | tf_op jit(solution)/shard_map/reduce_scatter | solution.py:183
  (97 shorter events, 5.2 us)
Async XLA Ops:
  7.2 234.7 %copy-start = (f32[8,16]{1,0:T(8,128)S(1)}, f32[8,16]{1,0:T(8,128)}, u32[]{:S(2)}) copy-start(f32[8,16]{1,0:T(8,128)} %param.24) | copy-start | bytes 1540
  25.9 7.5 %copy-start.7 = (bf16[8,768]{1,0:T(8,128)(2,1)S(1)}, bf16[8,768]{1,0:T(8,128)(2,1)}, u32[]{:S(2)}) copy-start(bf16[8,768]{1,0:T(8,128)(2,1)} %param.15) | copy-start | bytes 36868
  25.9 118.9 %copy-start.6 = (f32[6144]{0:T(1024)S(1)}, f32[6144]{0:T(1024)}, u32[]{:S(2)}) copy-start(f32[6144]{0:T(1024)} %param.17) | copy-start | bytes 73732
  25.9 217.3 %all-to-all-start = ((bf16[32,3,16,1536]{3,2,1,0:T(8,128)(2,1)}), bf16[32,3,16,1536]{3,2,1,0:T(8,128)(2,1)}, u32[]{:S(2)}, u32[]{:S(2)}) async-start(bf16[32,3,16,1536]{3,2,1,0:T(8,128)(2,1)} %bitcast.96), calls=%async_computation | async-start | bytes 9437184 | tf_op jit(solution)/shard_map/all_to_all | solution.py:119
  33.3 247.2 %all-reduce.3.cloned.1.call-start = ((), (), s32[]{:S(2)}) async-start(), calls=%async_computation.3 | async-start | bytes 786432
  154.6 11.4 %copy-start.8 = (s32[8]{0:T(128)S(1)}, s32[8]{0:T(128)}, u32[]{:S(2)}) copy-start(s32[8]{0:T(128)} %param.26) | copy-start | bytes 100
  154.6 11.4 %copy-start.1 = (s32[8,5]{1,0:T(8,128)S(1)}, s32[8,5]{1,0:T(8,128)}, u32[]{:S(2)}) copy-start(s32[8,5]{1,0:T(8,128)} %param.27) | copy-start | bytes 484
  154.6 11.6 %copy-start.5 = (s32[8,8]{1,0:T(8,128)S(1)}, s32[8,8]{1,0:T(8,128)}, u32[]{:S(2)}) copy-start(s32[8,8]{1,0:T(8,128)} %param.29) | copy-start | bytes 772
  165.7 150.4 %reduce-scatter.2.cloned.1.call-start = ((), (), s32[]{:S(2)}) async-start(), calls=%async_computation.2 | async-start | bytes 110592 | tf_op jit(solution)/shard_map/reduce_scatter | solution.py:183
  169.0 36.8 %copy-start.4 = (f32[6144]{0:T(1024)S(1)}, f32[6144]{0:T(1024)}, u32[]{:S(2)}) copy-start(f32[6144]{0:T(1024)} %param.16) | copy-start | bytes 73732
  205.7 11.4 %copy-start.3 = (bf16[1,8,6144]{2,1,0:T(8,128)(2,1)S(1)}, bf16[1,8,6144]{2,1,0:T(8,128)(2,1)}, u32[]{:S(2)}) copy-start(bf16[1,8,6144]{2,1,0:T(8,128)(2,1)} %param.23) | copy-start | bytes 294916
  233.5 6.3 %copy-start.10 = (u32[32]{0:T(128)S(1)}, u32[32]{0:T(128)}, u32[]{:S(2)}) copy-start(u32[32]{0:T(128)} %constant.208) | copy-start | bytes 388
  233.5 8.4 %copy-start.9 = (s32[8,12]{1,0:T(8,128)S(1)}, s32[8,12]{1,0:T(8,128)}, u32[]{:S(2)}) copy-start(s32[8,12]{1,0:T(8,128)} %param.28) | copy-start | bytes 1156
  253.3 14.4 %copy-start.2 = (bf16[8,12,1,1536]{3,0,1,2:T(8,128)(2,1)}, bf16[8,12,1,1536]{3,0,1,2:T(8,128)(2,1)S(1)}, u32[]{:S(2)}) copy-start(bf16[8,12,1,1536]{3,0,1,2:T(8,128)(2,1)S(1)} %copy.96) | copy-start | bytes 884740
Sparse Core Ops, SparseCore 0:
  165.8 43.3 all-reduce.2
  286.3 29.7 reduce-scatter.1
where the time goes:
time: 324 us; the launch traced here: 323 us
  blocking collectives  136 us (42%)
  local copies, waits for them, and re-layouts  83.3 us (26%)
  matrix products  45 us (14%)
  waiting for transfers between devices  29.9 us (9%)
  between operations  15.1 us (5%)
  starting transfers between devices  7.67 us (2%)
  other arithmetic  5.45 us (2%)
    all_gather x1, blocking collectives, on_device(): whole = lax.all_gather(new_hidden, 'blk', axis=1, tiled=True)  111 us
    unnamed x27, local copies, waits for them, and re-layouts  42.5 us
    reduce_scatter x1, waiting for transfers between devices, on_device(): lax.psum_scatter((row_share + attn_part).astype(jnp.bfloat16), 'blk', sca...  29.9 us
    all_gather x1, blocking collectives, on_device(): piece = lax.all_gather(held_states, 'blk', axis=0, tiled=True)  15.7 us
    dot_general x1, matrix products, on_device(): jnp.dot(activated, out_weight, preferred_element_type=jnp.float32)  11.1 us
    dot_general x1, matrix products, on_device(): jnp.dot(normed_attn, qkv_weight, preferred_element_type=jnp.float32)  11.1 us
    all_gather x1, blocking collectives, on_device(): every_row = lax.all_gather(normed_mlp, 'pages', axis=0, tiled=True)  9.68 us
    reshape x1, local copies, waits for them, and re-layouts, on_device(): arrived.reshape(group_rows * PPR, PAGE, width)[kept_index]  8.43 us
  transfers between devices with their start and end apart: 3, of which 1 were waited for; matrix products, arithmetic and copies ran while one was open for 34% of the time, Pallas kernels for 0%

commit v1 on v0

v1 whole, which is shorter than its diff:
```python
import functools
import math

import jax
import jax.numpy as jnp
import numpy as np
from jax import lax
from jax.experimental import pallas as pl
from jax.experimental.pallas import tpu as pltpu
from jax.sharding import PartitionSpec as P

D = 6144
H = 64
HD = 96
ROT = 24
PAGE = 16
PPR = 12
KP = 5
NREC = 8
NF = 8
FF = 24576

EPSILON = 1e-05
ROT_BASE = 10000.0
NEVER = -1e30
F32 = jnp.float32
BF16 = jnp.bfloat16
SCALE = 1.0 / math.sqrt(HD)
MIB = 1024 * 1024
STEP_HEADS = 32
QUAD = 4
OCTET = 8


def iota(shape, axis):
    return lax.broadcasted_iota(jnp.int32, shape, axis)


def dot(left, right):
    return jnp.dot(left, right, preferred_element_type=F32)


def dot_nt(left, right):
    return lax.dot_general(left, right, (((1,), (1,)), ((), ())), preferred_element_type=F32)


def dot_tn(left, right):
    return lax.dot_general(left, right, (((0,), (0,)), ((), ())), preferred_element_type=F32)


def parts_of(values, count):
    parts = []
    for _ in range(count):
        part = values.astype(BF16)
        parts.append(part)
        values = values - part.astype(F32)
    return parts


def split_dot(values, selector, count):
    total = None
    for part in parts_of(values, count):
        term = dot(part, selector)
        total = term if total is None else total + term
    return total


def wire_split(width):
    return (width // 128 + 1) // 2 * 128 if width % 128 == 0 else (width + 1) // 2


def to_wire(ref, index, rows):
    width = rows.shape[1]
    first = wire_split(width)
    ref[(*index, slice(None), slice(0, width))] = rows[:2].astype(BF16)
    rest = rows[2:3, first:]
    if width < 2 * first:
        rest = jnp.concatenate([rest, jnp.zeros((1, 2 * first - width), F32)], axis=1)
    tail = jnp.concatenate([rows[2:3, :first], rest], axis=0)
    ref[(*index, slice(None), slice(width, width + first))] = tail.astype(BF16)


def from_wire(ref, index, width, start, stop):
    first = wire_split(width)
    pair = ref[(*index, slice(None), slice(start, stop))].astype(F32)
    third = []
    if start < first:
        third.append(ref[(*index, slice(0, 1), slice(width + start, width + min(stop, first)))].astype(F32))
    if stop > first:
        begin = max(start, first) - first
        third.append(ref[(*index, slice(1, 2), slice(width + begin, width + stop - first))].astype(F32))
    third = third[0] if len(third) == 1 else jnp.concatenate(third, axis=1)
    return jnp.concatenate([pair, third, jnp.zeros_like(third)], axis=0)


def prep_kernel(dims, table_smem, table_ref, length_ref, keep_ref, choice_ref, list_ref, frequency_ref, *refs):
    n_pages, pages_dev, slots, period_heads = dims
    cos_ref, low_ref, high_ref, sel_ref, sel_all_ref, back_ref, pick_ref, number_ref = refs
    group = keep_ref.shape[0]
    n_rows = sel_ref.shape[0]
    mine = lax.axis_index("pages")

    ids = table_ref[:, :group]
    for g in range(1, n_pages):
        ids = jnp.where(mine == g, table_ref[:, g * group : (g + 1) * group], ids)
    holder = jnp.floor((ids.astype(F32) + 0.5) * (1.0 / pages_dev)).astype(jnp.int32)

    def one_request(r, rank):
        for j in range(PPR):
            other = table_smem[j, mine * group + r]
            earlier = (holder == lax.div(other, jnp.int32(pages_dev))) & (ids > other)
            rank = rank + jnp.where(earlier, 1, 0)
        return rank

    row = holder * slots + lax.fori_loop(0, group, one_request, jnp.zeros_like(ids))
    at = iota((n_rows, group), 0)
    hit = None
    for j in range(PPR):
        one = at == row[j : j + 1, :]
        hit = one if hit is None else hit | one
    hit = jnp.where(hit, 1.0, 0.0)
    same = jnp.where(iota((group, group), 0) == iota((group, group), 1), 1.0, 0.0)
    sel_ref[...] = hit.astype(BF16)
    sel_all_ref[:n_rows, :] = hit
    sel_all_ref[n_rows:, :] = same
    turned = row.astype(F32).T
    at = iota((group, n_rows), 1).astype(F32)
    back = jnp.zeros((group, n_rows), F32)
    for j in range(PPR):
        one = jnp.where(at == turned[:, j : j + 1], 1.0, 0.0)
        pick_ref[j * group : (j + 1) * group, :] = one.astype(BF16)
        back = back + one
    back_ref[:, :n_rows] = back.astype(BF16)
    back_ref[:, n_rows:] = same.astype(BF16)

    length = jnp.sum(same * length_ref[...].astype(F32), axis=1, keepdims=True)
    renewed = list_ref[...]
    slot = jnp.zeros_like(renewed)
    for k in range(KP):
        slot = jnp.where(jnp.right_shift(renewed, 4) == k, keep_ref[:, k : k + 1], slot)
    place = (slot * PAGE + jnp.bitwise_and(renewed, PAGE - 1)).astype(F32)
    place = jnp.broadcast_to(place[:, None, :], (group, NREC, NREC)).reshape(group * NREC, NREC)
    shape = (group * NREC, NREC)
    place = jnp.where(jnp.bitwise_and(iota(shape, 0), NREC - 1) == iota(shape, 1), place, 0.0)
    place = jnp.concatenate([length, jnp.sum(place, axis=1, keepdims=True)], axis=0)
    angle = place * frequency_ref[...]
    cosine, sine = jnp.cos(angle), jnp.sin(angle)
    lane = iota(angle.shape, 1)
    low = jnp.where(lane < ROT // 2, -sine, 0.0)
    high = jnp.where((lane >= ROT // 2) & (lane < ROT), sine, 0.0)
    one, none = jnp.ones_like(angle), jnp.zeros_like(angle)
    cos_ref[...] = jnp.concatenate([cosine, cosine, one] * period_heads, axis=1)
    low_ref[...] = jnp.concatenate([low, low, none] * period_heads, axis=1)
    high_ref[...] = jnp.concatenate([high, high, none] * period_heads, axis=1)
    numbers = [length.astype(jnp.int32), keep_ref[...], choice_ref[...], renewed]
    number_ref[...] = jnp.concatenate(numbers, axis=1)


def pack_kernel(held_ref, new_ref, out_ref):
    held_rows = held_ref.shape[0]
    group, chunk = new_ref.shape
    held = held_ref[...].astype(F32)
    rows = [held[:, c * chunk : (c + 1) * chunk] for c in range(D // chunk)] + [new_ref[...].astype(F32)]
    rows = jnp.concatenate(rows, axis=0).astype(BF16)
    for i in range(out_ref.shape[0]):
        out_ref[i] = rows


def project_kernel(dims, *refs):
    group, n_blk, held_rows, heads, slots = dims
    pack_refs, refs = refs[:2], refs[2:]
    gain_ref, weight_hbm, cos_ref, low_ref, high_ref, sel_ref, *refs = refs
    send_ref, own_ref, leaf_ref, weight_buf, rows_ref, acc_ref, sems = refs
    chunk = D // n_blk
    width = 3 * heads * HD
    head_lanes = heads * HD
    extra = 2 * heads * NREC
    period = cos_ref.shape[1]
    period_heads = period // (3 * HD)
    core = jnp.bitwise_and(lax.axis_index("blk"), 1)

    def weight_copy(part, step):
        return pltpu.make_async_copy(
            weight_hbm.at[pl.ds(step * chunk, chunk), pl.ds(part * period, period)],
            weight_buf.at[part, step],
            sems.at[part, step],
        )

    for part in range(width // period):
        for step in range(n_blk):
            weight_copy(part, step).start()

    pieces, places = [], []
    for other in range(2):
        for z in range(n_blk // 2):
            b = 2 * z + jnp.bitwise_xor(core, other)
            values = pack_refs[other][z].astype(F32)
            pieces.append(values[n_blk * held_rows :])
            places.append(b)
            values = values[: n_blk * held_rows].reshape(n_blk, held_rows, chunk)
            mean = jnp.sum(jnp.sum(values, axis=0), axis=1, keepdims=True) / D
            values = values - mean[None]
            spread = jnp.sum(jnp.sum(values * values, axis=0), axis=1, keepdims=True) / D
            values = values * lax.rsqrt(spread + EPSILON)[None]
            first = pl.multiple_of(group + b * held_rows, 8)
            for c in range(n_blk):
                rows_ref[c, pl.ds(first, held_rows), :] = values[c] * gain_ref[:, c * chunk : (c + 1) * chunk]
    leaf_ref[...] = jnp.concatenate(pieces, axis=0).astype(BF16)
    mean = sum(jnp.sum(piece, axis=1, keepdims=True) for piece in pieces) / D
    pieces = [piece - mean for piece in pieces]
    spread = sum(jnp.sum(piece * piece, axis=1, keepdims=True) for piece in pieces) / D
    spread = lax.rsqrt(spread + EPSILON)
    for i, (b, piece) in enumerate(zip(places, pieces)):
        z = i % (n_blk // 2)
        gain = gain_ref[:, 2 * z * chunk : 2 * (z + 1) * chunk]
        gain = jnp.where(b == 2 * z, gain[:, :chunk], gain[:, chunk:])
        rows_ref[b, 0:group, :] = piece * spread * gain

    rows = acc_ref.shape[0]
    wide = heads * NREC
    score = jnp.zeros((rows, wide), F32)
    head_at = jnp.right_shift(iota((rows, wide), 1), 3)
    queries, values = [], []
    for j in range(width // period):
        acc_ref[...] = jnp.zeros_like(acc_ref)

        def one_chunk(step, carry, j=j):
            weight_copy(j, step).wait()
            acc_ref[...] += dot(rows_ref[step].astype(BF16), weight_buf[j, step])
            return carry

        lax.fori_loop(0, n_blk, one_chunk, 0)
        block = acc_ref[...]
        up = jnp.concatenate([block[:, ROT // 2 :], block[:, : ROT // 2]], axis=1)
        down = jnp.concatenate([block[:, -ROT // 2 :], block[:, : -ROT // 2]], axis=1)
        turned = block * cos_ref[...] + up * low_ref[...] + down * high_ref[...]
        turned = turned.astype(BF16).astype(F32)
        for h in range(period_heads):
            first = h * 3 * HD
            query = turned[:group, first : first + HD]
            key = turned[:, first + HD : first + 2 * HD]
            queries.append(query)
            values.append(turned[:group, first + 2 * HD : first + 3 * HD])
            own_product = key[:group] * query
            held_product = key[group:].reshape(group, -1, HD) * query[:, None, :]
            product = jnp.concatenate([own_product, held_product.reshape(rows - group, HD)], axis=0)
            score = jnp.where(
                head_at == j * period_heads + h, jnp.sum(product, axis=1, keepdims=True), score
            )
    score = score * SCALE
    sel = sel_ref[...]
    asked = dot(sel, jnp.concatenate(queries, axis=1).astype(BF16))
    own_ref[:, :head_lanes] = jnp.concatenate(values, axis=1).astype(BF16)

    held_score = score[group:]
    held_count = held_score.shape[0]
    row_id = jnp.bitwise_and(iota((held_count, wide), 0), NREC - 1)
    lane_id = jnp.bitwise_and(iota((held_count, wide), 1), NREC - 1)
    held_score = jnp.where(row_id == lane_id, held_score, 0.0)
    per_request = held_count // group
    spread_ids = jnp.right_shift(iota((group, held_count), 1), per_request.bit_length() - 1)
    spread_rows = jnp.where(spread_ids == iota((group, held_count), 0), 1.0, 0.0).astype(BF16)
    sel_rows = dot(sel, spread_rows).astype(BF16)
    both = jnp.concatenate(parts_of(held_score, 2), axis=1)
    given = dot(sel_rows, both)
    both = jnp.concatenate([asked, given], axis=1)
    for d in range(send_ref.shape[0]):
        to_wire(send_ref, (d,), both[d * slots : (d + 1) * slots])

    own_score = score[:group]
    lane = iota((group, extra), 1)
    own = jnp.zeros((group, extra), F32)
    for i, part in enumerate(parts_of(own_score, 3)):
        part = part.astype(F32)
        for h in range(heads):
            own = jnp.where(lane == i * heads + h, part[:, h * NREC : h * NREC + 1], own)
    own_ref[:, head_lanes : head_lanes + extra] = own.astype(BF16)


def fold_kernel(weight_ref, page_ref, fold_ref):
    parts = jnp.concatenate(parts_of(weight_ref[...], 3), axis=0)
    rows = weight_ref.shape[0]
    sums = dot(parts, page_ref[...])
    folded = sums[:rows] + sums[rows : 2 * rows] + sums[2 * rows :]
    fold_ref[...] = folded.astype(BF16)


def place_kernel(dims, pick_ref, got_ref, out_ref, rows_ref):
    slots, width, first_lane = dims
    for d in range(got_ref.shape[0]):
        rows_ref[d * slots : (d + 1) * slots, :] = from_wire(got_ref, (d,), width, first_lane, width)
    found = dot(pick_ref[...], rows_ref[...].astype(BF16)).astype(BF16)
    group = out_ref.shape[1]
    for j in range(out_ref.shape[0]):
        out_ref[j] = found[j * group : (j + 1) * group]


def attend_kernel(dims, ask_ref, valid_ref, place_ref, page_ref, fold_ref, *refs):
    send_ref = refs[-1]
    n_pages, slots, dests, heads = dims
    rows = n_pages * slots
    head_lanes = heads * HD
    extra = 2 * heads * NREC
    tokens = page_ref.shape[0]
    asks = [
        jnp.concatenate(
            [from_wire(ask_ref, (g, b), head_lanes + extra, 0, head_lanes + extra) for g in range(n_pages)],
            axis=0,
        )
        for b in range(dests)
    ]
    query = jnp.concatenate([a[:, :head_lanes] for a in asks], axis=1)
    given = jnp.concatenate([a[:, head_lanes : head_lanes + extra] for a in asks], axis=1)
    valid = valid_ref[...] > 0.5
    place = place_ref[...]
    touched = jnp.sum(place[:, :NREC].astype(F32), axis=1, keepdims=True) > 0.5
    lanes = OCTET * rows
    shift = rows.bit_length() - 1
    lane_head = jnp.right_shift(iota((HD, lanes), 1), shift)
    blank = jnp.zeros((HD, lanes), F32)
    lane = iota((lanes, lanes), 1)
    lane_in = jnp.bitwise_and(lane, extra - 1)
    lane_dest = jnp.right_shift(lane, extra.bit_length() - 1) * heads
    given_head = jnp.right_shift(jnp.bitwise_and(lane_in, heads * NREC - 1), 3) + lane_dest
    row_head = jnp.right_shift(iota((lanes, lanes), 0), shift)
    own_lane = jnp.bitwise_and(iota((rows, lanes), 1), rows - 1) == iota((rows, lanes), 0)
    goals = []
    for i in range(3):
        hit = (lane_in >= i * heads) & (lane_in < (i + 1) * heads)
        hit = hit & (row_head == lane_dest + lane_in - i * heads)
        goals.append(jnp.where(hit, 1.0, 0.0).astype(BF16))
    gathered, extras = [], []
    for o in range(STEP_HEADS // OCTET):
        heads_here = range(o * OCTET, (o + 1) * OCTET)
        asked = jnp.concatenate([query[:, h * HD : (h + 1) * HD] for h in heads_here], axis=0)
        asked = jnp.concatenate([asked, jnp.zeros((lanes, 128 - HD), F32)], axis=1).T[:HD]
        stacked = []
        for h in range(OCTET):
            stacked += [jnp.where(lane_head == h, asked, 0.0), blank]
        stacked = jnp.concatenate(stacked, axis=0).astype(BF16)
        told = jnp.concatenate([given[:, o * lanes : (o + 1) * lanes]] * OCTET, axis=0)
        told = jnp.where(given_head == row_head, told, 0.0).T.astype(BF16)
        some = slice(o * OCTET * 2 * HD, (o + 1) * OCTET * 2 * HD)
        page = jnp.concatenate([page_ref[:, some], fold_ref[:, some]], axis=0)
        scores = jnp.where(touched, dot(place, told), dot(page, stacked) * SCALE)
        scores = jnp.where(valid, scores, NEVER)
        top = jnp.max(scores, axis=0, keepdims=True)
        weights = jnp.where(valid, jnp.exp(scores - top), 0.0)
        total = jnp.sum(weights, axis=0, keepdims=True)
        safe = jnp.where(total > 0.0, total, 1.0)
        rest = jnp.zeros((256 - weights.shape[0], lanes), F32)
        weights = jnp.concatenate([weights * (1.0 / safe), rest], axis=0).T.astype(BF16)
        page = jnp.concatenate([page, jnp.zeros((rest.shape[0], page.shape[1]), BF16)], axis=0)
        for i in range(OCTET // QUAD):
            mixed = dot(
                weights[i * QUAD * rows : (i + 1) * QUAD * rows],
                page[:, i * QUAD * 2 * HD : (i + 1) * QUAD * 2 * HD],
            )
            for h in range(QUAD):
                gathered.append(mixed[h * rows : (h + 1) * rows, 2 * HD * h + HD : 2 * HD * (h + 1)])
        lse = jnp.where(own_lane, jnp.where(total > 0.0, top + jnp.log(safe), NEVER), 0.0)
        spread = jnp.zeros((rows, lanes), F32)
        for part, goal in zip(parts_of(lse, 3), goals):
            spread = spread + dot(part, goal)
        extras.append(spread)
    gathered = jnp.concatenate(gathered, axis=1)
    extras = jnp.concatenate(extras, axis=1)
    width = 2 * head_lanes
    folded = fold_ref[...].astype(F32)
    for b in range(dests):
        whole = jnp.concatenate(
            [
                gathered[:, b * head_lanes : (b + 1) * head_lanes],
                extras[:, b * extra : (b + 1) * extra],
                folded[:, b * width : (b + 1) * width],
            ],
            axis=1,
        )
        for g in range(n_pages):
            to_wire(send_ref, (g, b), whole[g * slots : (g + 1) * slots])


def merge_kernel(
    dims, got_ref, own_ref, sel_ref, back_ref, *refs
):
    group, n_dev, slots, heads, n_pages = dims
    share_refs, dense_hbm, refs = refs[:n_pages], refs[n_pages], refs[n_pages + 1 :]
    head_lanes = heads * HD
    extra = 2 * heads * NREC
    n_blk = n_dev // n_pages
    out_ref, dense_buf, rows_ref, sems = refs
    chunk = D // n_blk
    steps, _, cols = dense_buf.shape

    def dense_copy(step):
        return pltpu.make_async_copy(
            dense_hbm.at[:, pl.ds(step * cols, cols)], dense_buf.at[step], sems.at[step]
        )

    for step in range(steps):
        dense_copy(step).start()
    for d in range(n_dev):
        rows_ref[d * slots : (d + 1) * slots, :] = from_wire(
            got_ref, (d,), 3 * head_lanes + extra, 0, head_lanes + extra
        )
    rows_ref[n_dev * slots :, :] = own_ref[...].astype(F32)
    count = rows_ref.shape[0]
    parts = rows_ref[:, head_lanes : head_lanes + extra].astype(BF16)
    to, source = iota((extra, 128), 1), iota((extra, 128), 0)
    hit = None
    for i in range(3):
        one = (to < heads) & (source == to + i * heads)
        hit = one if hit is None else hit | one
    lse = dot(parts, jnp.where(hit, 1.0, 0.0).astype(BF16))
    tops = jnp.zeros((count, 128), F32)
    for r in range(group):
        mine = sel_ref[:, r : r + 1] > 0.5
        top = jnp.max(jnp.where(mine, lse, -3e38), axis=0, keepdims=True)
        tops = jnp.where(mine, top, tops)
    weights = jnp.exp(jnp.minimum(lse - tops, 0.0))
    back = back_ref[...]
    totals = jnp.zeros((group, 128), F32)
    for part in parts_of(weights, 3):
        totals = totals + dot(back, part)
    inverse = 1.0 / totals
    lanes, heads_of = iota((128, head_lanes), 1), iota((128, head_lanes), 0)
    over = lanes - heads_of * HD
    spread = jnp.where((over >= 0) & (over < HD), 1.0, 0.0).astype(BF16)
    weighted = split_dot(weights, spread, 2) * rows_ref[:, :head_lanes]
    mixed = jnp.zeros((group, head_lanes), F32)
    for part in parts_of(weighted, 2):
        mixed = mixed + dot(back, part)
    attended = (mixed * split_dot(inverse, spread, 3)).astype(BF16)
    for step in range(steps):
        dense_copy(step).wait()
        some = slice(step * cols, (step + 1) * cols)
        result = dot(attended, dense_buf[step])
        for share_ref in share_refs:
            result = result + share_ref[:, some].astype(F32)
        for i in range(cols // chunk):
            out_ref[step * (cols // chunk) + i] = result[:, i * chunk : (i + 1) * chunk].astype(BF16)


def mlp_kernel(dims, *refs):
    group, n_pages, n_blk = dims
    leaf_refs, refs = refs[:n_pages], refs[n_pages:]
    gain_ref, in_hbm, out_hbm, _, *refs = refs
    part_refs, (in_buf, out_buf, rows_ref, sems_in, sems_out) = refs[:n_pages], refs[n_pages:]
    chunk = D // n_blk
    n_steps, cols = out_buf.shape[0], out_buf.shape[2]
    core = jnp.bitwise_and(lax.axis_index("blk"), 1)

    def in_copy(step):
        return pltpu.make_async_copy(
            in_hbm.at[pl.ds(step * chunk, chunk), :], in_buf.at[step], sems_in.at[step]
        )

    def out_copy(step):
        return pltpu.make_async_copy(
            out_hbm.at[:, pl.ds(step * cols, cols)], out_buf.at[step], sems_out.at[step]
        )

    for step in range(n_blk):
        in_copy(step).start()
    for step in range(n_steps):
        out_copy(step).start()
    for g in range(n_pages):
        leaf = leaf_refs[g][...].astype(F32)
        pieces = [leaf[i * group : (i + 1) * group] for i in range(n_blk)]
        mean = sum(jnp.sum(piece, axis=1, keepdims=True) for piece in pieces) / D
        pieces = [piece - mean for piece in pieces]
        spread = sum(jnp.sum(piece * piece, axis=1, keepdims=True) for piece in pieces) / D
        spread = lax.rsqrt(spread + EPSILON)
        for i in range(n_blk):
            c = 2 * (i % (n_blk // 2)) + jnp.bitwise_xor(core, i // (n_blk // 2))
            z = i % (n_blk // 2)
            gain = gain_ref[:, 2 * z * chunk : 2 * (z + 1) * chunk]
            gain = jnp.where(c == 2 * z, gain[:, :chunk], gain[:, chunk:])
            rows_ref[c, g * group : (g + 1) * group, :] = pieces[i] * spread * gain
    hidden = jnp.zeros((n_pages * group, in_buf.shape[2]), F32)
    for step in range(n_blk):
        in_copy(step).wait()
        hidden = hidden + dot(rows_ref[step].astype(BF16), in_buf[step])
    active = (0.5 * hidden * (1.0 + lax.erf(hidden * math.sqrt(0.5)))).astype(BF16)
    for step in range(n_steps):
        out_copy(step).wait()
        result = dot(active, out_buf[step]).astype(BF16)
        for g in range(n_pages):
            part_refs[g][:, step * cols : (step + 1) * cols] = result[g * group : (g + 1) * group]


VMEM = pl.BlockSpec(memory_space=pltpu.VMEM)
HBM = pl.BlockSpec(memory_space=pltpu.HBM)
ANY = pl.BlockSpec(memory_space=pl.ANY)


def shape_of(shape, kind=BF16):
    return jax.ShapeDtypeStruct(shape, kind)


def params_of(mib):
    return pltpu.CompilerParams(vmem_limit_bytes=mib * MIB)


def cost_of(flops, nbytes):
    return pl.CostEstimate(flops=int(flops), bytes_accessed=int(nbytes), transcendentals=0)


def on_device(
    new_hidden,
    attn_gain,
    mlp_gain,
    qkv_weight,
    dense_weight,
    in_weight,
    out_weight,
    page_store,
    held_states,
    fold_weights,
    page_table,
    lengths,
    keep_slots,
    fold_index,
    recompute_list,
):
    n_pages = lax.axis_size("pages")
    n_blk = lax.axis_size("blk")
    n_dev = n_pages * n_blk
    mine = lax.axis_index("pages")
    device = lax.axis_index(("pages", "blk"))
    group = lengths.shape[0]
    pages_dev = page_store.shape[0]
    slots = -(-(pages_dev // n_pages) // 4) * 4
    ranks = n_pages * slots
    heads = H // n_blk
    head_lanes = heads * HD
    extra = 2 * heads * NREC
    lanes = head_lanes + extra
    chunk = D // n_blk
    held_rows = held_states.shape[0] * NREC
    kept_count = KP * PAGE

    def swapped(array, axis, size, by):
        return lax.ppermute(array, axis, [(i, i ^ by) for i in range(size)])

    def swapped(array, axis, size, by):
        return lax.ppermute(array, axis, [(i, i ^ by) for i in range(size)])

    def fixed(array):
        return pltpu.with_memory_space_constraint(array, pltpu.HBM)

    half = n_blk // 2
    pack = pl.pallas_call(
        pack_kernel,
        in_specs=[VMEM, VMEM],
        out_specs=VMEM,
        out_shape=shape_of((half, n_blk * held_rows + group, chunk)),
        compiler_params=params_of(16),
        name="pack",
    )(fixed(held_states.reshape(held_rows, D)), fixed(new_hidden))
    pack = lax.all_to_all(
        pack,
        "blk",
        0,
        0,
        axis_index_groups=[list(range(core, n_blk, 2)) for core in range(2)],
        tiled=True,
    )
    packs = [pack, swapped(pack, "blk", n_blk, 1)]

    n_rows = n_dev * slots
    rows = group * (1 + NREC)
    period = 12 * HD if (3 * head_lanes) % (12 * HD) == 0 else 3 * head_lanes
    lane = np.arange(HD)
    frequency = np.where(lane < ROT, ROT_BASE ** (-2.0 * (lane % (ROT // 2)) / ROT), 0.0).astype(np.float32)
    cosine, low, high, sel, sel_all, back, pick, numbers = pl.pallas_call(
        functools.partial(prep_kernel, (n_pages, pages_dev, slots, period // (3 * HD))),
        in_specs=[pl.BlockSpec(memory_space=pltpu.SMEM)] + [VMEM] * 6,
        out_specs=[VMEM] * 8,
        out_shape=[
            *[shape_of((rows, period), F32)] * 3,
            shape_of((n_rows, group)),
            shape_of((n_rows + group, group), F32),
            shape_of((group, n_rows + group)),
            shape_of((PPR * group, n_rows)),
            shape_of((group, 1 + KP + PPR + NREC), jnp.int32),
        ],
        compiler_params=params_of(16),
        cost_estimate=cost_of(0, 0),
        name="prep",
    )(
        page_table.T,
        fixed(page_table.T),
        fixed(lengths[None]),
        fixed(keep_slots),
        fixed(fold_index),
        fixed(recompute_list),
        fixed(jnp.asarray(frequency[None])),
    )

    numbers = jnp.concatenate(
        [numbers] + [swapped(numbers, "pages", n_pages, i) for i in range(1, n_pages)], axis=0
    )

    tokens = pages_dev * PAGE
    pages = page_store.reshape(tokens, 2 * D)
    steps = H // STEP_HEADS
    step_lanes = STEP_HEADS * 2 * HD
    dests = STEP_HEADS // heads
    fold_width = 2 * head_lanes

    wire = lanes + wire_split(lanes)
    send, own, leaf = pl.pallas_call(
        functools.partial(project_kernel, (group, n_blk, held_rows, heads, slots)),
        in_specs=[VMEM] * 3 + [HBM] + [VMEM] * 4,
        out_specs=[VMEM] * 3,
        out_shape=[
            shape_of((n_dev, 2, wire)),
            shape_of((group, lanes)),
            shape_of((n_blk * group, chunk)),
        ],
        scratch_shapes=[
            pltpu.VMEM((3 * head_lanes // period, n_blk, chunk, period), BF16),
            pltpu.VMEM((n_blk, rows, chunk), F32),
            pltpu.VMEM((rows, period), F32),
            pltpu.SemaphoreType.DMA((3 * head_lanes // period, n_blk)),
        ],
        compiler_params=params_of(50),
        cost_estimate=cost_of(2 * rows * D * 3 * head_lanes, 6 * D * head_lanes),
        name="project",
    )(
        *packs,
        fixed(attn_gain[None]),
        fixed(qkv_weight),
        cosine,
        low,
        high,
        sel,
    )
    send, numbers, late_table = lax.optimization_barrier((send, numbers, page_table))
    asked = lax.all_to_all(send, ("pages", "blk"), 0, 0, tiled=True)

    token = jnp.arange(tokens, dtype=jnp.int32)
    local, inside = token // PAGE, token % PAGE
    found = late_table[:, :, None] == (device * pages_dev + local)[None, None, :]
    request_hit = jnp.any(found, axis=1)
    slot_hit = jnp.any(found, axis=0)
    slot_ids = jnp.arange(PPR, dtype=jnp.int32)
    slot = jnp.sum(jnp.where(slot_hit, slot_ids[:, None], 0), axis=0)
    request = jnp.sum(jnp.where(request_hit, jnp.arange(n_pages * group, dtype=jnp.int32)[:, None], 0), axis=0)
    owner = request // group
    request_hit = (
        jnp.arange(n_pages * group, dtype=jnp.int32)[:, None]
        == (jnp.bitwise_xor(owner, mine) * group + request % group)[None]
    )
    facts = jnp.dot(numbers.astype(BF16).T, request_hit.astype(BF16), preferred_element_type=F32).astype(jnp.int32)
    length, keeps = facts[0], facts[1 : 1 + KP]
    choices, renewed = facts[1 + KP : 1 + KP + PPR], facts[1 + KP + PPR :]
    choice = jnp.sum(jnp.where(slot_hit, choices, 0), axis=0)
    kept_hit = keeps == slot[None]
    kept = jnp.any(kept_hit, axis=0)
    kept_place = jnp.sum(jnp.where(kept_hit, jnp.arange(KP, dtype=jnp.int32)[:, None] * PAGE, 0), axis=0)
    dropped = jnp.logical_and(jnp.logical_not(kept), slot * PAGE < length)
    live = slot * PAGE + inside < length
    fold_row = jnp.sum(
        jnp.where(
            choice[None] == jnp.arange(NF, dtype=jnp.int32)[:, None],
            jnp.tile(fold_weights, (1, pages_dev)),
            0.0,
        ),
        axis=0,
    )
    earlier = (owner[:, None] == owner[None]) & (local[:, None] < local[None]) & (inside == 0)[:, None]
    rank_in = jnp.sum(earlier.astype(jnp.int32), axis=0)
    rank = owner * slots + rank_in
    ids = jnp.arange(ranks, dtype=jnp.int32)
    rank_hit = ids[:, None] == rank[None]
    fold_rows = jnp.where(rank_hit & (dropped & live)[None], fold_row[None], 0.0)
    fold_drop = jnp.any(rank_hit & dropped[None], axis=1)
    octet_lane = jnp.arange(OCTET * ranks, dtype=jnp.int32) % ranks
    valid = jnp.concatenate(
        [
            ((rank[:, None] == octet_lane[None]) & kept[:, None]).astype(F32),
            ((ids[:, None] == octet_lane[None]) & fold_drop[:, None]).astype(F32),
        ],
        axis=0,
    )
    renew = ((renewed == (kept_place + inside)[None]) & kept[None]).astype(BF16)
    renew = jnp.pad(jnp.tile(renew.T, (1, 2 * OCTET)), ((0, ranks), (0, 0)))

    leaf, fold_rows = lax.optimization_barrier((leaf, fold_rows))
    leaves = [leaf] + [swapped(leaf, "pages", n_pages, i) for i in range(1, n_pages)]

    folded_rows = pl.pallas_call(
        fold_kernel,
        grid=(steps,),
        in_specs=[
            pl.BlockSpec((ranks, tokens), lambda i: (0, 0)),
            pl.BlockSpec((tokens, step_lanes), lambda i: (0, i)),
        ],
        out_specs=pl.BlockSpec((ranks, step_lanes), lambda i: (0, i)),
        out_shape=shape_of((ranks, 2 * D)),
        compiler_params=params_of(16),
        cost_estimate=cost_of(0, 0),
        name="fold",
    )(fold_rows, fixed(pages))

    all_lanes = lanes + fold_width
    all_wire = all_lanes + wire_split(all_lanes)
    partial = pl.pallas_call(
        functools.partial(attend_kernel, (n_pages, slots, dests, heads)),
        grid=(steps,),
        in_specs=[
            pl.BlockSpec((n_pages, dests, 2, wire), lambda i: (0, i, 0, 0)),
            pl.BlockSpec((tokens + ranks, OCTET * ranks), lambda i: (0, 0)),
            pl.BlockSpec((tokens + ranks, 2 * OCTET * NREC), lambda i: (0, 0)),
            pl.BlockSpec((tokens, step_lanes), lambda i: (0, i)),
            pl.BlockSpec((ranks, step_lanes), lambda i: (0, i)),
            *[ANY] * (n_pages - 1),
        ],
        out_specs=pl.BlockSpec((n_pages, dests, 2, all_wire), lambda i: (0, i, 0, 0)),
        out_shape=shape_of((n_pages, n_blk, 2, all_wire)),
        compiler_params=params_of(16),
        cost_estimate=cost_of(2 * 128 * tokens * 2 * D, tokens * 4 * D),
        name="attend",
    )(asked.reshape(n_pages, n_blk, 2, wire), valid, renew, fixed(pages), folded_rows, *leaves[1:])
    got = lax.all_to_all(partial.reshape(n_dev, 2, all_wire), ("pages", "blk"), 0, 0, tiled=True)

    hidden = in_weight.shape[1]
    mlp_parts = pl.pallas_call(
        functools.partial(mlp_kernel, (group, n_pages, n_blk)),
        in_specs=[VMEM] * (n_pages + 1) + [HBM, HBM, ANY],
        out_specs=[VMEM] * n_pages,
        out_shape=[shape_of((group, D))] * n_pages,
        scratch_shapes=[
            pltpu.VMEM((n_blk, chunk, hidden), BF16),
            pltpu.VMEM((8, hidden, D // 8), BF16),
            pltpu.VMEM((n_blk, n_pages * group, chunk), F32),
            pltpu.SemaphoreType.DMA((n_blk,)),
            pltpu.SemaphoreType.DMA((8,)),
        ],
        compiler_params=params_of(24),
        cost_estimate=cost_of(4 * n_pages * group * D * hidden, 4 * D * hidden),
        name="mlp",
    )(*leaves, fixed(mlp_gain[None]), fixed(in_weight), fixed(out_weight), partial)
    mlp_share = [mlp_parts[0]] + [swapped(mlp_parts[i], "pages", n_pages, i) for i in range(1, n_pages)]

    out_part = pl.pallas_call(
        functools.partial(merge_kernel, (group, n_dev, slots, heads, n_pages)),
        in_specs=[VMEM] * (n_pages + 4) + [HBM],
        out_specs=VMEM,
        out_shape=shape_of((n_blk, group, chunk)),
        scratch_shapes=[
            pltpu.VMEM((8, head_lanes, D // 8), BF16),
            pltpu.VMEM((n_rows + group, lanes), F32),
            pltpu.SemaphoreType.DMA((8,)),
        ],
        compiler_params=params_of(24),
        cost_estimate=cost_of(2 * group * D * head_lanes, 2 * D * head_lanes),
        name="merge",
    )(
        got,
        own,
        sel_all,
        back,
        *mlp_share,
        fixed(dense_weight),
    )
    out_got = lax.all_to_all(out_part, "blk", 0, 0, tiled=True)
    summed = jnp.sum(out_got.astype(F32), axis=0).astype(BF16)

    folded = pl.pallas_call(
        functools.partial(place_kernel, (slots, all_lanes, lanes)),
        in_specs=[VMEM, VMEM],
        out_specs=VMEM,
        out_shape=shape_of((PPR, group, fold_width)),
        scratch_shapes=[pltpu.VMEM((n_rows, fold_width), F32)],
        compiler_params=params_of(16),
        cost_estimate=cost_of(0, 4 * n_rows * fold_width),
        name="place",
    )(pick, got)
    folded = jnp.transpose(folded, (1, 0, 2))
    return (summed, folded)


def solution(mesh):
    in_specs = (
        P("pages", "blk"),
        P(),
        P(),
        P(None, "blk"),
        P("blk", None),
        P(None, ("pages", "blk")),
        P(("pages", "blk"), None),
        P(("pages", "blk"), None, None),
        P(("pages", "blk"), None, None),
        P(),
        P(),
        P("pages"),
        P("pages", None),
        P("pages", None),
        P("pages", None),
    )
    out_specs = (P("pages", "blk"), P("pages", None, "blk"))
    return jax.shard_map(
        on_device, mesh=mesh, in_specs=in_specs, out_specs=out_specs, check_vma=False
    )
```

time: 324 us -> 100 us (0.31)
  blocking collectives: 136 us -> 0 us
  local copies, waits for them, and re-layouts: 83.3 us -> 0.28 us
  matrix products: 45 us -> 0.18 us
  Pallas kernels: 0 us -> 44.4 us
  starting transfers between devices: 7.67 us -> 28.1 us
  between operations: 15.1 us -> 0.86 us
  waiting for transfers between devices: 29.9 us -> 24.2 us
  other arithmetic: 5.45 us -> 1.56 us
    all_gather x3 -> x0, blocking collectives: 136 us -> none  [the longest x1 111 us: on_device(): whole = lax.all_gather(new_hidden, 'blk', axis=1, tiled=True)]
    dot_general x10 -> x1, matrix products: 45 us -> 0.18 us  [on_device(): jnp.dot(numbers.astype(BF16).T, request_hit.astype(BF16), preferred_eleme...]
    pallas_call x0 -> x8, Pallas kernels: none -> 44.4 us  [the longest x1 12.3 us: on_device(): pl.pallas_call(functools.partial(project_kernel, (group, n_blk, held_rows...]
    unnamed x27 -> x4, local copies, waits for them, and re-layouts: 42.5 us -> 0.01 us
    reduce_scatter x1 -> x0, waiting for transfers between devices: 29.9 us -> none  [on_device(): lax.psum_scatter((row_share + attn_part).astype(jnp.bfloat16), 'blk', sca...]
    gather x8 -> x0, local copies, waits for them, and re-layouts: 17.6 us -> none  [the longest x1 5.5 us: on_device(): arrived = incoming[place.reshape(-1)].reshape(group_rows, PPR, PAGE, width)]
    all_to_all x1 -> x4, waiting for transfers between devices: 0.01 us -> 17.3 us  [the longest x1 7.13 us: on_device(): lax.all_to_all(pack, 'blk', 0, 0, axis_index_groups=[list(range(core, n_b...]
    ppermute x0 -> x10, starting transfers between devices: none -> 10.7 us  [swapped(): return lax.ppermute(array, axis, [(i, i ^ by) for i in range(size)])]
  transfers between devices with their start and end apart: 3 -> 14, of which waited for: 1 -> 6; matrix products, arithmetic and copies ran while one was open for 34% -> 0% of each run, Pallas kernels for 0% -> 17%
where the time goes in v1:
time: 100 us; the launch traced here: 99.6 us
  Pallas kernels  44.4 us (44%)
  starting transfers between devices  28.1 us (28%)
  waiting for transfers between devices  24.2 us (24%)
  other arithmetic  1.56 us (2%)
    pallas_call x1, Pallas kernels, on_device(): pl.pallas_call(functools.partial(project_kernel, (group, n_blk, held_rows...  12.3 us
    ppermute x10, starting transfers between devices, swapped(): return lax.ppermute(array, axis, [(i, i ^ by) for i in range(size)])  10.7 us
    pallas_call x1, Pallas kernels, on_device(): pl.pallas_call(functools.partial(mlp_kernel, (group, n_pages, n_blk)), in...  10.4 us
    pallas_call x1, Pallas kernels, on_device(): pl.pallas_call(functools.partial(attend_kernel, (n_pages, slots, dests, h...  8.28 us
    all_to_all x1, waiting for transfers between devices, on_device(): lax.all_to_all(pack, 'blk', 0, 0, axis_index_groups=[list(range(core, n_b...  7.13 us
    ppermute x10, waiting for transfers between devices, swapped(): return lax.ppermute(array, axis, [(i, i ^ by) for i in range(size)])  6.82 us
    all_to_all x1, starting transfers between devices, on_device(): lax.all_to_all(pack, 'blk', 0, 0, axis_index_groups=[list(range(core, n_b...  6.32 us
    pallas_call x1, Pallas kernels, on_device(): pl.pallas_call(functools.partial(merge_kernel, (group, n_dev, slots, head...  5.45 us
  transfers between devices with their start and end apart: 14, of which 6 were waited for; matrix products, arithmetic and copies ran while one was open for 0% of the time, Pallas kernels for 17%

profile of v1, /device:TPU:0, one launch (start us, length us, event | category | flops | bytes accessed | tf_op | source)
XLA Modules:
  0.0 99.6 jit_solution(15717839723200008291)
XLA Ops:
  0.6 1.7 %pack.1 = bf16[4,72,768]{2,1,0:T(8,128)(2,1)} custom-call(bf16[8,6144]{1,0:T(8,128)(2,1)} %bitcast.18, bf16[8,768]{1,0:T(8,128)(2,1)} %new_ref.1), custom_call_target="tpu_custom_call" | custom-call | tf_op jit(solution)/shard_map/pack/pallas_call | solution.py:553
  2.3 6.3 %all-to-all-start = ((bf16[4,72,768]{2,1,0:T(8,128)(2,1)}), bf16[4,72,768]{2,1,0:T(8,128)(2,1)S(1)}, u32[]{:S(2)}, u32[]{:S(2)}) async-start(bf16[4,72,768]{2,1,0:T(8,128)(2,1)} %pack.1), calls=%async_computation | async-start | bytes 884736 | tf_op jit(solution)/shard_map/all_to_all | solution.py:561
  8.6 2.0 %prep.1 = (f32[72,1152]{1,0:T(8,128)S(1)}, f32[72,1152]{1,0:T(8,128)S(1)}, f32[72,1152]{1,0:T(8,128)S(1)}, bf16[128,8]{1,0:T(8,128)(2,1)S(1)}, f32[136,8]{1,0:T(...) custom-call(s32[12,32]{1,0:T(8,128)} %bitcast.19, s32[12,32]{1,0:T(8,128)} %bitcast.20, ...), custom_call_target="tpu_custom_call" | custom-call | tf_op jit(solution)/shard_map/prep/pallas_call | solution.py:576
  10.7 2.5 %collective-permute-start.3 = (s32[8,26]{1,0:T(8,128)S(1)}, s32[8,26]{1,0:T(8,128)S(1)}, u32[]{:S(2)}, u32[]{:S(2)}) collective-permute-start(s32[8,26]{1,0:T(8,128)S(1)} %get-tuple-element.27), channel_id=1, source_target_pairs={{0,24},{8,16},{16,8},{24,0},{1,25},{9,17},{17,9},{25,1},{2,26},{10... | collective-permute-start | bytes 2504 | tf_op jit(solution)/shard_map/ppermute | solution.py:547
  13.2 0.5 collective-permute-start.2
  13.7 0.5 collective-permute-start.1
  14.2 7.1 %all-to-all-done.refs_0_ = bf16[4,72,768]{2,1,0:T(8,128)(2,1)S(1)} async-done(((bf16[4,72,768]{2,1,0:T(8,128)(2,1)}), bf16[4,72,768]{2,1,0:T(8,128)(2,1)S(1)}, u32[]{:S(2)}, u32[]{:S(2)}) %all-to-all-start) | async-done | bytes 442400 | tf_op jit(solution)/shard_map/all_to_all | solution.py:561
  21.5 1.7 %collective-permute-done.refs_1_ = bf16[4,72,768]{2,1,0:T(8,128)(2,1)S(1)} collective-permute-done((bf16[4,72,768]{2,1,0:T(8,128)(2,1)S(1)}, bf16[4,72,768]{2,1,0:T(8,128)(2,1)S(1)}, u32[]{:S(2)}, u32[]{:S(2)}) %collective-permute-start) | collective-permute-done | bytes 442400 | tf_op jit(solution)/shard_map/ppermute | solution.py:547
  23.2 12.3 %project.1 = (bf16[32,2,1408]{2,1,0:T(2,128)(2,1)}, bf16[8,896]{1,0:T(8,128)(2,1)S(1)}, bf16[64,768]{1,0:T(8,128)(2,1)S(1)}) custom-call(bf16[4,72,768]{2,1,0:T(8,128)(2,1)S(1)} %all-to-all-done.refs_0_, bf16[4,72,768]{2,1,0:T(8,128)(2,1)S(1)} %collective-permute-done.refs_1_, f32[1,6144]{1,0:T(1,128)} %bitcast.21, bf16[6144,2304]{1,0:T(8,128)(2,1)} %refs_3_.1, ...), custom_call_target="tpu_custom_call" | custom-call | flops 2038431744 | bytes 28311552 | tf_op jit(solution)/shard_map/project/pallas_call | solution.py:613
  35.5 0.2 compare_reduce_fusion
  35.7 0.2 convert_reduce_fusion
  35.9 0.2 convolution_convert_fusion
  36.5 1.6 %collective-permute-start.4 = (bf16[64,768]{1,0:T(8,128)(2,1)S(1)}, bf16[64,768]{1,0:T(8,128)(2,1)S(1)}, u32[]{:S(2)}, u32[]{:S(2)}) collective-permute-start(bf16[64,768]{1,0:T(8,128)(2,1)S(1)} %get-tuple-element.33.refs_0_), channel_id=1, source_target_pairs={{0,8},{8,0},{16,24},{24,16},{1,9},{9,1},{17,25},{25,17},{2,10},{10... | collective-permute-start | bytes 294920 | tf_op jit(solution)/shard_map/ppermute | solution.py:547
  38.0 1.5 %collective-permute-start.5 = (bf16[64,768]{1,0:T(8,128)(2,1)S(1)}, bf16[64,768]{1,0:T(8,128)(2,1)S(1)}, u32[]{:S(2)}, u32[]{:S(2)}) collective-permute-start(bf16[64,768]{1,0:T(8,128)(2,1)S(1)} %get-tuple-element.33.refs_0_), channel_id=1, source_target_pairs={{0,16},{8,24},{16,0},{24,8},{1,17},{9,25},{17,1},{25,9},{2,18},{10... | collective-permute-start | bytes 294920 | tf_op jit(solution)/shard_map/ppermute | solution.py:547
  39.6 0.5 collective-permute-start.6
  40.0 3.7 %all-to-all-start.1 = ((bf16[32,2,1408]{2,1,0:T(2,128)(2,1)}), bf16[32,2,1408]{2,1,0:T(2,128)(2,1)S(1)}, u32[]{:S(2)}, u32[]{:S(2)}) async-start(bf16[32,2,1408]{2,1,0:T(2,128)(2,1)} %get-tuple-element.28), calls=%async_computation.1 | async-start | bytes 360448 | tf_op jit(solution)/shard_map/all_to_all | solution.py:641
  43.8 0.1 fusion.4
  44.1 2.9 %fold.1.fold_ref = bf16[16,12288]{1,0:T(8,128)(2,1)S(1)} custom-call(f32[16,192]{1,0:T(8,128)S(1)} %fusion.5.weight_ref, bf16[192,12288]{1,0:T(8,128)(2,1)} %bitcast.15), custom_call_target="tpu_custom_call" | custom-call | tf_op jit(solution)/shard_map/fold/pallas_call | solution.py:694
  47.2 5.2 %all-to-all-done.1 = bf16[32,2,1408]{2,1,0:T(2,128)(2,1)S(1)} async-done(((bf16[32,2,1408]{2,1,0:T(2,128)(2,1)}), bf16[32,2,1408]{2,1,0:T(2,128)(2,1)S(1)}, u32[]{:S(2)}, u32[]{:S(2)}) %all-to-all-start.1) | async-done | bytes 180256 | tf_op jit(solution)/shard_map/all_to_all | solution.py:641
  52.4 8.3 %attend.1.refs_7_ = bf16[4,8,2,3712]{3,2,1,0:T(2,128)(2,1)} custom-call(bf16[4,8,2,1408]{3,2,1,0:T(2,128)(2,1)S(1)} %bitcast.14, f32[208,128]{1,0:T(8,128)S(1)} %add_convert_fusion.valid_ref, bf16[208,128]{1,0:T(8,128)(2,1)S(1)} %pad.4.place_ref, bf16[192,12288]{1,0:T(8,128)(2,1)} %bitcast.16, bf16[16,12288]{1,0:T(8,128)(2,1)S(1)} %fold.1.fold_ref, ...), custom_call_target="tpu_custom_call" | custom-call | flops 603979776 | bytes 4718592 | tf_op jit(solution)/shard_map/attend/pallas_call | solution.py:710
  60.6 2.8 %all-to-all-start.2 = ((bf16[32,2,3712]{2,1,0:T(2,128)(2,1)}), bf16[32,2,3712]{2,1,0:T(2,128)(2,1)S(1)}, u32[]{:S(2)}, u32[]{:S(2)}) async-start(bf16[32,2,3712]{2,1,0:T(2,128)(2,1)} %bitcast.9), calls=%async_computation.2 | async-start | bytes 950272 | tf_op jit(solution)/shard_map/all_to_all | solution.py:727
  63.4 10.4 %mlp.1 = (bf16[8,6144]{1,0:T(8,128)(2,1)S(1)}, bf16[8,6144]{1,0:T(8,128)(2,1)S(1)}, bf16[8,6144]{1,0:T(8,128)(2,1)S(1)}, bf16[8,6144]{1,0:T(8,128)(2,1)S(1)}) custom-call(bf16[64,768]{1,0:T(8,128)(2,1)S(1)} %get-tuple-element.33.refs_0_, bf16[64,768]{1,0:T(8,128)(2,1)S(1)} %collective-permute-done.4.refs_0_.refs_1_, ...), custom_call_target="tpu_custom_call" | custom-call | flops 603979776 | bytes 18874368 | tf_op jit(solution)/shard_map/mlp/pallas_call | solution.py:730
  73.8 1.6 %collective-permute-start.7 = (bf16[8,6144]{1,0:T(8,128)(2,1)S(1)}, bf16[8,6144]{1,0:T(8,128)(2,1)S(1)}, u32[]{:S(2)}, u32[]{:S(2)}) collective-permute-start(bf16[8,6144]{1,0:T(8,128)(2,1)S(1)} %get-tuple-element.38), channel_id=1, source_target_pairs={{0,8},{8,0},{16,24},{24,16},{1,9},{9,1},{17,25},{25,17},{2,10},{10... | collective-permute-start | bytes 294920 | tf_op jit(solution)/shard_map/ppermute | solution.py:547
  75.4 1.5 %collective-permute-start.8 = (bf16[8,6144]{1,0:T(8,128)(2,1)S(1)}, bf16[8,6144]{1,0:T(8,128)(2,1)S(1)}, u32[]{:S(2)}, u32[]{:S(2)}) collective-permute-start(bf16[8,6144]{1,0:T(8,128)(2,1)S(1)} %get-tuple-element.39), channel_id=1, source_target_pairs={{0,16},{8,24},{16,0},{24,8},{1,17},{9,25},{17,1},{25,9},{2,18},{10... | collective-permute-start | bytes 294920 | tf_op jit(solution)/shard_map/ppermute | solution.py:547
  76.9 0.5 collective-permute-start.9
  77.4 2.5 %collective-permute-done.7.refs_1_ = bf16[8,6144]{1,0:T(8,128)(2,1)S(1)} collective-permute-done((bf16[8,6144]{1,0:T(8,128)(2,1)S(1)}, bf16[8,6144]{1,0:T(8,128)(2,1)S(1)}, u32[]{:S(2)}, u32[]{:S(2)}) %collective-permute-start.7) | collective-permute-done | bytes 98336 | tf_op jit(solution)/shard_map/ppermute | solution.py:547
  79.9 2.6 %collective-permute-done.8.refs_2_ = bf16[8,6144]{1,0:T(8,128)(2,1)S(1)} collective-permute-done((bf16[8,6144]{1,0:T(8,128)(2,1)S(1)}, bf16[8,6144]{1,0:T(8,128)(2,1)S(1)}, u32[]{:S(2)}, u32[]{:S(2)}) %collective-permute-start.8) | collective-permute-done | bytes 98336 | tf_op jit(solution)/shard_map/ppermute | solution.py:547
  82.5 5.4 %merge.1 = bf16[8,8,768]{2,1,0:T(8,128)(2,1)} custom-call(bf16[32,2,3712]{2,1,0:T(2,128)(2,1)S(1)} %all-to-all-done.2.got_ref, bf16[8,896]{1,0:T(8,128)(2,1)S(1)} %get-tuple-element.34.own_ref, f32[136,8]{1,0:T(8,128)S(1)} %get-tuple-element.35.sel_ref, bf16[8,136]{1,0:T(8,128)(2,1)S(1)} %get-tuple-element.36.back_ref, ...), custom_call_target="tpu_custom_call" | custom-call | flops 75497472 | bytes 9437184 | tf_op jit(solution)/shard_map/merge/pallas_call | solution.py:748
  87.9 4.7 %all-to-all-start.3 = ((bf16[8,8,768]{2,1,0:T(8,128)(2,1)}), bf16[8,8,768]{2,1,0:T(8,128)(2,1)S(1)}, u32[]{:S(2)}, u32[]{:S(2)}) async-start(bf16[8,8,768]{2,1,0:T(8,128)(2,1)} %merge.1), calls=%async_computation.3 | async-start | bytes 196608 | tf_op jit(solution)/shard_map/all_to_all | solution.py:769
  92.6 1.3 %place.1 = bf16[12,8,1536]{2,1,0:T(8,128)(2,1)} custom-call(bf16[96,128]{1,0:T(8,128)(2,1)S(1)} %get-tuple-element.41.pick_ref, bf16[32,2,3712]{2,1,0:T(2,128)(2,1)S(1)} %all-to-all-done.2.got_ref), custom_call_target="tpu_custom_call" | custom-call | bytes 786432 | tf_op jit(solution)/shard_map/place/pallas_call | solution.py:772
  93.9 5.0 %all-to-all-done.3 = bf16[8,8,768]{2,1,0:T(8,128)(2,1)S(1)} async-done(((bf16[8,8,768]{2,1,0:T(8,128)(2,1)}), bf16[8,8,768]{2,1,0:T(8,128)(2,1)S(1)}, u32[]{:S(2)}, u32[]{:S(2)}) %all-to-all-start.3) | async-done | bytes 98336 | tf_op jit(solution)/shard_map/all_to_all | solution.py:769
  98.9 0.6 reduce_sum.72
  (39 shorter events, 0.8 us)
Async XLA Ops:
  2.3 19.1 %all-to-all-start = ((bf16[4,72,768]{2,1,0:T(8,128)(2,1)}), bf16[4,72,768]{2,1,0:T(8,128)(2,1)S(1)}, u32[]{:S(2)}, u32[]{:S(2)}) async-start(bf16[4,72,768]{2,1,0:T(8,128)(2,1)} %pack.1), calls=%async_computation | async-start | bytes 884736 | tf_op jit(solution)/shard_map/all_to_all | solution.py:561
  10.7 10.7 %collective-permute-start.3 = (s32[8,26]{1,0:T(8,128)S(1)}, s32[8,26]{1,0:T(8,128)S(1)}, u32[]{:S(2)}, u32[]{:S(2)}) collective-permute-start(s32[8,26]{1,0:T(8,128)S(1)} %get-tuple-element.27), channel_id=1, source_target_pairs={{0,24},{8,16},{16,8},{24,0},{1,25},{9,17},{17,9},{25,1},{2,26},{10... | collective-permute-start | bytes 2504 | tf_op jit(solution)/shard_map/ppermute | solution.py:547
  13.2 8.2 %collective-permute-start.2 = (s32[8,26]{1,0:T(8,128)S(1)}, s32[8,26]{1,0:T(8,128)S(1)}, u32[]{:S(2)}, u32[]{:S(2)}) collective-permute-start(s32[8,26]{1,0:T(8,128)S(1)} %get-tuple-element.27), channel_id=1, source_target_pairs={{0,16},{8,24},{16,0},{24,8},{1,17},{9,25},{17,1},{25,9},{2,18},{10... | collective-permute-start | bytes 2504 | tf_op jit(solution)/shard_map/ppermute | solution.py:547
  13.7 7.7 %collective-permute-start.1 = (s32[8,26]{1,0:T(8,128)S(1)}, s32[8,26]{1,0:T(8,128)S(1)}, u32[]{:S(2)}, u32[]{:S(2)}) collective-permute-start(s32[8,26]{1,0:T(8,128)S(1)} %get-tuple-element.27), channel_id=1, source_target_pairs={{0,8},{8,0},{16,24},{24,16},{1,9},{9,1},{17,25},{25,17},{2,10},{10... | collective-permute-start | bytes 2504 | tf_op jit(solution)/shard_map/ppermute | solution.py:547
  21.4 1.8 %collective-permute-start = (bf16[4,72,768]{2,1,0:T(8,128)(2,1)S(1)}, bf16[4,72,768]{2,1,0:T(8,128)(2,1)S(1)}, u32[]{:S(2)}, u32[]{:S(2)}) collective-permute-start(bf16[4,72,768]{2,1,0:T(8,128)(2,1)S(1)} %all-to-all-done.refs_0_), channel_id=1, source_target_pairs={{0,1},{1,0},{2,3},{3,2},{4,5},{5,4},{6,7},{7,6},{8,9},{9,8},{10,11... | collective-permute-start | bytes 1327112 | tf_op jit(solution)/shard_map/ppermute | solution.py:547
  23.2 12.4 %copy-start = (s32[32,12]{0,1:T(8,128)S(1)}, s32[32,12]{0,1:T(8,128)}, u32[]{:S(2)}) copy-start(s32[32,12]{0,1:T(8,128)} %param.26) | copy-start | bytes 4612
  23.2 13.2 %copy-start.1 = (f32[8,16]{1,0:T(8,128)S(1)}, f32[8,16]{1,0:T(8,128)}, u32[]{:S(2)}) copy-start(f32[8,16]{1,0:T(8,128)} %param.25) | copy-start | bytes 1540
  36.5 10.6 %collective-permute-start.4 = (bf16[64,768]{1,0:T(8,128)(2,1)S(1)}, bf16[64,768]{1,0:T(8,128)(2,1)S(1)}, u32[]{:S(2)}, u32[]{:S(2)}) collective-permute-start(bf16[64,768]{1,0:T(8,128)(2,1)S(1)} %get-tuple-element.33.refs_0_), channel_id=1, source_target_pairs={{0,8},{8,0},{16,24},{24,16},{1,9},{9,1},{17,25},{25,17},{2,10},{10... | collective-permute-start | bytes 294920 | tf_op jit(solution)/shard_map/ppermute | solution.py:547
  38.0 9.1 %collective-permute-start.5 = (bf16[64,768]{1,0:T(8,128)(2,1)S(1)}, bf16[64,768]{1,0:T(8,128)(2,1)S(1)}, u32[]{:S(2)}, u32[]{:S(2)}) collective-permute-start(bf16[64,768]{1,0:T(8,128)(2,1)S(1)} %get-tuple-element.33.refs_0_), channel_id=1, source_target_pairs={{0,16},{8,24},{16,0},{24,8},{1,17},{9,25},{17,1},{25,9},{2,18},{10... | collective-permute-start | bytes 294920 | tf_op jit(solution)/shard_map/ppermute | solution.py:547
  39.6 7.6 %collective-permute-start.6 = (bf16[64,768]{1,0:T(8,128)(2,1)S(1)}, bf16[64,768]{1,0:T(8,128)(2,1)S(1)}, u32[]{:S(2)}, u32[]{:S(2)}) collective-permute-start(bf16[64,768]{1,0:T(8,128)(2,1)S(1)} %get-tuple-element.33.refs_0_), channel_id=1, source_target_pairs={{0,24},{8,16},{16,8},{24,0},{1,25},{9,17},{17,9},{25,1},{2,26},{10... | collective-permute-start | bytes 294920 | tf_op jit(solution)/shard_map/ppermute | solution.py:547
  40.0 12.3 %all-to-all-start.1 = ((bf16[32,2,1408]{2,1,0:T(2,128)(2,1)}), bf16[32,2,1408]{2,1,0:T(2,128)(2,1)S(1)}, u32[]{:S(2)}, u32[]{:S(2)}) async-start(bf16[32,2,1408]{2,1,0:T(2,128)(2,1)} %get-tuple-element.28), calls=%async_computation.1 | async-start | bytes 360448 | tf_op jit(solution)/shard_map/all_to_all | solution.py:641
  60.6 21.8 %all-to-all-start.2 = ((bf16[32,2,3712]{2,1,0:T(2,128)(2,1)}), bf16[32,2,3712]{2,1,0:T(2,128)(2,1)S(1)}, u32[]{:S(2)}, u32[]{:S(2)}) async-start(bf16[32,2,3712]{2,1,0:T(2,128)(2,1)} %bitcast.9), calls=%async_computation.2 | async-start | bytes 950272 | tf_op jit(solution)/shard_map/all_to_all | solution.py:727
  73.8 6.1 %collective-permute-start.7 = (bf16[8,6144]{1,0:T(8,128)(2,1)S(1)}, bf16[8,6144]{1,0:T(8,128)(2,1)S(1)}, u32[]{:S(2)}, u32[]{:S(2)}) collective-permute-start(bf16[8,6144]{1,0:T(8,128)(2,1)S(1)} %get-tuple-element.38), channel_id=1, source_target_pairs={{0,8},{8,0},{16,24},{24,16},{1,9},{9,1},{17,25},{25,17},{2,10},{10... | collective-permute-start | bytes 294920 | tf_op jit(solution)/shard_map/ppermute | solution.py:547
  75.4 7.0 %collective-permute-start.8 = (bf16[8,6144]{1,0:T(8,128)(2,1)S(1)}, bf16[8,6144]{1,0:T(8,128)(2,1)S(1)}, u32[]{:S(2)}, u32[]{:S(2)}) collective-permute-start(bf16[8,6144]{1,0:T(8,128)(2,1)S(1)} %get-tuple-element.39), channel_id=1, source_target_pairs={{0,16},{8,24},{16,0},{24,8},{1,17},{9,25},{17,1},{25,9},{2,18},{10... | collective-permute-start | bytes 294920 | tf_op jit(solution)/shard_map/ppermute | solution.py:547
  76.9 5.6 %collective-permute-start.9 = (bf16[8,6144]{1,0:T(8,128)(2,1)S(1)}, bf16[8,6144]{1,0:T(8,128)(2,1)S(1)}, u32[]{:S(2)}, u32[]{:S(2)}) collective-permute-start(bf16[8,6144]{1,0:T(8,128)(2,1)S(1)} %get-tuple-element.40), channel_id=1, source_target_pairs={{0,24},{8,16},{16,8},{24,0},{1,25},{9,17},{17,9},{25,1},{2,26},{10... | collective-permute-start | bytes 294920 | tf_op jit(solution)/shard_map/ppermute | solution.py:547
  87.9 11.0 %all-to-all-start.3 = ((bf16[8,8,768]{2,1,0:T(8,128)(2,1)}), bf16[8,8,768]{2,1,0:T(8,128)(2,1)S(1)}, u32[]{:S(2)}, u32[]{:S(2)}) async-start(bf16[8,8,768]{2,1,0:T(8,128)(2,1)} %merge.1), calls=%async_computation.3 | async-start | bytes 196608 | tf_op jit(solution)/shard_map/all_to_all | solution.py:769

commit v2 on v1

--- a/solution.py
+++ b/solution.py
@@ -156,10 +156,86 @@
     number_ref[...] = jnp.concatenate(numbers, axis=1)
 
 
-def pack_kernel(held_ref, new_ref, out_ref):
-    held_rows = held_ref.shape[0]
+def facts_kernel(dims, *refs):
+    n_pages, pages_dev, slots = dims
+    number_refs, (table_ref, fold_ref, weight_ref, valid_ref, renew_ref) = refs[:n_pages], refs[n_pages:]
+    group = number_refs[0].shape[0]
+    requests = n_pages * group
+    ranks = n_pages * slots
+    mine = lax.axis_index("pages")
+    device = lax.axis_index(("pages", "blk"))
+    numbers = []
+    for g in range(n_pages):
+        got = number_refs[0][...]
+        for i in range(1, n_pages):
+            got = jnp.where(jnp.bitwise_xor(mine, g) == i, number_refs[i][...], got)
+        numbers.append(got.astype(F32))
+    numbers = jnp.concatenate(numbers, axis=0).astype(BF16)
+
+    local = iota((ranks, requests), 0)
+    hits = jnp.zeros((ranks, requests), F32)
+    slot = jnp.zeros((ranks, 1), F32)
+    for j in range(PPR):
+        one = jnp.where(local == table_ref[j : j + 1, :] - device * pages_dev, 1.0, 0.0)
+        hits = hits + one
+        slot = slot + j * jnp.sum(one, axis=1, keepdims=True)
+    hits = jnp.where(local < pages_dev, hits, 0.0)
+    facts = dot(hits.astype(BF16), numbers)
+    length, keeps = facts[:, :1], facts[:, 1 : 1 + KP]
+    choices, renewed = facts[:, 1 + KP : 1 + KP + PPR], facts[:, 1 + KP + PPR : 1 + KP + PPR + NREC]
+    place = iota((ranks, PPR), 1).astype(F32)
+    choice = jnp.sum(jnp.where(place == slot, choices, 0.0), axis=1, keepdims=True)
+    found = jnp.sum(hits, axis=1, keepdims=True) > 0.5
+    kept_hit = jnp.where(keeps == slot, 1.0, 0.0)
+    kept = (jnp.sum(kept_hit, axis=1, keepdims=True) > 0.5) & found
+    kept_place = PAGE * jnp.sum(kept_hit * iota((ranks, KP), 1).astype(F32), axis=1, keepdims=True)
+    dropped = jnp.logical_not(kept) & found & (slot * PAGE < length)
+
+    owner = jnp.concatenate(
+        [jnp.sum(hits[:, g * group : (g + 1) * group], axis=1, keepdims=True) for g in range(n_pages)], axis=1
+    )
+    below = jnp.where(iota((ranks, ranks), 0) > iota((ranks, ranks), 1), 1.0, 0.0).astype(BF16)
+    before = dot(below, owner.astype(BF16))
+    rank = jnp.sum(owner * (before + slots * iota((ranks, n_pages), 1).astype(F32)), axis=1, keepdims=True)
+    rank = jnp.where(found, rank, -1.0)
+    rank_hit = jnp.where(rank == iota((ranks, ranks), 1).astype(F32), 1.0, 0.0).astype(BF16)
+
+    weights = jnp.zeros((ranks, PAGE), F32)
+    for f in range(NF):
+        weights = jnp.where(choice == f, fold_ref[f : f + 1, :], weights)
+    live = slot * PAGE + iota((ranks, PAGE), 1).astype(F32) < length
+    weights = jnp.where(live & dropped, weights, 0.0)
+    weights = jnp.concatenate([weights] * pages_dev, axis=1)
+    tokens = pages_dev * PAGE
+    own = jnp.right_shift(iota((ranks, tokens), 1), 4) == iota((ranks, tokens), 0)
+    weights = jnp.where(own, weights, 0.0)
+    total = jnp.zeros((ranks, tokens), F32)
+    for part in parts_of(weights, 3):
+        total = total + dot_tn(rank_hit, part)
+    weight_ref[...] = total
+
+    lanes = valid_ref.shape[1]
+    lane_rank = jnp.bitwise_and(iota((ranks, lanes), 1), ranks - 1).astype(F32)
+    for_rank = jnp.where(lane_rank == rank, 1.0, 0.0)
+    kept_for = jnp.where(kept, for_rank, 0.0)
+    dropped_for = jnp.where(dropped, for_rank, 0.0)
+    renewed = jnp.concatenate([renewed] * (renew_ref.shape[1] // NREC), axis=1)
+    renewed = jnp.where(kept, renewed - kept_place, -1.0)
+    inside = iota((PAGE, renew_ref.shape[1]), 0).astype(F32)
+    for p in range(pages_dev):
+        some = slice(p * PAGE, (p + 1) * PAGE)
+        valid_ref[some, :] = jnp.broadcast_to(kept_for[p : p + 1, :], (PAGE, lanes))
+        renew_ref[some, :] = jnp.where(inside == renewed[p : p + 1, :], 1.0, 0.0).astype(BF16)
+    valid_ref[tokens:, :] = dot_tn(rank_hit, dropped_for.astype(BF16))
+    renew_ref[tokens:, :] = jnp.zeros((ranks, renew_ref.shape[1]), BF16)
+
+
+def pack_kernel(held_ref, new_ref, gain_ref, out_ref):
     group, chunk = new_ref.shape
     held = held_ref[...].astype(F32)
+    held = held - jnp.sum(held, axis=1, keepdims=True) / D
+    spread = jnp.sum(held * held, axis=1, keepdims=True) / D
+    held = held * lax.rsqrt(spread + EPSILON) * gain_ref[...]
     rows = [held[:, c * chunk : (c + 1) * chunk] for c in range(D // chunk)] + [new_ref[...].astype(F32)]
     rows = jnp.concatenate(rows, axis=0).astype(BF16)
     for i in range(out_ref.shape[0]):
@@ -169,7 +245,7 @@
 def project_kernel(dims, *refs):
     group, n_blk, held_rows, heads, slots = dims
     pack_refs, refs = refs[:2], refs[2:]
-    gain_ref, weight_hbm, cos_ref, low_ref, high_ref, sel_ref, *refs = refs
+    gain_ref, mlp_gain_ref, weight_hbm, cos_ref, low_ref, high_ref, sel_ref, *refs = refs
     send_ref, own_ref, leaf_ref, weight_buf, rows_ref, acc_ref, sems = refs
     chunk = D // n_blk
     width = 3 * heads * HD
@@ -197,24 +273,25 @@
             values = pack_refs[other][z].astype(F32)
             pieces.append(values[n_blk * held_rows :])
             places.append(b)
-            values = values[: n_blk * held_rows].reshape(n_blk, held_rows, chunk)
-            mean = jnp.sum(jnp.sum(values, axis=0), axis=1, keepdims=True) / D
-            values = values - mean[None]
-            spread = jnp.sum(jnp.sum(values * values, axis=0), axis=1, keepdims=True) / D
-            values = values * lax.rsqrt(spread + EPSILON)[None]
             first = pl.multiple_of(group + b * held_rows, 8)
             for c in range(n_blk):
-                rows_ref[c, pl.ds(first, held_rows), :] = values[c] * gain_ref[:, c * chunk : (c + 1) * chunk]
-    leaf_ref[...] = jnp.concatenate(pieces, axis=0).astype(BF16)
+                rows_ref[c, pl.ds(first, held_rows), :] = values[c * held_rows : (c + 1) * held_rows]
     mean = sum(jnp.sum(piece, axis=1, keepdims=True) for piece in pieces) / D
     pieces = [piece - mean for piece in pieces]
     spread = sum(jnp.sum(piece * piece, axis=1, keepdims=True) for piece in pieces) / D
     spread = lax.rsqrt(spread + EPSILON)
+    leaves = []
     for i, (b, piece) in enumerate(zip(places, pieces)):
         z = i % (n_blk // 2)
-        gain = gain_ref[:, 2 * z * chunk : 2 * (z + 1) * chunk]
-        gain = jnp.where(b == 2 * z, gain[:, :chunk], gain[:, chunk:])
-        rows_ref[b, 0:group, :] = piece * spread * gain
+        some = slice(2 * z * chunk, 2 * (z + 1) * chunk)
+        gain, mlp_gain = (
+            jnp.where(b == 2 * z, ref[:, some][:, :chunk], ref[:, some][:, chunk:])
+            for ref in (gain_ref, mlp_gain_ref)
+        )
+        piece = piece * spread
+        rows_ref[b, 0:group, :] = piece * gain
+        leaves.append(piece * mlp_gain)
+    leaf_ref[...] = jnp.concatenate(leaves, axis=0).astype(BF16)
 
     rows = acc_ref.shape[0]
     wide = heads * NREC
@@ -444,8 +521,8 @@
 def mlp_kernel(dims, *refs):
     group, n_pages, n_blk = dims
     leaf_refs, refs = refs[:n_pages], refs[n_pages:]
-    gain_ref, in_hbm, out_hbm, _, *refs = refs
-    part_refs, (in_buf, out_buf, rows_ref, sems_in, sems_out) = refs[:n_pages], refs[n_pages:]
+    in_hbm, out_hbm, _, *refs = refs
+    part_refs, (in_buf, out_buf, sems_in, sems_out) = refs[:n_pages], refs[n_pages:]
     chunk = D // n_blk
     n_steps, cols = out_buf.shape[0], out_buf.shape[2]
     core = jnp.bitwise_and(lax.axis_index("blk"), 1)
@@ -464,23 +541,15 @@
         in_copy(step).start()
     for step in range(n_steps):
         out_copy(step).start()
-    for g in range(n_pages):
-        leaf = leaf_refs[g][...].astype(F32)
-        pieces = [leaf[i * group : (i + 1) * group] for i in range(n_blk)]
-        mean = sum(jnp.sum(piece, axis=1, keepdims=True) for piece in pieces) / D
-        pieces = [piece - mean for piece in pieces]
-        spread = sum(jnp.sum(piece * piece, axis=1, keepdims=True) for piece in pieces) / D
-        spread = lax.rsqrt(spread + EPSILON)
-        for i in range(n_blk):
-            c = 2 * (i % (n_blk // 2)) + jnp.bitwise_xor(core, i // (n_blk // 2))
-            z = i % (n_blk // 2)
-            gain = gain_ref[:, 2 * z * chunk : 2 * (z + 1) * chunk]
-            gain = jnp.where(c == 2 * z, gain[:, :chunk], gain[:, chunk:])
-            rows_ref[c, g * group : (g + 1) * group, :] = pieces[i] * spread * gain
+    leaves = [ref[...].astype(F32) for ref in leaf_refs]
+    half = n_blk // 2
     hidden = jnp.zeros((n_pages * group, in_buf.shape[2]), F32)
-    for step in range(n_blk):
-        in_copy(step).wait()
-        hidden = hidden + dot(rows_ref[step].astype(BF16), in_buf[step])
+    for z in range(half):
+        in_copy(2 * z).wait()
+        in_copy(2 * z + 1).wait()
+        for i, c in ((z, 2 * z + core), (half + z, 2 * z + 1 - core)):
+            rows = [leaf[i * group : (i + 1) * group] for leaf in leaves]
+            hidden = hidden + dot(jnp.concatenate(rows, axis=0).astype(BF16), in_buf[c])
     active = (0.5 * hidden * (1.0 + lax.erf(hidden * math.sqrt(0.5)))).astype(BF16)
     for step in range(n_steps):
         out_copy(step).wait()
@@ -552,12 +621,12 @@
     half = n_blk // 2
     pack = pl.pallas_call(
         pack_kernel,
-        in_specs=[VMEM, VMEM],
+        in_specs=[VMEM] * 3,
         out_specs=VMEM,
         out_shape=shape_of((half, n_blk * held_rows + group, chunk)),
         compiler_params=params_of(16),
         name="pack",
-    )(fixed(held_states.reshape(held_rows, D)), fixed(new_hidden))
+    )(fixed(held_states.reshape(held_rows, D)), fixed(new_hidden), fixed(attn_gain[None]))
     pack = lax.all_to_all(
         pack,
         "blk",
@@ -598,9 +667,7 @@
         fixed(jnp.asarray(frequency[None])),
     )
 
-    numbers = jnp.concatenate(
-        [numbers] + [swapped(numbers, "pages", n_pages, i) for i in range(1, n_pages)], axis=0
-    )
+    numbers = [numbers] + [swapped(numbers, "pages", n_pages, i) for i in range(1, n_pages)]
 
     tokens = pages_dev * PAGE
     pages = page_store.reshape(tokens, 2 * D)
@@ -612,7 +679,7 @@
     wire = lanes + wire_split(lanes)
     send, own, leaf = pl.pallas_call(
         functools.partial(project_kernel, (group, n_blk, held_rows, heads, slots)),
-        in_specs=[VMEM] * 3 + [HBM] + [VMEM] * 4,
+        in_specs=[VMEM] * 4 + [HBM] + [VMEM] * 4,
         out_specs=[VMEM] * 3,
         out_shape=[
             shape_of((n_dev, 2, wire)),
@@ -631,62 +698,28 @@
     )(
         *packs,
         fixed(attn_gain[None]),
+        fixed(mlp_gain[None]),
         fixed(qkv_weight),
         cosine,
         low,
         high,
         sel,
     )
-    send, numbers, late_table = lax.optimization_barrier((send, numbers, page_table))
+    send, *numbers = lax.optimization_barrier((send, *numbers))
     asked = lax.all_to_all(send, ("pages", "blk"), 0, 0, tiled=True)
-
-    token = jnp.arange(tokens, dtype=jnp.int32)
-    local, inside = token // PAGE, token % PAGE
-    found = late_table[:, :, None] == (device * pages_dev + local)[None, None, :]
-    request_hit = jnp.any(found, axis=1)
-    slot_hit = jnp.any(found, axis=0)
-    slot_ids = jnp.arange(PPR, dtype=jnp.int32)
-    slot = jnp.sum(jnp.where(slot_hit, slot_ids[:, None], 0), axis=0)
-    request = jnp.sum(jnp.where(request_hit, jnp.arange(n_pages * group, dtype=jnp.int32)[:, None], 0), axis=0)
-    owner = request // group
-    request_hit = (
-        jnp.arange(n_pages * group, dtype=jnp.int32)[:, None]
-        == (jnp.bitwise_xor(owner, mine) * group + request % group)[None]
-    )
-    facts = jnp.dot(numbers.astype(BF16).T, request_hit.astype(BF16), preferred_element_type=F32).astype(jnp.int32)
-    length, keeps = facts[0], facts[1 : 1 + KP]
-    choices, renewed = facts[1 + KP : 1 + KP + PPR], facts[1 + KP + PPR :]
-    choice = jnp.sum(jnp.where(slot_hit, choices, 0), axis=0)
-    kept_hit = keeps == slot[None]
-    kept = jnp.any(kept_hit, axis=0)
-    kept_place = jnp.sum(jnp.where(kept_hit, jnp.arange(KP, dtype=jnp.int32)[:, None] * PAGE, 0), axis=0)
-    dropped = jnp.logical_and(jnp.logical_not(kept), slot * PAGE < length)
-    live = slot * PAGE + inside < length
-    fold_row = jnp.sum(
-        jnp.where(
-            choice[None] == jnp.arange(NF, dtype=jnp.int32)[:, None],
-            jnp.tile(fold_weights, (1, pages_dev)),
-            0.0,
-        ),
-        axis=0,
-    )
-    earlier = (owner[:, None] == owner[None]) & (local[:, None] < local[None]) & (inside == 0)[:, None]
-    rank_in = jnp.sum(earlier.astype(jnp.int32), axis=0)
-    rank = owner * slots + rank_in
-    ids = jnp.arange(ranks, dtype=jnp.int32)
-    rank_hit = ids[:, None] == rank[None]
-    fold_rows = jnp.where(rank_hit & (dropped & live)[None], fold_row[None], 0.0)
-    fold_drop = jnp.any(rank_hit & dropped[None], axis=1)
-    octet_lane = jnp.arange(OCTET * ranks, dtype=jnp.int32) % ranks
-    valid = jnp.concatenate(
-        [
-            ((rank[:, None] == octet_lane[None]) & kept[:, None]).astype(F32),
-            ((ids[:, None] == octet_lane[None]) & fold_drop[:, None]).astype(F32),
+    fold_rows, valid, renew = pl.pallas_call(
+        functools.partial(facts_kernel, (n_pages, pages_dev, slots)),
+        in_specs=[VMEM] * (n_pages + 2),
+        out_specs=[VMEM] * 3,
+        out_shape=[
+            shape_of((ranks, tokens), F32),
+            shape_of((tokens + ranks, OCTET * ranks), F32),
+            shape_of((tokens + ranks, 2 * OCTET * NREC)),
         ],
-        axis=0,
-    )
-    renew = ((renewed == (kept_place + inside)[None]) & kept[None]).astype(BF16)
-    renew = jnp.pad(jnp.tile(renew.T, (1, 2 * OCTET)), ((0, ranks), (0, 0)))
+        compiler_params=params_of(16),
+        cost_estimate=cost_of(0, 0),
+        name="facts",
+    )(*numbers, fixed(page_table.T), fixed(fold_weights))
 
     leaf, fold_rows = lax.optimization_barrier((leaf, fold_rows))
     leaves = [leaf] + [swapped(leaf, "pages", n_pages, i) for i in range(1, n_pages)]
@@ -716,33 +749,32 @@
             pl.BlockSpec((tokens + ranks, 2 * OCTET * NREC), lambda i: (0, 0)),
             pl.BlockSpec((tokens, step_lanes), lambda i: (0, i)),
             pl.BlockSpec((ranks, step_lanes), lambda i: (0, i)),
-            *[ANY] * (n_pages - 1),
         ],
         out_specs=pl.BlockSpec((n_pages, dests, 2, all_wire), lambda i: (0, i, 0, 0)),
         out_shape=shape_of((n_pages, n_blk, 2, all_wire)),
         compiler_params=params_of(16),
         cost_estimate=cost_of(2 * 128 * tokens * 2 * D, tokens * 4 * D),
         name="attend",
-    )(asked.reshape(n_pages, n_blk, 2, wire), valid, renew, fixed(pages), folded_rows, *leaves[1:])
+    )(asked.reshape(n_pages, n_blk, 2, wire), valid, renew, fixed(pages), folded_rows)
+    partial, *leaves = lax.optimization_barrier((partial, *leaves))
     got = lax.all_to_all(partial.reshape(n_dev, 2, all_wire), ("pages", "blk"), 0, 0, tiled=True)
 
     hidden = in_weight.shape[1]
     mlp_parts = pl.pallas_call(
         functools.partial(mlp_kernel, (group, n_pages, n_blk)),
-        in_specs=[VMEM] * (n_pages + 1) + [HBM, HBM, ANY],
+        in_specs=[VMEM] * n_pages + [HBM, HBM, ANY],
         out_specs=[VMEM] * n_pages,
         out_shape=[shape_of((group, D))] * n_pages,
         scratch_shapes=[
             pltpu.VMEM((n_blk, chunk, hidden), BF16),
             pltpu.VMEM((8, hidden, D // 8), BF16),
-            pltpu.VMEM((n_blk, n_pages * group, chunk), F32),
             pltpu.SemaphoreType.DMA((n_blk,)),
             pltpu.SemaphoreType.DMA((8,)),
         ],
         compiler_params=params_of(24),
         cost_estimate=cost_of(4 * n_pages * group * D * hidden, 4 * D * hidden),
         name="mlp",
-    )(*leaves, fixed(mlp_gain[None]), fixed(in_weight), fixed(out_weight), partial)
+    )(*leaves, fixed(in_weight), fixed(out_weight), partial)
     mlp_share = [mlp_parts[0]] + [swapped(mlp_parts[i], "pages", n_pages, i) for i in range(1, n_pages)]
 
     out_part = pl.pallas_call(

time: 100 us -> 101 us (1.010)
  blocking collectives: 0 us -> 18.9 us
  waiting for transfers between devices: 24.2 us -> 11.4 us
  starting transfers between devices: 28.1 us -> 23.8 us
    all_to_all x0 -> x1, blocking collectives: none -> 18.9 us  [on_device(): lax.all_to_all(pack, 'blk', 0, 0, axis_index_groups=[list(range(core, n_b...]
    all_to_all x1 -> x0, waiting for transfers between devices: 7.13 us -> none  [on_device(): lax.all_to_all(pack, 'blk', 0, 0, axis_index_groups=[list(range(core, n_b...]
    all_to_all x1 -> x0, starting transfers between devices: 6.32 us -> none  [on_device(): lax.all_to_all(pack, 'blk', 0, 0, axis_index_groups=[list(range(core, n_b...]
    all_to_all x1, waiting for transfers between devices: 5.21 us -> 0.79 us  [on_device(): asked = lax.all_to_all(send, ('pages', 'blk'), 0, 0, tiled=True)]
    all_to_all x1, starting transfers between devices: 2.78 us -> 5.07 us  [on_device(): lax.all_to_all(partial.reshape(n_dev, 2, all_wire), ('pages', 'blk'), 0,...]
    ppermute x10, waiting for transfers between devices: 6.82 us -> 5.6 us  [swapped(): return lax.ppermute(array, axis, [(i, i ^ by) for i in range(size)])]
    pallas_call x1 -> x2, Pallas kernels: 1.69 us -> 2.61 us  [the longest x1 1.39 us: on_device(): pl.pallas_call(functools.partial(facts_kernel, (n_pages, pages_dev, slots...]
  transfers between devices with their start and end apart: 14 -> 13, of which waited for: 6 -> 4; matrix products, arithmetic and copies ran while one was open for 0% -> 0% of each run, Pallas kernels for 17% -> 38%
where the time goes in v2:
time: 101 us; the launch traced here: 100 us
  Pallas kernels  44.7 us (44%)
  starting transfers between devices  23.8 us (24%)
  blocking collectives  18.9 us (19%)
  waiting for transfers between devices  11.4 us (11%)
    all_to_all x1, blocking collectives, on_device(): lax.all_to_all(pack, 'blk', 0, 0, axis_index_groups=[list(range(core, n_b...  18.9 us
    pallas_call x1, Pallas kernels, on_device(): pl.pallas_call(functools.partial(project_kernel, (group, n_blk, held_rows...  12.3 us
    ppermute x10, starting transfers between devices, swapped(): return lax.ppermute(array, axis, [(i, i ^ by) for i in range(size)])  10.7 us
    pallas_call x1, Pallas kernels, on_device(): pl.pallas_call(functools.partial(mlp_kernel, (group, n_pages, n_blk)), in...  9.79 us
    pallas_call x1, Pallas kernels, on_device(): pl.pallas_call(functools.partial(attend_kernel, (n_pages, slots, dests, h...  8.3 us
    ppermute x10, waiting for transfers between devices, swapped(): return lax.ppermute(array, axis, [(i, i ^ by) for i in range(size)])  5.6 us
    pallas_call x1, Pallas kernels, on_device(): pl.pallas_call(functools.partial(merge_kernel, (group, n_dev, slots, head...  5.47 us
    all_to_all x1, starting transfers between devices, on_device(): lax.all_to_all(partial.reshape(n_dev, 2, all_wire), ('pages', 'blk'), 0,...  5.07 us
  transfers between devices with their start and end apart: 13, of which 4 were waited for; matrix products, arithmetic and copies ran while one was open for 0% of the time, Pallas kernels for 38%

profile of v2, /device:TPU:0, one launch (start us, length us, event | category | flops | bytes accessed | tf_op | source)
XLA Modules:
  0.0 100.1 jit_solution(16444331945669952292)
XLA Ops:
  0.6 1.2 %pack.1 = bf16[4,72,768]{2,1,0:T(8,128)(2,1)S(1)} custom-call(bf16[8,6144]{1,0:T(8,128)(2,1)} %bitcast.15, bf16[8,768]{1,0:T(8,128)(2,1)} %new_ref.1, f32[1,6144]{1,0:T(1,128)} %bitcast.13), custom_call_target="tpu_custom_call" | custom-call | tf_op jit(solution)/shard_map/pack/pallas_call | solution.py:622
  1.8 18.9 %all_to_all.20.refs_0_ = bf16[4,72,768]{2,1,0:T(8,128)(2,1)S(1)} all-to-all(bf16[4,72,768]{2,1,0:T(8,128)(2,1)S(1)} %pack.1), channel_id=1, replica_groups={{0,2,4,6},{1,3,5,7},{8,10,12,14},{9,11,13,15},{16,18,20,22},{17,19,21,2..., dimensions={0} | all-to-all | bytes 884736 | tf_op jit(solution)/shard_map/all_to_all | solution.py:630
  20.7 0.0 collective-permute-start
  20.7 2.0 %prep.1 = (f32[72,1152]{1,0:T(8,128)S(1)}, f32[72,1152]{1,0:T(8,128)S(1)}, f32[72,1152]{1,0:T(8,128)S(1)}, bf16[128,8]{1,0:T(8,128)(2,1)S(1)}, f32[136,8]{1,0:T(...) custom-call(s32[12,32]{1,0:T(8,128)} %bitcast.16, s32[12,32]{1,0:T(8,128)} %bitcast.17, ...), custom_call_target="tpu_custom_call" | custom-call | tf_op jit(solution)/shard_map/prep/pallas_call | solution.py:645
  22.7 2.5 %collective-permute-start.3 = (s32[8,26]{1,0:T(8,128)S(1)}, s32[8,26]{1,0:T(8,128)S(1)}, u32[]{:S(2)}, u32[]{:S(2)}) collective-permute-start(s32[8,26]{1,0:T(8,128)S(1)} %get-tuple-element.39.refs_0_), channel_id=1, source_target_pairs={{0,24},{8,16},{16,8},{24,0},{1,25},{9,17},{17,9},{25,1},{2,26},{10... | collective-permute-start | bytes 2504 | tf_op jit(solution)/shard_map/ppermute | solution.py:616
  25.3 0.5 collective-permute-start.2
  25.8 0.5 collective-permute-start.1
  26.3 12.3 %project.1 = (bf16[32,2,1408]{2,1,0:T(2,128)(2,1)}, bf16[8,896]{1,0:T(8,128)(2,1)S(1)}, bf16[64,768]{1,0:T(8,128)(2,1)S(1)}) custom-call(bf16[4,72,768]{2,1,0:T(8,128)(2,1)S(1)} %all_to_all.20.refs_0_, bf16[4,72,768]{2,1,0:T(8,128)(2,1)S(1)} %collective-permute-done.refs_1_, f32[1,6144]{1,0:T(1,128)} %bitcast.14, f32[1,6144]{1,0:T(1,128)} %bitcast.19, ...), custom_call_target="tpu_custom_call" | custom-call | flops 2038431744 | bytes 28311552 | tf_op jit(solution)/shard_map/project/pallas_call | solution.py:680
  38.7 0.0 collective-permute-done.3.refs_3_
  38.7 0.0 collective-permute-done.1.refs_1_
  38.7 3.7 %all-to-all-start.1 = ((bf16[32,2,1408]{2,1,0:T(2,128)(2,1)}), bf16[32,2,1408]{2,1,0:T(2,128)(2,1)S(1)}, u32[]{:S(2)}, u32[]{:S(2)}) async-start(bf16[32,2,1408]{2,1,0:T(2,128)(2,1)} %get-tuple-element.38), calls=%async_computation.1 | async-start | bytes 360448 | tf_op jit(solution)/shard_map/all_to_all | solution.py:709
  42.4 1.4 %facts.1 = (f32[16,192]{1,0:T(8,128)S(1)}, f32[208,128]{1,0:T(8,128)S(1)}, bf16[208,128]{1,0:T(8,128)(2,1)S(1)}) custom-call(s32[8,26]{1,0:T(8,128)S(1)} %get-tuple-element.39.refs_0_, s32[8,26]{1,0:T(8,128)S(1)} %collective-permute-done.1.refs_1_, s32[8,26]{1,0:T(8,128)S(1)} %collective-permute-done.2.refs_2_, s32[8,26]{1,0:T(8,128)S(1)} %collective-permute-done.3.refs_3_, ...), custom_call_target="tpu_custom_call" | custom-call | tf_op jit(solution)/shard_map/facts/pallas_call | solution.py:710
  43.8 2.7 %collective-permute-start.6 = (bf16[64,768]{1,0:T(8,128)(2,1)S(1)}, bf16[64,768]{1,0:T(8,128)(2,1)S(1)}, u32[]{:S(2)}, u32[]{:S(2)}) collective-permute-start(bf16[64,768]{1,0:T(8,128)(2,1)S(1)} %get-tuple-element.53.refs_0_), channel_id=1, source_target_pairs={{0,24},{8,16},{16,8},{24,0},{1,25},{9,17},{17,9},{25,1},{2,26},{10... | collective-permute-start | bytes 294920 | tf_op jit(solution)/shard_map/ppermute | solution.py:616
  46.5 0.6 collective-permute-start.5
  47.1 0.3 collective-permute-start.4
  47.4 2.9 %fold.1.fold_ref = bf16[16,12288]{1,0:T(8,128)(2,1)S(1)} custom-call(f32[16,192]{1,0:T(8,128)S(1)} %get-tuple-element.47.weight_ref, bf16[192,12288]{1,0:T(8,128)(2,1)} %bitcast.10), custom_call_target="tpu_custom_call" | custom-call | tf_op jit(solution)/shard_map/fold/pallas_call | solution.py:727
  50.2 0.8 all-to-all-done.1
  51.0 8.3 %attend.1.refs_6_ = bf16[4,8,2,3712]{3,2,1,0:T(2,128)(2,1)} custom-call(bf16[4,8,2,1408]{3,2,1,0:T(2,128)(2,1)S(1)} %bitcast.9, f32[208,128]{1,0:T(8,128)S(1)} %get-tuple-element.43.valid_ref, bf16[208,128]{1,0:T(8,128)(2,1)S(1)} %get-tuple-element.44.place_ref, bf16[192,12288]{1,0:T(8,128)(2,1)} %bitcast.11, bf16[16,12288]{1,0:T(8,128)(2,1)S(1)} %fold.1.fold_ref), custom_call_target="tpu_custom_call" | custom-call | flops 603979776 | bytes 4718592 | tf_op jit(solution)/shard_map/attend/pallas_call | solution.py:743
  59.3 0.0 collective-permute-done.6.refs_3_
  59.3 0.0 collective-permute-done.5.refs_2_
  59.3 5.1 %all-to-all-start.2 = ((bf16[32,2,3712]{2,1,0:T(2,128)(2,1)}), bf16[32,2,3712]{2,1,0:T(2,128)(2,1)S(1)}, u32[]{:S(2)}, u32[]{:S(2)}) async-start(bf16[32,2,3712]{2,1,0:T(2,128)(2,1)} %bitcast.7), calls=%async_computation.2 | async-start | bytes 950272 | tf_op jit(solution)/shard_map/all_to_all | solution.py:760
  64.4 9.8 %mlp.1 = (bf16[8,6144]{1,0:T(8,128)(2,1)S(1)}, bf16[8,6144]{1,0:T(8,128)(2,1)S(1)}, bf16[8,6144]{1,0:T(8,128)(2,1)S(1)}, bf16[8,6144]{1,0:T(8,128)(2,1)S(1)}) custom-call(bf16[64,768]{1,0:T(8,128)(2,1)S(1)} %get-tuple-element.53.refs_0_, bf16[64,768]{1,0:T(8,128)(2,1)S(1)} %collective-permute-done.4.refs_1_, ...), custom_call_target="tpu_custom_call" | custom-call | flops 603979776 | bytes 18874368 | tf_op jit(solution)/shard_map/mlp/pallas_call | solution.py:763
  74.2 1.8 %collective-permute-start.7 = (bf16[8,6144]{1,0:T(8,128)(2,1)S(1)}, bf16[8,6144]{1,0:T(8,128)(2,1)S(1)}, u32[]{:S(2)}, u32[]{:S(2)}) collective-permute-start(bf16[8,6144]{1,0:T(8,128)(2,1)S(1)} %get-tuple-element.58), channel_id=1, source_target_pairs={{0,8},{8,0},{16,24},{24,16},{1,9},{9,1},{17,25},{25,17},{2,10},{10... | collective-permute-start | bytes 294920 | tf_op jit(solution)/shard_map/ppermute | solution.py:616
  76.0 1.5 %collective-permute-start.8 = (bf16[8,6144]{1,0:T(8,128)(2,1)S(1)}, bf16[8,6144]{1,0:T(8,128)(2,1)S(1)}, u32[]{:S(2)}, u32[]{:S(2)}) collective-permute-start(bf16[8,6144]{1,0:T(8,128)(2,1)S(1)} %get-tuple-element.59), channel_id=1, source_target_pairs={{0,16},{8,24},{16,0},{24,8},{1,17},{9,25},{17,1},{25,9},{2,18},{10... | collective-permute-start | bytes 294920 | tf_op jit(solution)/shard_map/ppermute | solution.py:616
  77.5 0.3 collective-permute-start.9
  77.8 2.2 %collective-permute-done.7.refs_1_ = bf16[8,6144]{1,0:T(8,128)(2,1)S(1)} collective-permute-done((bf16[8,6144]{1,0:T(8,128)(2,1)S(1)}, bf16[8,6144]{1,0:T(8,128)(2,1)S(1)}, u32[]{:S(2)}, u32[]{:S(2)}) %collective-permute-start.7) | collective-permute-done | bytes 98336 | tf_op jit(solution)/shard_map/ppermute | solution.py:616
  80.0 3.4 %collective-permute-done.8.refs_2_ = bf16[8,6144]{1,0:T(8,128)(2,1)S(1)} collective-permute-done((bf16[8,6144]{1,0:T(8,128)(2,1)S(1)}, bf16[8,6144]{1,0:T(8,128)(2,1)S(1)}, u32[]{:S(2)}, u32[]{:S(2)}) %collective-permute-start.8) | collective-permute-done | bytes 98336 | tf_op jit(solution)/shard_map/ppermute | solution.py:616
  83.4 5.5 %merge.1 = bf16[8,8,768]{2,1,0:T(8,128)(2,1)} custom-call(bf16[32,2,3712]{2,1,0:T(2,128)(2,1)S(1)} %all-to-all-done.2.got_ref, bf16[8,896]{1,0:T(8,128)(2,1)S(1)} %get-tuple-element.50.own_ref, f32[136,8]{1,0:T(8,128)S(1)} %get-tuple-element.51.sel_ref, bf16[8,136]{1,0:T(8,128)(2,1)S(1)} %get-tuple-element.52.back_ref, ...), custom_call_target="tpu_custom_call" | custom-call | flops 75497472 | bytes 9437184 | tf_op jit(solution)/shard_map/merge/pallas_call | solution.py:780
  88.8 4.3 %all-to-all-start.3 = ((bf16[8,8,768]{2,1,0:T(8,128)(2,1)}), bf16[8,8,768]{2,1,0:T(8,128)(2,1)S(1)}, u32[]{:S(2)}, u32[]{:S(2)}) async-start(bf16[8,8,768]{2,1,0:T(8,128)(2,1)} %merge.1), calls=%async_computation.3 | async-start | bytes 196608 | tf_op jit(solution)/shard_map/all_to_all | solution.py:801
  93.2 1.3 %place.1 = bf16[12,8,1536]{2,1,0:T(8,128)(2,1)} custom-call(bf16[96,128]{1,0:T(8,128)(2,1)S(1)} %get-tuple-element.61.pick_ref, bf16[32,2,3712]{2,1,0:T(2,128)(2,1)S(1)} %all-to-all-done.2.got_ref), custom_call_target="tpu_custom_call" | custom-call | bytes 786432 | tf_op jit(solution)/shard_map/place/pallas_call | solution.py:804
  94.5 5.0 %all-to-all-done.3 = bf16[8,8,768]{2,1,0:T(8,128)(2,1)S(1)} async-done(((bf16[8,8,768]{2,1,0:T(8,128)(2,1)}), bf16[8,8,768]{2,1,0:T(8,128)(2,1)S(1)}, u32[]{:S(2)}, u32[]{:S(2)}) %all-to-all-start.3) | async-done | bytes 98336 | tf_op jit(solution)/shard_map/all_to_all | solution.py:801
  99.5 0.6 reduce_sum.12
  (5 shorter events, 0.0 us)
Async XLA Ops:
  20.7 5.6 %collective-permute-start = (bf16[4,72,768]{2,1,0:T(8,128)(2,1)S(1)}, bf16[4,72,768]{2,1,0:T(8,128)(2,1)S(1)}, u32[]{:S(2)}, u32[]{:S(2)}) collective-permute-start(bf16[4,72,768]{2,1,0:T(8,128)(2,1)S(1)} %all_to_all.20.refs_0_), channel_id=1, source_target_pairs={{0,1},{1,0},{2,3},{3,2},{4,5},{5,4},{6,7},{7,6},{8,9},{9,8},{10,11... | collective-permute-start | bytes 1327112 | tf_op jit(solution)/shard_map/ppermute | solution.py:616
  22.7 15.9 %collective-permute-start.3 = (s32[8,26]{1,0:T(8,128)S(1)}, s32[8,26]{1,0:T(8,128)S(1)}, u32[]{:S(2)}, u32[]{:S(2)}) collective-permute-start(s32[8,26]{1,0:T(8,128)S(1)} %get-tuple-element.39.refs_0_), channel_id=1, source_target_pairs={{0,24},{8,16},{16,8},{24,0},{1,25},{9,17},{17,9},{25,1},{2,26},{10... | collective-permute-start | bytes 2504 | tf_op jit(solution)/shard_map/ppermute | solution.py:616
  25.3 13.4 %collective-permute-start.2 = (s32[8,26]{1,0:T(8,128)S(1)}, s32[8,26]{1,0:T(8,128)S(1)}, u32[]{:S(2)}, u32[]{:S(2)}) collective-permute-start(s32[8,26]{1,0:T(8,128)S(1)} %get-tuple-element.39.refs_0_), channel_id=1, source_target_pairs={{0,16},{8,24},{16,0},{24,8},{1,17},{9,25},{17,1},{25,9},{2,18},{10... | collective-permute-start | bytes 2504 | tf_op jit(solution)/shard_map/ppermute | solution.py:616
  25.8 12.9 %collective-permute-start.1 = (s32[8,26]{1,0:T(8,128)S(1)}, s32[8,26]{1,0:T(8,128)S(1)}, u32[]{:S(2)}, u32[]{:S(2)}) collective-permute-start(s32[8,26]{1,0:T(8,128)S(1)} %get-tuple-element.39.refs_0_), channel_id=1, source_target_pairs={{0,8},{8,0},{16,24},{24,16},{1,9},{9,1},{17,25},{25,17},{2,10},{10... | collective-permute-start | bytes 2504 | tf_op jit(solution)/shard_map/ppermute | solution.py:616
  38.7 12.3 %all-to-all-start.1 = ((bf16[32,2,1408]{2,1,0:T(2,128)(2,1)}), bf16[32,2,1408]{2,1,0:T(2,128)(2,1)S(1)}, u32[]{:S(2)}, u32[]{:S(2)}) async-start(bf16[32,2,1408]{2,1,0:T(2,128)(2,1)} %get-tuple-element.38), calls=%async_computation.1 | async-start | bytes 360448 | tf_op jit(solution)/shard_map/all_to_all | solution.py:709
  43.8 15.5 %collective-permute-start.6 = (bf16[64,768]{1,0:T(8,128)(2,1)S(1)}, bf16[64,768]{1,0:T(8,128)(2,1)S(1)}, u32[]{:S(2)}, u32[]{:S(2)}) collective-permute-start(bf16[64,768]{1,0:T(8,128)(2,1)S(1)} %get-tuple-element.53.refs_0_), channel_id=1, source_target_pairs={{0,24},{8,16},{16,8},{24,0},{1,25},{9,17},{17,9},{25,1},{2,26},{10... | collective-permute-start | bytes 294920 | tf_op jit(solution)/shard_map/ppermute | solution.py:616
  46.5 12.8 %collective-permute-start.5 = (bf16[64,768]{1,0:T(8,128)(2,1)S(1)}, bf16[64,768]{1,0:T(8,128)(2,1)S(1)}, u32[]{:S(2)}, u32[]{:S(2)}) collective-permute-start(bf16[64,768]{1,0:T(8,128)(2,1)S(1)} %get-tuple-element.53.refs_0_), channel_id=1, source_target_pairs={{0,16},{8,24},{16,0},{24,8},{1,17},{9,25},{17,1},{25,9},{2,18},{10... | collective-permute-start | bytes 294920 | tf_op jit(solution)/shard_map/ppermute | solution.py:616
  47.1 12.2 %collective-permute-start.4 = (bf16[64,768]{1,0:T(8,128)(2,1)S(1)}, bf16[64,768]{1,0:T(8,128)(2,1)S(1)}, u32[]{:S(2)}, u32[]{:S(2)}) collective-permute-start(bf16[64,768]{1,0:T(8,128)(2,1)S(1)} %get-tuple-element.53.refs_0_), channel_id=1, source_target_pairs={{0,8},{8,0},{16,24},{24,16},{1,9},{9,1},{17,25},{25,17},{2,10},{10... | collective-permute-start | bytes 294920 | tf_op jit(solution)/shard_map/ppermute | solution.py:616
  59.3 24.0 %all-to-all-start.2 = ((bf16[32,2,3712]{2,1,0:T(2,128)(2,1)}), bf16[32,2,3712]{2,1,0:T(2,128)(2,1)S(1)}, u32[]{:S(2)}, u32[]{:S(2)}) async-start(bf16[32,2,3712]{2,1,0:T(2,128)(2,1)} %bitcast.7), calls=%async_computation.2 | async-start | bytes 950272 | tf_op jit(solution)/shard_map/all_to_all | solution.py:760
  74.2 5.8 %collective-permute-start.7 = (bf16[8,6144]{1,0:T(8,128)(2,1)S(1)}, bf16[8,6144]{1,0:T(8,128)(2,1)S(1)}, u32[]{:S(2)}, u32[]{:S(2)}) collective-permute-start(bf16[8,6144]{1,0:T(8,128)(2,1)S(1)} %get-tuple-element.58), channel_id=1, source_target_pairs={{0,8},{8,0},{16,24},{24,16},{1,9},{9,1},{17,25},{25,17},{2,10},{10... | collective-permute-start | bytes 294920 | tf_op jit(solution)/shard_map/ppermute | solution.py:616
  76.0 7.3 %collective-permute-start.8 = (bf16[8,6144]{1,0:T(8,128)(2,1)S(1)}, bf16[8,6144]{1,0:T(8,128)(2,1)S(1)}, u32[]{:S(2)}, u32[]{:S(2)}) collective-permute-start(bf16[8,6144]{1,0:T(8,128)(2,1)S(1)} %get-tuple-element.59), channel_id=1, source_target_pairs={{0,16},{8,24},{16,0},{24,8},{1,17},{9,25},{17,1},{25,9},{2,18},{10... | collective-permute-start | bytes 294920 | tf_op jit(solution)/shard_map/ppermute | solution.py:616
  77.5 5.8 %collective-permute-start.9 = (bf16[8,6144]{1,0:T(8,128)(2,1)S(1)}, bf16[8,6144]{1,0:T(8,128)(2,1)S(1)}, u32[]{:S(2)}, u32[]{:S(2)}) collective-permute-start(bf16[8,6144]{1,0:T(8,128)(2,1)S(1)} %get-tuple-element.60), channel_id=1, source_target_pairs={{0,24},{8,16},{16,8},{24,0},{1,25},{9,17},{17,9},{25,1},{2,26},{10... | collective-permute-start | bytes 294920 | tf_op jit(solution)/shard_map/ppermute | solution.py:616
  88.8 10.7 %all-to-all-start.3 = ((bf16[8,8,768]{2,1,0:T(8,128)(2,1)}), bf16[8,8,768]{2,1,0:T(8,128)(2,1)S(1)}, u32[]{:S(2)}, u32[]{:S(2)}) async-start(bf16[8,8,768]{2,1,0:T(8,128)(2,1)} %merge.1), calls=%async_computation.3 | async-start | bytes 196608 | tf_op jit(solution)/shard_map/all_to_all | solution.py:801

commit v3 on v2

--- a/solution.py
+++ b/solution.py
@@ -95,7 +95,10 @@
 
 def prep_kernel(dims, table_smem, table_ref, length_ref, keep_ref, choice_ref, list_ref, frequency_ref, *refs):
     n_pages, pages_dev, slots, period_heads = dims
-    cos_ref, low_ref, high_ref, sel_ref, sel_all_ref, back_ref, pick_ref, number_ref = refs
+    attn_gain_ref, mlp_gain_ref, *refs = refs
+    gain_ref, cos_ref, low_ref, high_ref, sel_ref, sel_all_ref, back_ref, pick_ref, number_ref = refs
+    gain_ref[0:1, :] = attn_gain_ref[...]
+    gain_ref[1:2, :] = mlp_gain_ref[...]
     group = keep_ref.shape[0]
     n_rows = sel_ref.shape[0]
     mine = lax.axis_index("pages")
@@ -242,11 +245,27 @@
         out_ref[i] = rows
 
 
+def load_kernel(weight_hbm, _, buf_ref, loaded_ref, sems):
+    rows, lanes = buf_ref.shape
+    count = sems.shape[0]
+    rows = rows // count
+
+    def copy(step):
+        some = pl.ds(step * rows, rows)
+        return pltpu.make_async_copy(weight_hbm.at[some, pl.ds(0, lanes)], buf_ref.at[some, :], sems.at[step])
+
+    for step in range(count):
+        copy(step).start()
+    loaded_ref[...] = jnp.zeros_like(loaded_ref)
+    for step in range(count):
+        copy(step).wait()
+
+
 def project_kernel(dims, *refs):
     group, n_blk, held_rows, heads, slots = dims
     pack_refs, refs = refs[:2], refs[2:]
-    gain_ref, mlp_gain_ref, weight_hbm, cos_ref, low_ref, high_ref, sel_ref, *refs = refs
-    send_ref, own_ref, leaf_ref, weight_buf, rows_ref, acc_ref, sems = refs
+    gain_ref, weight_ref, weight_hbm, cos_ref, low_ref, high_ref, sel_ref, *refs = refs
+    _, send_ref, own_ref, leaf_ref, weight_buf, rows_ref, acc_ref, sems = refs
     chunk = D // n_blk
     width = 3 * heads * HD
     head_lanes = heads * HD
@@ -258,11 +277,11 @@
     def weight_copy(part, step):
         return pltpu.make_async_copy(
             weight_hbm.at[pl.ds(step * chunk, chunk), pl.ds(part * period, period)],
-            weight_buf.at[part, step],
-            sems.at[part, step],
+            weight_buf.at[part - 1, step],
+            sems.at[part - 1, step],
         )
 
-    for part in range(width // period):
+    for part in range(1, width // period):
         for step in range(n_blk):
             weight_copy(part, step).start()
 
@@ -284,13 +303,11 @@
     for i, (b, piece) in enumerate(zip(places, pieces)):
         z = i % (n_blk // 2)
         some = slice(2 * z * chunk, 2 * (z + 1) * chunk)
-        gain, mlp_gain = (
-            jnp.where(b == 2 * z, ref[:, some][:, :chunk], ref[:, some][:, chunk:])
-            for ref in (gain_ref, mlp_gain_ref)
-        )
+        gain = gain_ref[:, some]
+        gain = jnp.where(b == 2 * z, gain[:, :chunk], gain[:, chunk:])
         piece = piece * spread
-        rows_ref[b, 0:group, :] = piece * gain
-        leaves.append(piece * mlp_gain)
+        rows_ref[b, 0:group, :] = piece * gain[0:1]
+        leaves.append(piece * gain[1:2])
     leaf_ref[...] = jnp.concatenate(leaves, axis=0).astype(BF16)
 
     rows = acc_ref.shape[0]
@@ -302,8 +319,12 @@
         acc_ref[...] = jnp.zeros_like(acc_ref)
 
         def one_chunk(step, carry, j=j):
-            weight_copy(j, step).wait()
-            acc_ref[...] += dot(rows_ref[step].astype(BF16), weight_buf[j, step])
+            if j == 0:
+                weight = weight_ref[pl.ds(pl.multiple_of(step * chunk, 16), chunk), :]
+            else:
+                weight_copy(j, step).wait()
+                weight = weight_buf[j - 1, step]
+            acc_ref[...] += dot(rows_ref[step].astype(BF16), weight)
             return carry
 
         lax.fori_loop(0, n_blk, one_chunk, 0)
@@ -537,22 +558,28 @@
             out_hbm.at[:, pl.ds(step * cols, cols)], out_buf.at[step], sems_out.at[step]
         )
 
-    for step in range(n_blk):
-        in_copy(step).start()
-    for step in range(n_steps):
-        out_copy(step).start()
+    copies = [in_copy(step) for step in range(n_blk)] + [out_copy(step) for step in range(n_steps)]
+    flight = 4
+    for copy in copies[:flight]:
+        copy.start()
+
+    def arrived(step):
+        copies[step].wait()
+        if step + flight < len(copies):
+            copies[step + flight].start()
+
     leaves = [ref[...].astype(F32) for ref in leaf_refs]
     half = n_blk // 2
     hidden = jnp.zeros((n_pages * group, in_buf.shape[2]), F32)
     for z in range(half):
-        in_copy(2 * z).wait()
-        in_copy(2 * z + 1).wait()
+        arrived(2 * z)
+        arrived(2 * z + 1)
         for i, c in ((z, 2 * z + core), (half + z, 2 * z + 1 - core)):
             rows = [leaf[i * group : (i + 1) * group] for leaf in leaves]
             hidden = hidden + dot(jnp.concatenate(rows, axis=0).astype(BF16), in_buf[c])
     active = (0.5 * hidden * (1.0 + lax.erf(hidden * math.sqrt(0.5)))).astype(BF16)
     for step in range(n_steps):
-        out_copy(step).wait()
+        arrived(n_blk + step)
         result = dot(active, out_buf[step]).astype(BF16)
         for g in range(n_pages):
             part_refs[g][:, step * cols : (step + 1) * cols] = result[g * group : (g + 1) * group]
@@ -635,18 +662,18 @@
         axis_index_groups=[list(range(core, n_blk, 2)) for core in range(2)],
         tiled=True,
     )
-    packs = [pack, swapped(pack, "blk", n_blk, 1)]
 
     n_rows = n_dev * slots
     rows = group * (1 + NREC)
     period = 12 * HD if (3 * head_lanes) % (12 * HD) == 0 else 3 * head_lanes
     lane = np.arange(HD)
     frequency = np.where(lane < ROT, ROT_BASE ** (-2.0 * (lane % (ROT // 2)) / ROT), 0.0).astype(np.float32)
-    cosine, low, high, sel, sel_all, back, pick, numbers = pl.pallas_call(
+    gains, cosine, low, high, sel, sel_all, back, pick, numbers = pl.pallas_call(
         functools.partial(prep_kernel, (n_pages, pages_dev, slots, period // (3 * HD))),
-        in_specs=[pl.BlockSpec(memory_space=pltpu.SMEM)] + [VMEM] * 6,
-        out_specs=[VMEM] * 8,
+        in_specs=[pl.BlockSpec(memory_space=pltpu.SMEM)] + [VMEM] * 8,
+        out_specs=[VMEM] * 9,
         out_shape=[
+            shape_of((2, D), F32),
             *[shape_of((rows, period), F32)] * 3,
             shape_of((n_rows, group)),
             shape_of((n_rows + group, group), F32),
@@ -665,6 +692,8 @@
         fixed(fold_index),
         fixed(recompute_list),
         fixed(jnp.asarray(frequency[None])),
+        fixed(attn_gain[None]),
+        fixed(mlp_gain[None]),
     )
 
     numbers = [numbers] + [swapped(numbers, "pages", n_pages, i) for i in range(1, n_pages)]
@@ -676,10 +705,24 @@
     dests = STEP_HEADS // heads
     fold_width = 2 * head_lanes
 
+    later = max(3 * head_lanes // period - 1, 1)
+    first_part, loaded = pl.pallas_call(
+        load_kernel,
+        in_specs=[HBM, ANY],
+        out_specs=[VMEM, VMEM],
+        out_shape=[pltpu.VMEM((D, period), BF16), shape_of((8, 128), F32)],
+        scratch_shapes=[pltpu.SemaphoreType.DMA((8,))],
+        compiler_params=params_of(4),
+        cost_estimate=cost_of(0, 0),
+        name="load_qkv",
+    )(fixed(qkv_weight), numbers[0])
+    pack, cosine, loaded = lax.optimization_barrier((pack, cosine, loaded))
+    packs = [pack, swapped(pack, "blk", n_blk, 1)]
+
     wire = lanes + wire_split(lanes)
     send, own, leaf = pl.pallas_call(
         functools.partial(project_kernel, (group, n_blk, held_rows, heads, slots)),
-        in_specs=[VMEM] * 4 + [HBM] + [VMEM] * 4,
+        in_specs=[VMEM] * 4 + [HBM] + [VMEM] * 4 + [ANY],
         out_specs=[VMEM] * 3,
         out_shape=[
             shape_of((n_dev, 2, wire)),
@@ -687,23 +730,24 @@
             shape_of((n_blk * group, chunk)),
         ],
         scratch_shapes=[
-            pltpu.VMEM((3 * head_lanes // period, n_blk, chunk, period), BF16),
+            pltpu.VMEM((later, n_blk, chunk, period), BF16),
             pltpu.VMEM((n_blk, rows, chunk), F32),
             pltpu.VMEM((rows, period), F32),
-            pltpu.SemaphoreType.DMA((3 * head_lanes // period, n_blk)),
+            pltpu.SemaphoreType.DMA((later, n_blk)),
         ],
-        compiler_params=params_of(50),
+        compiler_params=params_of(32),
         cost_estimate=cost_of(2 * rows * D * 3 * head_lanes, 6 * D * head_lanes),
         name="project",
     )(
         *packs,
-        fixed(attn_gain[None]),
-        fixed(mlp_gain[None]),
+        gains,
+        pltpu.with_memory_space_constraint(first_part, pltpu.VMEM),
         fixed(qkv_weight),
         cosine,
         low,
         high,
         sel,
+        loaded,
     )
     send, *numbers = lax.optimization_barrier((send, *numbers))
     asked = lax.all_to_all(send, ("pages", "blk"), 0, 0, tiled=True)

time: 101 us -> 102 us (level)
  blocking collectives: 18.9 us -> 0 us
  local copies, waits for them, and re-layouts: 0 us -> 10.1 us
  starting transfers between devices: 23.8 us -> 31.6 us
  Pallas kernels: 44.7 us -> 45.9 us
    all_to_all x1 -> x0, blocking collectives: 18.9 us -> none  [on_device(): lax.all_to_all(pack, 'blk', 0, 0, axis_index_groups=[list(range(core, n_b...]
    unnamed x0 -> x4, local copies, waits for them, and re-layouts: none -> 10.1 us
    all_to_all x0 -> x1, starting transfers between devices: none -> 6.32 us  [on_device(): lax.all_to_all(pack, 'blk', 0, 0, axis_index_groups=[list(range(core, n_b...]
    pallas_call x0 -> x1, Pallas kernels: none -> 5.18 us  [on_device(): pl.pallas_call(load_kernel, in_specs=[HBM, ANY], out_specs=[VMEM, VMEM],...]
    pallas_call x1, Pallas kernels: 12.3 us -> 9.68 us  [on_device(): pl.pallas_call(functools.partial(project_kernel, (group, n_blk, held_rows...]
    pallas_call x1, Pallas kernels: 9.79 us -> 7.7 us  [on_device(): pl.pallas_call(functools.partial(mlp_kernel, (group, n_pages, n_blk)), in...]
    all_to_all x1, starting transfers between devices: 3.71 us -> 5.62 us  [on_device(): asked = lax.all_to_all(send, ('pages', 'blk'), 0, 0, tiled=True)]
  transfers between devices with their start and end apart: 13 -> 14, of which waited for: 4 -> 6; matrix products, arithmetic and copies ran while one was open for 0% -> 0% of each run, Pallas kernels for 38% -> 38%
where the time goes in v3:
time: 102 us; the launch traced here: 101 us
  Pallas kernels  45.9 us (45%)
  starting transfers between devices  31.6 us (31%)
  waiting for transfers between devices  12.2 us (12%)
  local copies, waits for them, and re-layouts  10.1 us (10%)
    ppermute x10, starting transfers between devices, swapped(): return lax.ppermute(array, axis, [(i, i ^ by) for i in range(size)])  10.6 us
    unnamed x4, local copies, waits for them, and re-layouts  10.1 us
    pallas_call x1, Pallas kernels, on_device(): pl.pallas_call(functools.partial(project_kernel, (group, n_blk, held_rows...  9.68 us
    pallas_call x1, Pallas kernels, on_device(): pl.pallas_call(functools.partial(attend_kernel, (n_pages, slots, dests, h...  8.29 us
    pallas_call x1, Pallas kernels, on_device(): pl.pallas_call(functools.partial(mlp_kernel, (group, n_pages, n_blk)), in...  7.7 us
    all_to_all x1, starting transfers between devices, on_device(): lax.all_to_all(pack, 'blk', 0, 0, axis_index_groups=[list(range(core, n_b...  6.32 us
    ppermute x10, waiting for transfers between devices, swapped(): return lax.ppermute(array, axis, [(i, i ^ by) for i in range(size)])  5.96 us
    all_to_all x1, starting transfers between devices, on_device(): asked = lax.all_to_all(send, ('pages', 'blk'), 0, 0, tiled=True)  5.62 us
  transfers between devices with their start and end apart: 14, of which 6 were waited for; matrix products, arithmetic and copies ran while one was open for 0% of the time, Pallas kernels for 38%

profile of v3, /device:TPU:0, one launch (start us, length us, event | category | flops | bytes accessed | tf_op | source)
XLA Modules:
  0.0 101.2 jit_solution(9525579363128347209)
XLA Ops:
  0.6 2.0 %pack.1 = bf16[4,72,768]{2,1,0:T(8,128)(2,1)} custom-call(bf16[8,6144]{1,0:T(8,128)(2,1)} %bitcast.15, bf16[8,768]{1,0:T(8,128)(2,1)} %new_ref.1, f32[1,6144]{1,0:T(1,128)} %bitcast.13), custom_call_target="tpu_custom_call" | custom-call | tf_op jit(solution)/shard_map/pack/pallas_call | solution.py:649
  2.6 6.3 %all-to-all-start = ((bf16[4,72,768]{2,1,0:T(8,128)(2,1)}), bf16[4,72,768]{2,1,0:T(8,128)(2,1)S(1)}, u32[]{:S(2)}, u32[]{:S(2)}) async-start(bf16[4,72,768]{2,1,0:T(8,128)(2,1)} %pack.1), calls=%async_computation | async-start | bytes 884736 | tf_op jit(solution)/shard_map/all_to_all | solution.py:657
  8.9 2.0 %prep.1 = (f32[2,6144]{1,0:T(2,128)S(1)}, f32[72,1152]{1,0:T(8,128)S(1)}, f32[72,1152]{1,0:T(8,128)S(1)}, f32[72,1152]{1,0:T(8,128)S(1)}, bf16[128,8]{1,0:T(8,12...) custom-call(s32[12,32]{1,0:T(8,128)} %bitcast.16, ...), custom_call_target="tpu_custom_call" | custom-call | tf_op jit(solution)/shard_map/prep/pallas_call | solution.py:671
  11.0 5.2 %load_qkv.1 = (bf16[6144,1152]{1,0:T(8,128)(2,1)S(1)}, f32[8,128]{1,0:T(8,128)S(1)}) custom-call(bf16[6144,2304]{1,0:T(8,128)(2,1)} %refs_4_.3, s32[8,26]{1,0:T(8,128)S(1)} %get-tuple-element.51._.refs_0_), custom_call_target="tpu_custom_call" | custom-call | tf_op jit(solution)/shard_map/load_qkv/pallas_call | solution.py:709
  16.2 5.0 %copy-done = bf16[6144,1152]{1,0:T(8,128)(2,1)} copy-done((bf16[6144,1152]{1,0:T(8,128)(2,1)}, bf16[6144,1152]{1,0:T(8,128)(2,1)S(1)}, u32[]{:S(2)}) %copy-start) | copy-done | bytes 14155800
  21.2 0.5 all-to-all-done.refs_0_
  21.7 1.5 %collective-permute-start.1 = (s32[8,26]{1,0:T(8,128)S(1)}, s32[8,26]{1,0:T(8,128)S(1)}, u32[]{:S(2)}, u32[]{:S(2)}) collective-permute-start(s32[8,26]{1,0:T(8,128)S(1)} %get-tuple-element.51._.refs_0_), channel_id=1, source_target_pairs={{0,8},{8,0},{16,24},{24,16},{1,9},{9,1},{17,25},{25,17},{2,10},{10... | collective-permute-start | bytes 2504 | tf_op jit(solution)/shard_map/ppermute | solution.py:643
  23.2 1.5 %collective-permute-start.2 = (s32[8,26]{1,0:T(8,128)S(1)}, s32[8,26]{1,0:T(8,128)S(1)}, u32[]{:S(2)}, u32[]{:S(2)}) collective-permute-start(s32[8,26]{1,0:T(8,128)S(1)} %get-tuple-element.51._.refs_0_), channel_id=1, source_target_pairs={{0,16},{8,24},{16,0},{24,8},{1,17},{9,25},{17,1},{25,9},{2,18},{10... | collective-permute-start | bytes 2504 | tf_op jit(solution)/shard_map/ppermute | solution.py:643
  24.7 0.5 collective-permute-start.3
  25.2 5.0 %copy-done.1 = bf16[6144,1152]{1,0:T(8,128)(2,1)S(1)} copy-done((bf16[6144,1152]{1,0:T(8,128)(2,1)S(1)}, bf16[6144,1152]{1,0:T(8,128)(2,1)}, u32[]{:S(2)}) %copy-start.1) | copy-done | bytes 14155800
  30.2 9.7 %project.1 = (bf16[32,2,1408]{2,1,0:T(2,128)(2,1)}, bf16[8,896]{1,0:T(8,128)(2,1)S(1)}, bf16[64,768]{1,0:T(8,128)(2,1)S(1)}) custom-call(bf16[4,72,768]{2,1,0:T(8,128)(2,1)S(1)} %all-to-all-done.refs_0_, bf16[4,72,768]{2,1,0:T(8,128)(2,1)S(1)} %collective-permute-done.refs_1_, f32[2,6144]{1,0:T(2,128)S(1)} %get-tuple-element.42.refs_2_, ...), custom_call_target="tpu_custom_call" | custom-call | flops 2038431744 | bytes 28311552 | tf_op jit(solution)/shard_map/project/pallas_call | solution.py:723
  39.9 5.6 %all-to-all-start.1 = ((bf16[32,2,1408]{2,1,0:T(2,128)(2,1)}), bf16[32,2,1408]{2,1,0:T(2,128)(2,1)S(1)}, u32[]{:S(2)}, u32[]{:S(2)}) async-start(bf16[32,2,1408]{2,1,0:T(2,128)(2,1)} %get-tuple-element.50), calls=%async_computation.1 | async-start | bytes 360448 | tf_op jit(solution)/shard_map/all_to_all | solution.py:753
  45.5 1.4 %facts.1 = (f32[16,192]{1,0:T(8,128)S(1)}, f32[208,128]{1,0:T(8,128)S(1)}, bf16[208,128]{1,0:T(8,128)(2,1)S(1)}) custom-call(s32[8,26]{1,0:T(8,128)S(1)} %get-tuple-element.51._.refs_0_, s32[8,26]{1,0:T(8,128)S(1)} %collective-permute-done.1.refs_1_, s32[8,26]{1,0:T(8,128)S(1)} %collective-permute-done.2.refs_2_, ...), custom_call_target="tpu_custom_call" | custom-call | tf_op jit(solution)/shard_map/facts/pallas_call | solution.py:754
  46.9 1.8 %collective-permute-start.4 = (bf16[64,768]{1,0:T(8,128)(2,1)S(1)}, bf16[64,768]{1,0:T(8,128)(2,1)S(1)}, u32[]{:S(2)}, u32[]{:S(2)}) collective-permute-start(bf16[64,768]{1,0:T(8,128)(2,1)S(1)} %get-tuple-element.65.refs_0_), channel_id=1, source_target_pairs={{0,8},{8,0},{16,24},{24,16},{1,9},{9,1},{17,25},{25,17},{2,10},{10... | collective-permute-start | bytes 294920 | tf_op jit(solution)/shard_map/ppermute | solution.py:643
  48.8 1.5 %collective-permute-start.5 = (bf16[64,768]{1,0:T(8,128)(2,1)S(1)}, bf16[64,768]{1,0:T(8,128)(2,1)S(1)}, u32[]{:S(2)}, u32[]{:S(2)}) collective-permute-start(bf16[64,768]{1,0:T(8,128)(2,1)S(1)} %get-tuple-element.65.refs_0_), channel_id=1, source_target_pairs={{0,16},{8,24},{16,0},{24,8},{1,17},{9,25},{17,1},{25,9},{2,18},{10... | collective-permute-start | bytes 294920 | tf_op jit(solution)/shard_map/ppermute | solution.py:643
  50.2 0.3 collective-permute-start.6
  50.5 2.9 %fold.1.fold_ref = bf16[16,12288]{1,0:T(8,128)(2,1)S(1)} custom-call(f32[16,192]{1,0:T(8,128)S(1)} %get-tuple-element.59.weight_ref, bf16[192,12288]{1,0:T(8,128)(2,1)} %bitcast.10), custom_call_target="tpu_custom_call" | custom-call | tf_op jit(solution)/shard_map/fold/pallas_call | solution.py:771
  53.4 0.8 all-to-all-done.1
  54.1 8.3 %attend.1.refs_6_ = bf16[4,8,2,3712]{3,2,1,0:T(2,128)(2,1)} custom-call(bf16[4,8,2,1408]{3,2,1,0:T(2,128)(2,1)S(1)} %bitcast.9, f32[208,128]{1,0:T(8,128)S(1)} %get-tuple-element.55.valid_ref, bf16[208,128]{1,0:T(8,128)(2,1)S(1)} %get-tuple-element.56.place_ref, bf16[192,12288]{1,0:T(8,128)(2,1)} %bitcast.11, bf16[16,12288]{1,0:T(8,128)(2,1)S(1)} %fold.1.fold_ref), custom_call_target="tpu_custom_call" | custom-call | flops 603979776 | bytes 4718592 | tf_op jit(solution)/shard_map/attend/pallas_call | solution.py:787
  62.5 5.1 %all-to-all-start.2 = ((bf16[32,2,3712]{2,1,0:T(2,128)(2,1)}), bf16[32,2,3712]{2,1,0:T(2,128)(2,1)S(1)}, u32[]{:S(2)}, u32[]{:S(2)}) async-start(bf16[32,2,3712]{2,1,0:T(2,128)(2,1)} %bitcast.7), calls=%async_computation.2 | async-start | bytes 950272 | tf_op jit(solution)/shard_map/all_to_all | solution.py:804
  67.5 7.7 %mlp.1 = (bf16[8,6144]{1,0:T(8,128)(2,1)S(1)}, bf16[8,6144]{1,0:T(8,128)(2,1)S(1)}, bf16[8,6144]{1,0:T(8,128)(2,1)S(1)}, bf16[8,6144]{1,0:T(8,128)(2,1)S(1)}) custom-call(bf16[64,768]{1,0:T(8,128)(2,1)S(1)} %get-tuple-element.65.refs_0_, bf16[64,768]{1,0:T(8,128)(2,1)S(1)} %collective-permute-done.4.refs_1_, ...), custom_call_target="tpu_custom_call" | custom-call | flops 603979776 | bytes 18874368 | tf_op jit(solution)/shard_map/mlp/pallas_call | solution.py:807
  75.3 1.8 %collective-permute-start.7 = (bf16[8,6144]{1,0:T(8,128)(2,1)S(1)}, bf16[8,6144]{1,0:T(8,128)(2,1)S(1)}, u32[]{:S(2)}, u32[]{:S(2)}) collective-permute-start(bf16[8,6144]{1,0:T(8,128)(2,1)S(1)} %get-tuple-element.70), channel_id=1, source_target_pairs={{0,8},{8,0},{16,24},{24,16},{1,9},{9,1},{17,25},{25,17},{2,10},{10... | collective-permute-start | bytes 294920 | tf_op jit(solution)/shard_map/ppermute | solution.py:643
  77.1 1.5 %collective-permute-start.8 = (bf16[8,6144]{1,0:T(8,128)(2,1)S(1)}, bf16[8,6144]{1,0:T(8,128)(2,1)S(1)}, u32[]{:S(2)}, u32[]{:S(2)}) collective-permute-start(bf16[8,6144]{1,0:T(8,128)(2,1)S(1)} %get-tuple-element.71), channel_id=1, source_target_pairs={{0,16},{8,24},{16,0},{24,8},{1,17},{9,25},{17,1},{25,9},{2,18},{10... | collective-permute-start | bytes 294920 | tf_op jit(solution)/shard_map/ppermute | solution.py:643
  78.6 0.3 collective-permute-start.9
  78.8 2.4 %collective-permute-done.7.refs_1_ = bf16[8,6144]{1,0:T(8,128)(2,1)S(1)} collective-permute-done((bf16[8,6144]{1,0:T(8,128)(2,1)S(1)}, bf16[8,6144]{1,0:T(8,128)(2,1)S(1)}, u32[]{:S(2)}, u32[]{:S(2)}) %collective-permute-start.7) | collective-permute-done | bytes 98336 | tf_op jit(solution)/shard_map/ppermute | solution.py:643
  81.2 2.3 %collective-permute-done.8.refs_2_ = bf16[8,6144]{1,0:T(8,128)(2,1)S(1)} collective-permute-done((bf16[8,6144]{1,0:T(8,128)(2,1)S(1)}, bf16[8,6144]{1,0:T(8,128)(2,1)S(1)}, u32[]{:S(2)}, u32[]{:S(2)}) %collective-permute-start.8) | collective-permute-done | bytes 98336 | tf_op jit(solution)/shard_map/ppermute | solution.py:643
  83.4 1.3 %collective-permute-done.9.refs_3_ = bf16[8,6144]{1,0:T(8,128)(2,1)S(1)} collective-permute-done((bf16[8,6144]{1,0:T(8,128)(2,1)S(1)}, bf16[8,6144]{1,0:T(8,128)(2,1)S(1)}, u32[]{:S(2)}, u32[]{:S(2)}) %collective-permute-start.9) | collective-permute-done | bytes 98336 | tf_op jit(solution)/shard_map/ppermute | solution.py:643
  84.8 5.5 %merge.1 = bf16[8,8,768]{2,1,0:T(8,128)(2,1)} custom-call(bf16[32,2,3712]{2,1,0:T(2,128)(2,1)S(1)} %all-to-all-done.2.got_ref, bf16[8,896]{1,0:T(8,128)(2,1)S(1)} %get-tuple-element.62.own_ref, f32[136,8]{1,0:T(8,128)S(1)} %get-tuple-element.63.sel_ref, bf16[8,136]{1,0:T(8,128)(2,1)S(1)} %get-tuple-element.64.back_ref, ...), custom_call_target="tpu_custom_call" | custom-call | flops 75497472 | bytes 9437184 | tf_op jit(solution)/shard_map/merge/pallas_call | solution.py:824
  90.2 4.0 %all-to-all-start.3 = ((bf16[8,8,768]{2,1,0:T(8,128)(2,1)}), bf16[8,8,768]{2,1,0:T(8,128)(2,1)S(1)}, u32[]{:S(2)}, u32[]{:S(2)}) async-start(bf16[8,8,768]{2,1,0:T(8,128)(2,1)} %merge.1), calls=%async_computation.3 | async-start | bytes 196608 | tf_op jit(solution)/shard_map/all_to_all | solution.py:845
  94.2 1.3 %place.1 = bf16[12,8,1536]{2,1,0:T(8,128)(2,1)} custom-call(bf16[96,128]{1,0:T(8,128)(2,1)S(1)} %get-tuple-element.73.pick_ref, bf16[32,2,3712]{2,1,0:T(2,128)(2,1)S(1)} %all-to-all-done.2.got_ref), custom_call_target="tpu_custom_call" | custom-call | bytes 786432 | tf_op jit(solution)/shard_map/place/pallas_call | solution.py:848
  95.6 5.0 %all-to-all-done.3 = bf16[8,8,768]{2,1,0:T(8,128)(2,1)S(1)} async-done(((bf16[8,8,768]{2,1,0:T(8,128)(2,1)}), bf16[8,8,768]{2,1,0:T(8,128)(2,1)S(1)}, u32[]{:S(2)}, u32[]{:S(2)}) %all-to-all-start.3) | async-done | bytes 98336 | tf_op jit(solution)/shard_map/all_to_all | solution.py:845
  100.5 0.6 reduce_sum.12
  (11 shorter events, 0.0 us)
Async XLA Ops:
  2.6 19.1 %all-to-all-start = ((bf16[4,72,768]{2,1,0:T(8,128)(2,1)}), bf16[4,72,768]{2,1,0:T(8,128)(2,1)S(1)}, u32[]{:S(2)}, u32[]{:S(2)}) async-start(bf16[4,72,768]{2,1,0:T(8,128)(2,1)} %pack.1), calls=%async_computation | async-start | bytes 884736 | tf_op jit(solution)/shard_map/all_to_all | solution.py:657
  16.2 5.0 %copy-start = (bf16[6144,1152]{1,0:T(8,128)(2,1)}, bf16[6144,1152]{1,0:T(8,128)(2,1)S(1)}, u32[]{:S(2)}) copy-start(bf16[6144,1152]{1,0:T(8,128)(2,1)S(1)} %get-tuple-element.43.refs_3_) | copy-start | bytes 42467332
  21.7 3.5 %collective-permute-start = (bf16[4,72,768]{2,1,0:T(8,128)(2,1)S(1)}, bf16[4,72,768]{2,1,0:T(8,128)(2,1)S(1)}, u32[]{:S(2)}, u32[]{:S(2)}) collective-permute-start(bf16[4,72,768]{2,1,0:T(8,128)(2,1)S(1)} %all-to-all-done.refs_0_), channel_id=1, source_target_pairs={{0,1},{1,0},{2,3},{3,2},{4,5},{5,4},{6,7},{7,6},{8,9},{9,8},{10,11... | collective-permute-start | bytes 1327112 | tf_op jit(solution)/shard_map/ppermute | solution.py:643
  21.7 18.2 %collective-permute-start.1 = (s32[8,26]{1,0:T(8,128)S(1)}, s32[8,26]{1,0:T(8,128)S(1)}, u32[]{:S(2)}, u32[]{:S(2)}) collective-permute-start(s32[8,26]{1,0:T(8,128)S(1)} %get-tuple-element.51._.refs_0_), channel_id=1, source_target_pairs={{0,8},{8,0},{16,24},{24,16},{1,9},{9,1},{17,25},{25,17},{2,10},{10... | collective-permute-start | bytes 2504 | tf_op jit(solution)/shard_map/ppermute | solution.py:643
  23.2 16.7 %collective-permute-start.2 = (s32[8,26]{1,0:T(8,128)S(1)}, s32[8,26]{1,0:T(8,128)S(1)}, u32[]{:S(2)}, u32[]{:S(2)}) collective-permute-start(s32[8,26]{1,0:T(8,128)S(1)} %get-tuple-element.51._.refs_0_), channel_id=1, source_target_pairs={{0,16},{8,24},{16,0},{24,8},{1,17},{9,25},{17,1},{25,9},{2,18},{10... | collective-permute-start | bytes 2504 | tf_op jit(solution)/shard_map/ppermute | solution.py:643
  24.7 15.2 %collective-permute-start.3 = (s32[8,26]{1,0:T(8,128)S(1)}, s32[8,26]{1,0:T(8,128)S(1)}, u32[]{:S(2)}, u32[]{:S(2)}) collective-permute-start(s32[8,26]{1,0:T(8,128)S(1)} %get-tuple-element.51._.refs_0_), channel_id=1, source_target_pairs={{0,24},{8,16},{16,8},{24,0},{1,25},{9,17},{17,9},{25,1},{2,26},{10... | collective-permute-start | bytes 2504 | tf_op jit(solution)/shard_map/ppermute | solution.py:643
  25.2 5.0 %copy-start.1 = (bf16[6144,1152]{1,0:T(8,128)(2,1)S(1)}, bf16[6144,1152]{1,0:T(8,128)(2,1)}, u32[]{:S(2)}) copy-start(bf16[6144,1152]{1,0:T(8,128)(2,1)} %copy-done) | copy-start | bytes 42467332
  39.9 14.2 %all-to-all-start.1 = ((bf16[32,2,1408]{2,1,0:T(2,128)(2,1)}), bf16[32,2,1408]{2,1,0:T(2,128)(2,1)S(1)}, u32[]{:S(2)}, u32[]{:S(2)}) async-start(bf16[32,2,1408]{2,1,0:T(2,128)(2,1)} %get-tuple-element.50), calls=%async_computation.1 | async-start | bytes 360448 | tf_op jit(solution)/shard_map/all_to_all | solution.py:753
  46.9 15.5 %collective-permute-start.4 = (bf16[64,768]{1,0:T(8,128)(2,1)S(1)}, bf16[64,768]{1,0:T(8,128)(2,1)S(1)}, u32[]{:S(2)}, u32[]{:S(2)}) collective-permute-start(bf16[64,768]{1,0:T(8,128)(2,1)S(1)} %get-tuple-element.65.refs_0_), channel_id=1, source_target_pairs={{0,8},{8,0},{16,24},{24,16},{1,9},{9,1},{17,25},{25,17},{2,10},{10... | collective-permute-start | bytes 294920 | tf_op jit(solution)/shard_map/ppermute | solution.py:643
  48.8 13.7 %collective-permute-start.5 = (bf16[64,768]{1,0:T(8,128)(2,1)S(1)}, bf16[64,768]{1,0:T(8,128)(2,1)S(1)}, u32[]{:S(2)}, u32[]{:S(2)}) collective-permute-start(bf16[64,768]{1,0:T(8,128)(2,1)S(1)} %get-tuple-element.65.refs_0_), channel_id=1, source_target_pairs={{0,16},{8,24},{16,0},{24,8},{1,17},{9,25},{17,1},{25,9},{2,18},{10... | collective-permute-start | bytes 294920 | tf_op jit(solution)/shard_map/ppermute | solution.py:643
  50.2 12.2 %collective-permute-start.6 = (bf16[64,768]{1,0:T(8,128)(2,1)S(1)}, bf16[64,768]{1,0:T(8,128)(2,1)S(1)}, u32[]{:S(2)}, u32[]{:S(2)}) collective-permute-start(bf16[64,768]{1,0:T(8,128)(2,1)S(1)} %get-tuple-element.65.refs_0_), channel_id=1, source_target_pairs={{0,24},{8,16},{16,8},{24,0},{1,25},{9,17},{17,9},{25,1},{2,26},{10... | collective-permute-start | bytes 294920 | tf_op jit(solution)/shard_map/ppermute | solution.py:643
  62.5 22.3 %all-to-all-start.2 = ((bf16[32,2,3712]{2,1,0:T(2,128)(2,1)}), bf16[32,2,3712]{2,1,0:T(2,128)(2,1)S(1)}, u32[]{:S(2)}, u32[]{:S(2)}) async-start(bf16[32,2,3712]{2,1,0:T(2,128)(2,1)} %bitcast.7), calls=%async_computation.2 | async-start | bytes 950272 | tf_op jit(solution)/shard_map/all_to_all | solution.py:804
  75.3 5.9 %collective-permute-start.7 = (bf16[8,6144]{1,0:T(8,128)(2,1)S(1)}, bf16[8,6144]{1,0:T(8,128)(2,1)S(1)}, u32[]{:S(2)}, u32[]{:S(2)}) collective-permute-start(bf16[8,6144]{1,0:T(8,128)(2,1)S(1)} %get-tuple-element.70), channel_id=1, source_target_pairs={{0,8},{8,0},{16,24},{24,16},{1,9},{9,1},{17,25},{25,17},{2,10},{10... | collective-permute-start | bytes 294920 | tf_op jit(solution)/shard_map/ppermute | solution.py:643
  77.1 6.3 %collective-permute-start.8 = (bf16[8,6144]{1,0:T(8,128)(2,1)S(1)}, bf16[8,6144]{1,0:T(8,128)(2,1)S(1)}, u32[]{:S(2)}, u32[]{:S(2)}) collective-permute-start(bf16[8,6144]{1,0:T(8,128)(2,1)S(1)} %get-tuple-element.71), channel_id=1, source_target_pairs={{0,16},{8,24},{16,0},{24,8},{1,17},{9,25},{17,1},{25,9},{2,18},{10... | collective-permute-start | bytes 294920 | tf_op jit(solution)/shard_map/ppermute | solution.py:643
  78.6 6.2 %collective-permute-start.9 = (bf16[8,6144]{1,0:T(8,128)(2,1)S(1)}, bf16[8,6144]{1,0:T(8,128)(2,1)S(1)}, u32[]{:S(2)}, u32[]{:S(2)}) collective-permute-start(bf16[8,6144]{1,0:T(8,128)(2,1)S(1)} %get-tuple-element.72), channel_id=1, source_target_pairs={{0,24},{8,16},{16,8},{24,0},{1,25},{9,17},{17,9},{25,1},{2,26},{10... | collective-permute-start | bytes 294920 | tf_op jit(solution)/shard_map/ppermute | solution.py:643
  90.2 10.3 %all-to-all-start.3 = ((bf16[8,8,768]{2,1,0:T(8,128)(2,1)}), bf16[8,8,768]{2,1,0:T(8,128)(2,1)S(1)}, u32[]{:S(2)}, u32[]{:S(2)}) async-start(bf16[8,8,768]{2,1,0:T(8,128)(2,1)} %merge.1), calls=%async_computation.3 | async-start | bytes 196608 | tf_op jit(solution)/shard_map/all_to_all | solution.py:845

commit v4 on v3

--- a/solution.py
+++ b/solution.py
@@ -69,32 +69,31 @@
     return (width // 128 + 1) // 2 * 128 if width % 128 == 0 else (width + 1) // 2
 
 
-def to_wire(ref, index, rows):
-    width = rows.shape[1]
+def wire_tail(thirds, width):
     first = wire_split(width)
-    ref[(*index, slice(None), slice(0, width))] = rows[:2].astype(BF16)
-    rest = rows[2:3, first:]
+    count = thirds.shape[0]
+    at, of = iota((2 * count, count), 0), iota((2 * count, count), 1)
+    upper = jnp.where(at == 2 * of, 1.0, 0.0).astype(BF16)
+    lower = jnp.where(at == 2 * of + 1, 1.0, 0.0).astype(BF16)
+    rest = thirds[:, first:]
     if width < 2 * first:
-        rest = jnp.concatenate([rest, jnp.zeros((1, 2 * first - width), F32)], axis=1)
-    tail = jnp.concatenate([rows[2:3, :first], rest], axis=0)
-    ref[(*index, slice(None), slice(width, width + first))] = tail.astype(BF16)
-
-
-def from_wire(ref, index, width, start, stop):
+        rest = jnp.concatenate([rest, jnp.zeros((count, 2 * first - width), BF16)], axis=1)
+    return (dot(upper, thirds[:, :first]) + dot(lower, rest)).astype(BF16)
+
+
+def third_row(ref, index, width, start, stop):
     first = wire_split(width)
-    pair = ref[(*index, slice(None), slice(start, stop))].astype(F32)
     third = []
     if start < first:
         third.append(ref[(*index, slice(0, 1), slice(width + start, width + min(stop, first)))].astype(F32))
     if stop > first:
         begin = max(start, first) - first
         third.append(ref[(*index, slice(1, 2), slice(width + begin, width + stop - first))].astype(F32))
-    third = third[0] if len(third) == 1 else jnp.concatenate(third, axis=1)
-    return jnp.concatenate([pair, third, jnp.zeros_like(third)], axis=0)
+    return third[0] if len(third) == 1 else jnp.concatenate(third, axis=1)
 
 
 def prep_kernel(dims, table_smem, table_ref, length_ref, keep_ref, choice_ref, list_ref, frequency_ref, *refs):
-    n_pages, pages_dev, slots, period_heads = dims
+    n_pages, pages_dev, period_heads = dims
     attn_gain_ref, mlp_gain_ref, *refs = refs
     gain_ref, cos_ref, low_ref, high_ref, sel_ref, sel_all_ref, back_ref, pick_ref, number_ref = refs
     gain_ref[0:1, :] = attn_gain_ref[...]
@@ -115,7 +114,8 @@
             rank = rank + jnp.where(earlier, 1, 0)
         return rank
 
-    row = holder * slots + lax.fori_loop(0, group, one_request, jnp.zeros_like(ids))
+    rank = lax.fori_loop(0, group, one_request, jnp.zeros_like(ids))
+    row = jnp.where(rank < 2, 2 * holder + rank, n_rows // 3 * 2 + holder)
     at = iota((n_rows, group), 0)
     hit = None
     for j in range(PPR):
@@ -199,7 +199,9 @@
     )
     below = jnp.where(iota((ranks, ranks), 0) > iota((ranks, ranks), 1), 1.0, 0.0).astype(BF16)
     before = dot(below, owner.astype(BF16))
-    rank = jnp.sum(owner * (before + slots * iota((ranks, n_pages), 1).astype(F32)), axis=1, keepdims=True)
+    group_of = iota((ranks, n_pages), 1).astype(F32)
+    rank = jnp.where(before < 1.5, 2 * group_of + before, 2 * n_pages + group_of)
+    rank = jnp.sum(owner * rank, axis=1, keepdims=True)
     rank = jnp.where(found, rank, -1.0)
     rank_hit = jnp.where(rank == iota((ranks, ranks), 1).astype(F32), 1.0, 0.0).astype(BF16)
 
@@ -245,27 +247,11 @@
         out_ref[i] = rows
 
 
-def load_kernel(weight_hbm, _, buf_ref, loaded_ref, sems):
-    rows, lanes = buf_ref.shape
-    count = sems.shape[0]
-    rows = rows // count
-
-    def copy(step):
-        some = pl.ds(step * rows, rows)
-        return pltpu.make_async_copy(weight_hbm.at[some, pl.ds(0, lanes)], buf_ref.at[some, :], sems.at[step])
-
-    for step in range(count):
-        copy(step).start()
-    loaded_ref[...] = jnp.zeros_like(loaded_ref)
-    for step in range(count):
-        copy(step).wait()
-
-
 def project_kernel(dims, *refs):
-    group, n_blk, held_rows, heads, slots = dims
+    group, n_blk, held_rows, heads = dims
     pack_refs, refs = refs[:2], refs[2:]
-    gain_ref, weight_ref, weight_hbm, cos_ref, low_ref, high_ref, sel_ref, *refs = refs
-    _, send_ref, own_ref, leaf_ref, weight_buf, rows_ref, acc_ref, sems = refs
+    gain_ref, weight_hbm, cos_ref, low_ref, high_ref, sel_ref, *refs = refs
+    send_ref, own_ref, leaf_ref, weight_buf, rows_ref, acc_ref, sems = refs
     chunk = D // n_blk
     width = 3 * heads * HD
     head_lanes = heads * HD
@@ -277,13 +263,13 @@
     def weight_copy(part, step):
         return pltpu.make_async_copy(
             weight_hbm.at[pl.ds(step * chunk, chunk), pl.ds(part * period, period)],
-            weight_buf.at[part - 1, step],
-            sems.at[part - 1, step],
+            weight_buf.at[part, step],
+            sems.at[part, step],
         )
 
-    for part in range(1, width // period):
-        for step in range(n_blk):
-            weight_copy(part, step).start()
+    flight = 6
+    for step in range(flight):
+        weight_copy(0, step).start()
 
     pieces, places = [], []
     for other in range(2):
@@ -319,12 +305,18 @@
         acc_ref[...] = jnp.zeros_like(acc_ref)
 
         def one_chunk(step, carry, j=j):
-            if j == 0:
-                weight = weight_ref[pl.ds(pl.multiple_of(step * chunk, 16), chunk), :]
-            else:
-                weight_copy(j, step).wait()
-                weight = weight_buf[j - 1, step]
-            acc_ref[...] += dot(rows_ref[step].astype(BF16), weight)
+            @pl.when(step + flight < n_blk)
+            def _():
+                weight_copy(j, step + flight).start()
+
+            if j + 1 < width // period:
+
+                @pl.when(step + flight >= n_blk)
+                def _():
+                    weight_copy(j + 1, step + flight - n_blk).start()
+
+            weight_copy(j, step).wait()
+            acc_ref[...] += dot(rows_ref[step].astype(BF16), weight_buf[j, step])
             return carry
 
         lax.fori_loop(0, n_blk, one_chunk, 0)
@@ -361,9 +353,13 @@
     sel_rows = dot(sel, spread_rows).astype(BF16)
     both = jnp.concatenate(parts_of(held_score, 2), axis=1)
     given = dot(sel_rows, both)
-    both = jnp.concatenate([asked, given], axis=1)
-    for d in range(send_ref.shape[0]):
-        to_wire(send_ref, (d,), both[d * slots : (d + 1) * slots])
+    both = jnp.concatenate([asked, given], axis=1).astype(BF16)
+    lanes = both.shape[1]
+    n_dev = send_ref.shape[0]
+    tails = wire_tail(both[2 * n_dev :], lanes)
+    for d in range(n_dev):
+        send_ref[d, :, :lanes] = both[2 * d : 2 * d + 2]
+        send_ref[d, :, lanes:] = tails[2 * d : 2 * d + 2]
 
     own_score = score[:group]
     lane = iota((group, extra), 1)
@@ -384,9 +380,11 @@
 
 
 def place_kernel(dims, pick_ref, got_ref, out_ref, rows_ref):
-    slots, width, first_lane = dims
-    for d in range(got_ref.shape[0]):
-        rows_ref[d * slots : (d + 1) * slots, :] = from_wire(got_ref, (d,), width, first_lane, width)
+    width, first_lane = dims
+    n_dev = got_ref.shape[0]
+    for d in range(n_dev):
+        rows_ref[2 * d : 2 * d + 2, :] = got_ref[d, :, first_lane:width].astype(F32)
+        rows_ref[2 * n_dev + d : 2 * n_dev + d + 1, :] = third_row(got_ref, (d,), width, first_lane, width)
     found = dot(pick_ref[...], rows_ref[...].astype(BF16)).astype(BF16)
     group = out_ref.shape[1]
     for j in range(out_ref.shape[0]):
@@ -400,13 +398,12 @@
     head_lanes = heads * HD
     extra = 2 * heads * NREC
     tokens = page_ref.shape[0]
-    asks = [
-        jnp.concatenate(
-            [from_wire(ask_ref, (g, b), head_lanes + extra, 0, head_lanes + extra) for g in range(n_pages)],
-            axis=0,
-        )
-        for b in range(dests)
-    ]
+    width = head_lanes + extra
+    asks = []
+    for b in range(dests):
+        pairs = [ask_ref[g, b, :, :width].astype(F32) for g in range(n_pages)]
+        thirds = [third_row(ask_ref, (g, b), width, 0, width) for g in range(n_pages)]
+        asks.append(jnp.concatenate([*pairs, *thirds, jnp.zeros((rows - 3 * n_pages, width), F32)], axis=0))
     query = jnp.concatenate([a[:, :head_lanes] for a in asks], axis=1)
     given = jnp.concatenate([a[:, head_lanes : head_lanes + extra] for a in asks], axis=1)
     valid = valid_ref[...] > 0.5
@@ -427,8 +424,9 @@
         hit = (lane_in >= i * heads) & (lane_in < (i + 1) * heads)
         hit = hit & (row_head == lane_dest + lane_in - i * heads)
         goals.append(jnp.where(hit, 1.0, 0.0).astype(BF16))
-    gathered, extras = [], []
-    for o in range(STEP_HEADS // OCTET):
+    octets = range(STEP_HEADS // OCTET)
+    all_scores = []
+    for o in octets:
         heads_here = range(o * OCTET, (o + 1) * OCTET)
         asked = jnp.concatenate([query[:, h * HD : (h + 1) * HD] for h in heads_here], axis=0)
         asked = jnp.concatenate([asked, jnp.zeros((lanes, 128 - HD), F32)], axis=1).T[:HD]
@@ -440,48 +438,54 @@
         told = jnp.where(given_head == row_head, told, 0.0).T.astype(BF16)
         some = slice(o * OCTET * 2 * HD, (o + 1) * OCTET * 2 * HD)
         page = jnp.concatenate([page_ref[:, some], fold_ref[:, some]], axis=0)
-        scores = jnp.where(touched, dot(place, told), dot(page, stacked) * SCALE)
+        all_scores.append(jnp.where(touched, dot(place, told), dot(page, stacked) * SCALE))
+    all_weights, extras = [], []
+    for scores in all_scores:
         scores = jnp.where(valid, scores, NEVER)
         top = jnp.max(scores, axis=0, keepdims=True)
         weights = jnp.where(valid, jnp.exp(scores - top), 0.0)
         total = jnp.sum(weights, axis=0, keepdims=True)
         safe = jnp.where(total > 0.0, total, 1.0)
         rest = jnp.zeros((256 - weights.shape[0], lanes), F32)
-        weights = jnp.concatenate([weights * (1.0 / safe), rest], axis=0).T.astype(BF16)
-        page = jnp.concatenate([page, jnp.zeros((rest.shape[0], page.shape[1]), BF16)], axis=0)
-        for i in range(OCTET // QUAD):
-            mixed = dot(
-                weights[i * QUAD * rows : (i + 1) * QUAD * rows],
-                page[:, i * QUAD * 2 * HD : (i + 1) * QUAD * 2 * HD],
-            )
-            for h in range(QUAD):
-                gathered.append(mixed[h * rows : (h + 1) * rows, 2 * HD * h + HD : 2 * HD * (h + 1)])
+        all_weights.append(jnp.concatenate([weights * (1.0 / safe), rest], axis=0).T.astype(BF16))
         lse = jnp.where(own_lane, jnp.where(total > 0.0, top + jnp.log(safe), NEVER), 0.0)
         spread = jnp.zeros((rows, lanes), F32)
         for part, goal in zip(parts_of(lse, 3), goals):
             spread = spread + dot(part, goal)
         extras.append(spread)
+    gathered = []
+    for o in octets:
+        for i in range(OCTET // QUAD):
+            first = (o * OCTET + i * QUAD) * 2 * HD
+            some = slice(first, first + QUAD * 2 * HD)
+            page = [page_ref[:, some], fold_ref[:, some]]
+            page.append(jnp.zeros((256 - tokens - rows, QUAD * 2 * HD), BF16))
+            mixed = dot(all_weights[o][i * QUAD * rows : (i + 1) * QUAD * rows], jnp.concatenate(page, axis=0))
+            for h in range(QUAD):
+                gathered.append(mixed[h * rows : (h + 1) * rows, 2 * HD * h + HD : 2 * HD * (h + 1)])
     gathered = jnp.concatenate(gathered, axis=1)
     extras = jnp.concatenate(extras, axis=1)
-    width = 2 * head_lanes
-    folded = fold_ref[...].astype(F32)
+    fold_lanes = 2 * head_lanes
+    all_lanes = width + fold_lanes
     for b in range(dests):
         whole = jnp.concatenate(
             [
-                gathered[:, b * head_lanes : (b + 1) * head_lanes],
-                extras[:, b * extra : (b + 1) * extra],
-                folded[:, b * width : (b + 1) * width],
+                gathered[:, b * head_lanes : (b + 1) * head_lanes].astype(BF16),
+                extras[:, b * extra : (b + 1) * extra].astype(BF16),
+                fold_ref[:, b * fold_lanes : (b + 1) * fold_lanes],
             ],
             axis=1,
         )
+        tails = wire_tail(whole[2 * n_pages : 3 * n_pages], all_lanes)
         for g in range(n_pages):
-            to_wire(send_ref, (g, b), whole[g * slots : (g + 1) * slots])
+            send_ref[g, b, :, :all_lanes] = whole[2 * g : 2 * g + 2]
+            send_ref[g, b, :, all_lanes:] = tails[2 * g : 2 * g + 2]
 
 
 def merge_kernel(
     dims, got_ref, own_ref, sel_ref, back_ref, *refs
 ):
-    group, n_dev, slots, heads, n_pages = dims
+    group, n_dev, heads, n_pages = dims
     share_refs, dense_hbm, refs = refs[:n_pages], refs[n_pages], refs[n_pages + 1 :]
     head_lanes = heads * HD
     extra = 2 * heads * NREC
@@ -498,10 +502,11 @@
     for step in range(steps):
         dense_copy(step).start()
     for d in range(n_dev):
-        rows_ref[d * slots : (d + 1) * slots, :] = from_wire(
+        rows_ref[2 * d : 2 * d + 2, :] = got_ref[d, :, : head_lanes + extra].astype(F32)
+        rows_ref[2 * n_dev + d : 2 * n_dev + d + 1, :] = third_row(
             got_ref, (d,), 3 * head_lanes + extra, 0, head_lanes + extra
         )
-    rows_ref[n_dev * slots :, :] = own_ref[...].astype(F32)
+    rows_ref[3 * n_dev :, :] = own_ref[...].astype(F32)
     count = rows_ref.shape[0]
     parts = rows_ref[:, head_lanes : head_lanes + extra].astype(BF16)
     to, source = iota((extra, 128), 1), iota((extra, 128), 0)
@@ -663,13 +668,13 @@
         tiled=True,
     )
 
-    n_rows = n_dev * slots
+    n_rows = n_dev * 3
     rows = group * (1 + NREC)
     period = 12 * HD if (3 * head_lanes) % (12 * HD) == 0 else 3 * head_lanes
     lane = np.arange(HD)
     frequency = np.where(lane < ROT, ROT_BASE ** (-2.0 * (lane % (ROT // 2)) / ROT), 0.0).astype(np.float32)
     gains, cosine, low, high, sel, sel_all, back, pick, numbers = pl.pallas_call(
-        functools.partial(prep_kernel, (n_pages, pages_dev, slots, period // (3 * HD))),
+        functools.partial(prep_kernel, (n_pages, pages_dev, period // (3 * HD))),
         in_specs=[pl.BlockSpec(memory_space=pltpu.SMEM)] + [VMEM] * 8,
         out_specs=[VMEM] * 9,
         out_shape=[
@@ -705,24 +710,13 @@
     dests = STEP_HEADS // heads
     fold_width = 2 * head_lanes
 
-    later = max(3 * head_lanes // period - 1, 1)
-    first_part, loaded = pl.pallas_call(
-        load_kernel,
-        in_specs=[HBM, ANY],
-        out_specs=[VMEM, VMEM],
-        out_shape=[pltpu.VMEM((D, period), BF16), shape_of((8, 128), F32)],
-        scratch_shapes=[pltpu.SemaphoreType.DMA((8,))],
-        compiler_params=params_of(4),
-        cost_estimate=cost_of(0, 0),
-        name="load_qkv",
-    )(fixed(qkv_weight), numbers[0])
-    pack, cosine, loaded = lax.optimization_barrier((pack, cosine, loaded))
+    pack, cosine = lax.optimization_barrier((pack, cosine))
     packs = [pack, swapped(pack, "blk", n_blk, 1)]
 
     wire = lanes + wire_split(lanes)
     send, own, leaf = pl.pallas_call(
-        functools.partial(project_kernel, (group, n_blk, held_rows, heads, slots)),
-        in_specs=[VMEM] * 4 + [HBM] + [VMEM] * 4 + [ANY],
+        functools.partial(project_kernel, (group, n_blk, held_rows, heads)),
+        in_specs=[VMEM] * 3 + [HBM] + [VMEM] * 4,
         out_specs=[VMEM] * 3,
         out_shape=[
             shape_of((n_dev, 2, wire)),
@@ -730,24 +724,22 @@
             shape_of((n_blk * group, chunk)),
         ],
         scratch_shapes=[
-            pltpu.VMEM((later, n_blk, chunk, period), BF16),
+            pltpu.VMEM((3 * head_lanes // period, n_blk, chunk, period), BF16),
             pltpu.VMEM((n_blk, rows, chunk), F32),
             pltpu.VMEM((rows, period), F32),
-            pltpu.SemaphoreType.DMA((later, n_blk)),
+            pltpu.SemaphoreType.DMA((3 * head_lanes // period, n_blk)),
         ],
-        compiler_params=params_of(32),
+        compiler_params=params_of(50),
         cost_estimate=cost_of(2 * rows * D * 3 * head_lanes, 6 * D * head_lanes),
         name="project",
     )(
         *packs,
         gains,
-        pltpu.with_memory_space_constraint(first_part, pltpu.VMEM),
         fixed(qkv_weight),
         cosine,
         low,
         high,
         sel,
-        loaded,
     )
     send, *numbers = lax.optimization_barrier((send, *numbers))
     asked = lax.all_to_all(send, ("pages", "blk"), 0, 0, tiled=True)
@@ -822,7 +814,7 @@
     mlp_share = [mlp_parts[0]] + [swapped(mlp_parts[i], "pages", n_pages, i) for i in range(1, n_pages)]
 
     out_part = pl.pallas_call(
-        functools.partial(merge_kernel, (group, n_dev, slots, heads, n_pages)),
+        functools.partial(merge_kernel, (group, n_dev, heads, n_pages)),
         in_specs=[VMEM] * (n_pages + 4) + [HBM],
         out_specs=VMEM,
         out_shape=shape_of((n_blk, group, chunk)),
@@ -846,7 +838,7 @@
     summed = jnp.sum(out_got.astype(F32), axis=0).astype(BF16)
 
     folded = pl.pallas_call(
-        functools.partial(place_kernel, (slots, all_lanes, lanes)),
+        functools.partial(place_kernel, (all_lanes, lanes)),
         in_specs=[VMEM, VMEM],
         out_specs=VMEM,
         out_shape=shape_of((PPR, group, fold_width)),

time: 102 us -> 94.7 us (0.928)
  waiting for transfers between devices: 12.2 us -> 22.6 us
  local copies, waits for them, and re-layouts: 10.1 us -> 0 us
  Pallas kernels: 45.9 us -> 40.6 us
  starting transfers between devices: 31.6 us -> 29.7 us
    all_to_all x1, waiting for transfers between devices: 0.45 us -> 10.7 us  [on_device(): lax.all_to_all(pack, 'blk', 0, 0, axis_index_groups=[list(range(core, n_b...]
    unnamed x4 -> x0, local copies, waits for them, and re-layouts: 10.1 us -> none
    pallas_call x4 -> x3, Pallas kernels: 14 us -> 8.5 us  [the longest x1 5.3 us: on_device(): pl.pallas_call(functools.partial(merge_kernel, (group, n_dev, heads, n_pa...]
    pallas_call x1, Pallas kernels: 9.68 us -> 11.8 us  [on_device(): pl.pallas_call(functools.partial(project_kernel, (group, n_blk, held_rows...]
    pallas_call x1, Pallas kernels: 8.29 us -> 6.33 us  [on_device(): pl.pallas_call(functools.partial(attend_kernel, (n_pages, slots, dests, h...]
    all_to_all x1, starting transfers between devices: 5.62 us -> 3.71 us  [on_device(): asked = lax.all_to_all(send, ('pages', 'blk'), 0, 0, tiled=True)]
  transfers between devices with their start and end apart: 14 -> 14, of which waited for: 6 -> 6; matrix products, arithmetic and copies ran while one was open for 0% -> 0% of each run, Pallas kernels for 38% -> 35%
where the time goes in v4:
time: 94.7 us; the launch traced here: 94.2 us
  Pallas kernels  40.6 us (43%)
  starting transfers between devices  29.7 us (31%)
  waiting for transfers between devices  22.6 us (24%)
    pallas_call x1, Pallas kernels, on_device(): pl.pallas_call(functools.partial(project_kernel, (group, n_blk, held_rows...  11.8 us
    all_to_all x1, waiting for transfers between devices, on_device(): lax.all_to_all(pack, 'blk', 0, 0, axis_index_groups=[list(range(core, n_b...  10.7 us
    ppermute x10, starting transfers between devices, swapped(): return lax.ppermute(array, axis, [(i, i ^ by) for i in range(size)])  10.6 us
    pallas_call x1, Pallas kernels, on_device(): pl.pallas_call(functools.partial(mlp_kernel, (group, n_pages, n_blk)), in...  7.71 us
    pallas_call x1, Pallas kernels, on_device(): pl.pallas_call(functools.partial(attend_kernel, (n_pages, slots, dests, h...  6.33 us
    all_to_all x1, starting transfers between devices, on_device(): lax.all_to_all(pack, 'blk', 0, 0, axis_index_groups=[list(range(core, n_b...  6.32 us
    ppermute x10, waiting for transfers between devices, swapped(): return lax.ppermute(array, axis, [(i, i ^ by) for i in range(size)])  5.96 us
    pallas_call x1, Pallas kernels, on_device(): pl.pallas_call(functools.partial(merge_kernel, (group, n_dev, heads, n_pa...  5.3 us
  transfers between devices with their start and end apart: 14, of which 6 were waited for; matrix products, arithmetic and copies ran while one was open for 0% of the time, Pallas kernels for 35%

profile of v4, /device:TPU:0, one launch (start us, length us, event | category | flops | bytes accessed | tf_op | source)
XLA Modules:
  0.0 94.2 jit_solution(11696219513184382667)
XLA Ops:
  0.6 2.0 %pack.1 = bf16[4,72,768]{2,1,0:T(8,128)(2,1)} custom-call(bf16[8,6144]{1,0:T(8,128)(2,1)} %bitcast.15, bf16[8,768]{1,0:T(8,128)(2,1)} %new_ref.1, f32[1,6144]{1,0:T(1,128)} %bitcast.13), custom_call_target="tpu_custom_call" | custom-call | tf_op jit(solution)/shard_map/pack/pallas_call | solution.py:654
  2.6 6.3 %all-to-all-start = ((bf16[4,72,768]{2,1,0:T(8,128)(2,1)}), bf16[4,72,768]{2,1,0:T(8,128)(2,1)S(1)}, u32[]{:S(2)}, u32[]{:S(2)}) async-start(bf16[4,72,768]{2,1,0:T(8,128)(2,1)} %pack.1), calls=%async_computation | async-start | bytes 884736 | tf_op jit(solution)/shard_map/all_to_all | solution.py:662
  8.9 2.0 %prep.1 = (f32[2,6144]{1,0:T(2,128)S(1)}, f32[72,1152]{1,0:T(8,128)S(1)}, f32[72,1152]{1,0:T(8,128)S(1)}, f32[72,1152]{1,0:T(8,128)S(1)}, bf16[96,8]{1,0:T(8,128...) custom-call(s32[12,32]{1,0:T(8,128)} %bitcast.16, ...), custom_call_target="tpu_custom_call" | custom-call | tf_op jit(solution)/shard_map/prep/pallas_call | solution.py:676
  10.9 10.7 %all-to-all-done.refs_0_ = bf16[4,72,768]{2,1,0:T(8,128)(2,1)S(1)} async-done(((bf16[4,72,768]{2,1,0:T(8,128)(2,1)}), bf16[4,72,768]{2,1,0:T(8,128)(2,1)S(1)}, u32[]{:S(2)}, u32[]{:S(2)}) %all-to-all-start) | async-done | bytes 442400 | tf_op jit(solution)/shard_map/all_to_all | solution.py:662
  21.7 1.5 %collective-permute-start.1 = (s32[8,26]{1,0:T(8,128)S(1)}, s32[8,26]{1,0:T(8,128)S(1)}, u32[]{:S(2)}, u32[]{:S(2)}) collective-permute-start(s32[8,26]{1,0:T(8,128)S(1)} %get-tuple-element.45.refs_0_), channel_id=1, source_target_pairs={{0,8},{8,0},{16,24},{24,16},{1,9},{9,1},{17,25},{25,17},{2,10},{10... | collective-permute-start | bytes 2504 | tf_op jit(solution)/shard_map/ppermute | solution.py:648
  23.2 1.5 %collective-permute-start.2 = (s32[8,26]{1,0:T(8,128)S(1)}, s32[8,26]{1,0:T(8,128)S(1)}, u32[]{:S(2)}, u32[]{:S(2)}) collective-permute-start(s32[8,26]{1,0:T(8,128)S(1)} %get-tuple-element.45.refs_0_), channel_id=1, source_target_pairs={{0,16},{8,24},{16,0},{24,8},{1,17},{9,25},{17,1},{25,9},{2,18},{10... | collective-permute-start | bytes 2504 | tf_op jit(solution)/shard_map/ppermute | solution.py:648
  24.7 0.5 collective-permute-start.3
  25.2 11.8 %project.1 = (bf16[32,2,1408]{2,1,0:T(2,128)(2,1)}, bf16[8,896]{1,0:T(8,128)(2,1)S(1)}, bf16[64,768]{1,0:T(8,128)(2,1)S(1)}) custom-call(bf16[4,72,768]{2,1,0:T(8,128)(2,1)S(1)} %all-to-all-done.refs_0_, bf16[4,72,768]{2,1,0:T(8,128)(2,1)S(1)} %collective-permute-done.refs_1_, f32[2,6144]{1,0:T(2,128)S(1)} %get-tuple-element.37.refs_2_, ...), custom_call_target="tpu_custom_call" | custom-call | flops 2038431744 | bytes 28311552 | tf_op jit(solution)/shard_map/project/pallas_call | solution.py:717
  37.0 0.0 collective-permute-done.1.refs_1_
  37.0 3.7 %all-to-all-start.1 = ((bf16[32,2,1408]{2,1,0:T(2,128)(2,1)}), bf16[32,2,1408]{2,1,0:T(2,128)(2,1)S(1)}, u32[]{:S(2)}, u32[]{:S(2)}) async-start(bf16[32,2,1408]{2,1,0:T(2,128)(2,1)} %get-tuple-element.44), calls=%async_computation.1 | async-start | bytes 360448 | tf_op jit(solution)/shard_map/all_to_all | solution.py:745
  40.7 1.4 %facts.1 = (f32[16,192]{1,0:T(8,128)S(1)}, f32[208,128]{1,0:T(8,128)S(1)}, bf16[208,128]{1,0:T(8,128)(2,1)S(1)}) custom-call(s32[8,26]{1,0:T(8,128)S(1)} %get-tuple-element.45.refs_0_, s32[8,26]{1,0:T(8,128)S(1)} %collective-permute-done.1.refs_1_, s32[8,26]{1,0:T(8,128)S(1)} %collective-permute-done.2.refs_2_, s32[8,26]{1,0:T(8,128)S(1)} %collective-permute-done.3.refs_3_, ...), custom_call_target="tpu_custom_call" | custom-call | tf_op jit(solution)/shard_map/facts/pallas_call | solution.py:746
  42.1 1.8 %collective-permute-start.4 = (bf16[64,768]{1,0:T(8,128)(2,1)S(1)}, bf16[64,768]{1,0:T(8,128)(2,1)S(1)}, u32[]{:S(2)}, u32[]{:S(2)}) collective-permute-start(bf16[64,768]{1,0:T(8,128)(2,1)S(1)} %get-tuple-element.59.refs_0_), channel_id=1, source_target_pairs={{0,8},{8,0},{16,24},{24,16},{1,9},{9,1},{17,25},{25,17},{2,10},{10... | collective-permute-start | bytes 294920 | tf_op jit(solution)/shard_map/ppermute | solution.py:648
  43.9 1.5 %collective-permute-start.5 = (bf16[64,768]{1,0:T(8,128)(2,1)S(1)}, bf16[64,768]{1,0:T(8,128)(2,1)S(1)}, u32[]{:S(2)}, u32[]{:S(2)}) collective-permute-start(bf16[64,768]{1,0:T(8,128)(2,1)S(1)} %get-tuple-element.59.refs_0_), channel_id=1, source_target_pairs={{0,16},{8,24},{16,0},{24,8},{1,17},{9,25},{17,1},{25,9},{2,18},{10... | collective-permute-start | bytes 294920 | tf_op jit(solution)/shard_map/ppermute | solution.py:648
  45.4 0.3 collective-permute-start.6
  45.7 2.8 %fold.1.fold_ref = bf16[16,12288]{1,0:T(8,128)(2,1)S(1)} custom-call(f32[16,192]{1,0:T(8,128)S(1)} %get-tuple-element.53.weight_ref, bf16[192,12288]{1,0:T(8,128)(2,1)} %bitcast.10), custom_call_target="tpu_custom_call" | custom-call | tf_op jit(solution)/shard_map/fold/pallas_call | solution.py:763
  48.5 0.8 all-to-all-done.1
  49.3 6.3 %attend.1.refs_6_ = bf16[4,8,2,3712]{3,2,1,0:T(2,128)(2,1)} custom-call(bf16[4,8,2,1408]{3,2,1,0:T(2,128)(2,1)S(1)} %bitcast.9, f32[208,128]{1,0:T(8,128)S(1)} %get-tuple-element.49.valid_ref, bf16[208,128]{1,0:T(8,128)(2,1)S(1)} %get-tuple-element.50.place_ref, bf16[192,12288]{1,0:T(8,128)(2,1)} %bitcast.11, bf16[16,12288]{1,0:T(8,128)(2,1)S(1)} %fold.1.fold_ref), custom_call_target="tpu_custom_call" | custom-call | flops 603979776 | bytes 4718592 | tf_op jit(solution)/shard_map/attend/pallas_call | solution.py:779
  55.7 0.0 collective-permute-done.4.refs_1_
  55.7 0.0 collective-permute-done.5.refs_2_
  55.7 5.1 %all-to-all-start.2 = ((bf16[32,2,3712]{2,1,0:T(2,128)(2,1)}), bf16[32,2,3712]{2,1,0:T(2,128)(2,1)S(1)}, u32[]{:S(2)}, u32[]{:S(2)}) async-start(bf16[32,2,3712]{2,1,0:T(2,128)(2,1)} %bitcast.7), calls=%async_computation.2 | async-start | bytes 950272 | tf_op jit(solution)/shard_map/all_to_all | solution.py:796
  60.7 7.7 %mlp.1 = (bf16[8,6144]{1,0:T(8,128)(2,1)S(1)}, bf16[8,6144]{1,0:T(8,128)(2,1)S(1)}, bf16[8,6144]{1,0:T(8,128)(2,1)S(1)}, bf16[8,6144]{1,0:T(8,128)(2,1)S(1)}) custom-call(bf16[64,768]{1,0:T(8,128)(2,1)S(1)} %get-tuple-element.59.refs_0_, bf16[64,768]{1,0:T(8,128)(2,1)S(1)} %collective-permute-done.4.refs_1_, ...), custom_call_target="tpu_custom_call" | custom-call | flops 603979776 | bytes 18874368 | tf_op jit(solution)/shard_map/mlp/pallas_call | solution.py:799
  68.5 1.8 %collective-permute-start.7 = (bf16[8,6144]{1,0:T(8,128)(2,1)S(1)}, bf16[8,6144]{1,0:T(8,128)(2,1)S(1)}, u32[]{:S(2)}, u32[]{:S(2)}) collective-permute-start(bf16[8,6144]{1,0:T(8,128)(2,1)S(1)} %get-tuple-element.64), channel_id=1, source_target_pairs={{0,8},{8,0},{16,24},{24,16},{1,9},{9,1},{17,25},{25,17},{2,10},{10... | collective-permute-start | bytes 294920 | tf_op jit(solution)/shard_map/ppermute | solution.py:648
  70.3 1.5 %collective-permute-start.8 = (bf16[8,6144]{1,0:T(8,128)(2,1)S(1)}, bf16[8,6144]{1,0:T(8,128)(2,1)S(1)}, u32[]{:S(2)}, u32[]{:S(2)}) collective-permute-start(bf16[8,6144]{1,0:T(8,128)(2,1)S(1)} %get-tuple-element.65), channel_id=1, source_target_pairs={{0,16},{8,24},{16,0},{24,8},{1,17},{9,25},{17,1},{25,9},{2,18},{10... | collective-permute-start | bytes 294920 | tf_op jit(solution)/shard_map/ppermute | solution.py:648
  71.8 0.3 collective-permute-start.9
  72.0 2.4 %collective-permute-done.7.refs_1_ = bf16[8,6144]{1,0:T(8,128)(2,1)S(1)} collective-permute-done((bf16[8,6144]{1,0:T(8,128)(2,1)S(1)}, bf16[8,6144]{1,0:T(8,128)(2,1)S(1)}, u32[]{:S(2)}, u32[]{:S(2)}) %collective-permute-start.7) | collective-permute-done | bytes 98336 | tf_op jit(solution)/shard_map/ppermute | solution.py:648
  74.4 2.3 %collective-permute-done.8.refs_2_ = bf16[8,6144]{1,0:T(8,128)(2,1)S(1)} collective-permute-done((bf16[8,6144]{1,0:T(8,128)(2,1)S(1)}, bf16[8,6144]{1,0:T(8,128)(2,1)S(1)}, u32[]{:S(2)}, u32[]{:S(2)}) %collective-permute-start.8) | collective-permute-done | bytes 98336 | tf_op jit(solution)/shard_map/ppermute | solution.py:648
  76.6 1.3 %collective-permute-done.9.refs_3_ = bf16[8,6144]{1,0:T(8,128)(2,1)S(1)} collective-permute-done((bf16[8,6144]{1,0:T(8,128)(2,1)S(1)}, bf16[8,6144]{1,0:T(8,128)(2,1)S(1)}, u32[]{:S(2)}, u32[]{:S(2)}) %collective-permute-start.9) | collective-permute-done | bytes 98336 | tf_op jit(solution)/shard_map/ppermute | solution.py:648
  78.0 5.3 %merge.1 = bf16[8,8,768]{2,1,0:T(8,128)(2,1)} custom-call(bf16[32,2,3712]{2,1,0:T(2,128)(2,1)S(1)} %all-to-all-done.2.got_ref, bf16[8,896]{1,0:T(8,128)(2,1)S(1)} %get-tuple-element.56.own_ref, f32[104,8]{1,0:T(8,128)S(1)} %get-tuple-element.57.sel_ref, bf16[8,104]{1,0:T(8,128)(2,1)S(1)} %get-tuple-element.58.back_ref, ...), custom_call_target="tpu_custom_call" | custom-call | flops 75497472 | bytes 9437184 | tf_op jit(solution)/shard_map/merge/pallas_call | solution.py:816
  83.3 4.0 %all-to-all-start.3 = ((bf16[8,8,768]{2,1,0:T(8,128)(2,1)}), bf16[8,8,768]{2,1,0:T(8,128)(2,1)S(1)}, u32[]{:S(2)}, u32[]{:S(2)}) async-start(bf16[8,8,768]{2,1,0:T(8,128)(2,1)} %merge.1), calls=%async_computation.3 | async-start | bytes 196608 | tf_op jit(solution)/shard_map/all_to_all | solution.py:837
  87.2 1.2 %place.1 = bf16[12,8,1536]{2,1,0:T(8,128)(2,1)} custom-call(bf16[96,96]{1,0:T(8,128)(2,1)S(1)} %get-tuple-element.67.pick_ref, bf16[32,2,3712]{2,1,0:T(2,128)(2,1)S(1)} %all-to-all-done.2.got_ref), custom_call_target="tpu_custom_call" | custom-call | bytes 589824 | tf_op jit(solution)/shard_map/place/pallas_call | solution.py:840
  88.4 5.1 %all-to-all-done.3 = bf16[8,8,768]{2,1,0:T(8,128)(2,1)S(1)} async-done(((bf16[8,8,768]{2,1,0:T(8,128)(2,1)}), bf16[8,8,768]{2,1,0:T(8,128)(2,1)S(1)}, u32[]{:S(2)}, u32[]{:S(2)}) %all-to-all-start.3) | async-done | bytes 98336 | tf_op jit(solution)/shard_map/all_to_all | solution.py:837
  93.6 0.6 reduce_sum.12
  (6 shorter events, 0.0 us)
Async XLA Ops:
  2.6 19.1 %all-to-all-start = ((bf16[4,72,768]{2,1,0:T(8,128)(2,1)}), bf16[4,72,768]{2,1,0:T(8,128)(2,1)S(1)}, u32[]{:S(2)}, u32[]{:S(2)}) async-start(bf16[4,72,768]{2,1,0:T(8,128)(2,1)} %pack.1), calls=%async_computation | async-start | bytes 884736 | tf_op jit(solution)/shard_map/all_to_all | solution.py:662
  21.7 3.5 %collective-permute-start = (bf16[4,72,768]{2,1,0:T(8,128)(2,1)S(1)}, bf16[4,72,768]{2,1,0:T(8,128)(2,1)S(1)}, u32[]{:S(2)}, u32[]{:S(2)}) collective-permute-start(bf16[4,72,768]{2,1,0:T(8,128)(2,1)S(1)} %all-to-all-done.refs_0_), channel_id=1, source_target_pairs={{0,1},{1,0},{2,3},{3,2},{4,5},{5,4},{6,7},{7,6},{8,9},{9,8},{10,11... | collective-permute-start | bytes 1327112 | tf_op jit(solution)/shard_map/ppermute | solution.py:648
  21.7 15.3 %collective-permute-start.1 = (s32[8,26]{1,0:T(8,128)S(1)}, s32[8,26]{1,0:T(8,128)S(1)}, u32[]{:S(2)}, u32[]{:S(2)}) collective-permute-start(s32[8,26]{1,0:T(8,128)S(1)} %get-tuple-element.45.refs_0_), channel_id=1, source_target_pairs={{0,8},{8,0},{16,24},{24,16},{1,9},{9,1},{17,25},{25,17},{2,10},{10... | collective-permute-start | bytes 2504 | tf_op jit(solution)/shard_map/ppermute | solution.py:648
  23.2 13.8 %collective-permute-start.2 = (s32[8,26]{1,0:T(8,128)S(1)}, s32[8,26]{1,0:T(8,128)S(1)}, u32[]{:S(2)}, u32[]{:S(2)}) collective-permute-start(s32[8,26]{1,0:T(8,128)S(1)} %get-tuple-element.45.refs_0_), channel_id=1, source_target_pairs={{0,16},{8,24},{16,0},{24,8},{1,17},{9,25},{17,1},{25,9},{2,18},{10... | collective-permute-start | bytes 2504 | tf_op jit(solution)/shard_map/ppermute | solution.py:648
  24.7 12.3 %collective-permute-start.3 = (s32[8,26]{1,0:T(8,128)S(1)}, s32[8,26]{1,0:T(8,128)S(1)}, u32[]{:S(2)}, u32[]{:S(2)}) collective-permute-start(s32[8,26]{1,0:T(8,128)S(1)} %get-tuple-element.45.refs_0_), channel_id=1, source_target_pairs={{0,24},{8,16},{16,8},{24,0},{1,25},{9,17},{17,9},{25,1},{2,26},{10... | collective-permute-start | bytes 2504 | tf_op jit(solution)/shard_map/ppermute | solution.py:648
  37.0 12.3 %all-to-all-start.1 = ((bf16[32,2,1408]{2,1,0:T(2,128)(2,1)}), bf16[32,2,1408]{2,1,0:T(2,128)(2,1)S(1)}, u32[]{:S(2)}, u32[]{:S(2)}) async-start(bf16[32,2,1408]{2,1,0:T(2,128)(2,1)} %get-tuple-element.44), calls=%async_computation.1 | async-start | bytes 360448 | tf_op jit(solution)/shard_map/all_to_all | solution.py:745
  42.1 13.5 %collective-permute-start.4 = (bf16[64,768]{1,0:T(8,128)(2,1)S(1)}, bf16[64,768]{1,0:T(8,128)(2,1)S(1)}, u32[]{:S(2)}, u32[]{:S(2)}) collective-permute-start(bf16[64,768]{1,0:T(8,128)(2,1)S(1)} %get-tuple-element.59.refs_0_), channel_id=1, source_target_pairs={{0,8},{8,0},{16,24},{24,16},{1,9},{9,1},{17,25},{25,17},{2,10},{10... | collective-permute-start | bytes 294920 | tf_op jit(solution)/shard_map/ppermute | solution.py:648
  43.9 11.7 %collective-permute-start.5 = (bf16[64,768]{1,0:T(8,128)(2,1)S(1)}, bf16[64,768]{1,0:T(8,128)(2,1)S(1)}, u32[]{:S(2)}, u32[]{:S(2)}) collective-permute-start(bf16[64,768]{1,0:T(8,128)(2,1)S(1)} %get-tuple-element.59.refs_0_), channel_id=1, source_target_pairs={{0,16},{8,24},{16,0},{24,8},{1,17},{9,25},{17,1},{25,9},{2,18},{10... | collective-permute-start | bytes 294920 | tf_op jit(solution)/shard_map/ppermute | solution.py:648
  45.4 10.2 %collective-permute-start.6 = (bf16[64,768]{1,0:T(8,128)(2,1)S(1)}, bf16[64,768]{1,0:T(8,128)(2,1)S(1)}, u32[]{:S(2)}, u32[]{:S(2)}) collective-permute-start(bf16[64,768]{1,0:T(8,128)(2,1)S(1)} %get-tuple-element.59.refs_0_), channel_id=1, source_target_pairs={{0,24},{8,16},{16,8},{24,0},{1,25},{9,17},{17,9},{25,1},{2,26},{10... | collective-permute-start | bytes 294920 | tf_op jit(solution)/shard_map/ppermute | solution.py:648
  55.7 22.3 %all-to-all-start.2 = ((bf16[32,2,3712]{2,1,0:T(2,128)(2,1)}), bf16[32,2,3712]{2,1,0:T(2,128)(2,1)S(1)}, u32[]{:S(2)}, u32[]{:S(2)}) async-start(bf16[32,2,3712]{2,1,0:T(2,128)(2,1)} %bitcast.7), calls=%async_computation.2 | async-start | bytes 950272 | tf_op jit(solution)/shard_map/all_to_all | solution.py:796
  68.5 5.9 %collective-permute-start.7 = (bf16[8,6144]{1,0:T(8,128)(2,1)S(1)}, bf16[8,6144]{1,0:T(8,128)(2,1)S(1)}, u32[]{:S(2)}, u32[]{:S(2)}) collective-permute-start(bf16[8,6144]{1,0:T(8,128)(2,1)S(1)} %get-tuple-element.64), channel_id=1, source_target_pairs={{0,8},{8,0},{16,24},{24,16},{1,9},{9,1},{17,25},{25,17},{2,10},{10... | collective-permute-start | bytes 294920 | tf_op jit(solution)/shard_map/ppermute | solution.py:648
  70.3 6.3 %collective-permute-start.8 = (bf16[8,6144]{1,0:T(8,128)(2,1)S(1)}, bf16[8,6144]{1,0:T(8,128)(2,1)S(1)}, u32[]{:S(2)}, u32[]{:S(2)}) collective-permute-start(bf16[8,6144]{1,0:T(8,128)(2,1)S(1)} %get-tuple-element.65), channel_id=1, source_target_pairs={{0,16},{8,24},{16,0},{24,8},{1,17},{9,25},{17,1},{25,9},{2,18},{10... | collective-permute-start | bytes 294920 | tf_op jit(solution)/shard_map/ppermute | solution.py:648
  71.8 6.2 %collective-permute-start.9 = (bf16[8,6144]{1,0:T(8,128)(2,1)S(1)}, bf16[8,6144]{1,0:T(8,128)(2,1)S(1)}, u32[]{:S(2)}, u32[]{:S(2)}) collective-permute-start(bf16[8,6144]{1,0:T(8,128)(2,1)S(1)} %get-tuple-element.66), channel_id=1, source_target_pairs={{0,24},{8,16},{16,8},{24,0},{1,25},{9,17},{17,9},{25,1},{2,26},{10... | collective-permute-start | bytes 294920 | tf_op jit(solution)/shard_map/ppermute | solution.py:648
  83.3 10.3 %all-to-all-start.3 = ((bf16[8,8,768]{2,1,0:T(8,128)(2,1)}), bf16[8,8,768]{2,1,0:T(8,128)(2,1)S(1)}, u32[]{:S(2)}, u32[]{:S(2)}) async-start(bf16[8,8,768]{2,1,0:T(8,128)(2,1)} %merge.1), calls=%async_computation.3 | async-start | bytes 196608 | tf_op jit(solution)/shard_map/all_to_all | solution.py:837

commit v5 on v4

--- a/solution.py
+++ b/solution.py
@@ -28,6 +28,7 @@
 SCALE = 1.0 / math.sqrt(HD)
 MIB = 1024 * 1024
 STEP_HEADS = 32
+ATTEND_HEADS = 64
 QUAD = 4
 OCTET = 8
 
@@ -391,13 +392,22 @@
         out_ref[j] = found[j * group : (j + 1) * group]
 
 
-def attend_kernel(dims, ask_ref, valid_ref, place_ref, page_ref, fold_ref, *refs):
-    send_ref = refs[-1]
+def attend_kernel(dims, ask_ref, valid_ref, place_ref, page_hbm, fold_ref, send_ref, page_buf, sems):
     n_pages, slots, dests, heads = dims
     rows = n_pages * slots
     head_lanes = heads * HD
     extra = 2 * heads * NREC
-    tokens = page_ref.shape[0]
+    tokens = page_hbm.shape[0]
+    octets = range(ATTEND_HEADS // OCTET)
+    octet_lanes = OCTET * 2 * HD
+
+    def page_copy(o):
+        return pltpu.make_async_copy(
+            page_hbm.at[:, pl.ds(o * octet_lanes, octet_lanes)], page_buf.at[o], sems.at[o]
+        )
+
+    for o in octets:
+        page_copy(o).start()
     width = head_lanes + extra
     asks = []
     for b in range(dests):
@@ -424,7 +434,6 @@
         hit = (lane_in >= i * heads) & (lane_in < (i + 1) * heads)
         hit = hit & (row_head == lane_dest + lane_in - i * heads)
         goals.append(jnp.where(hit, 1.0, 0.0).astype(BF16))
-    octets = range(STEP_HEADS // OCTET)
     all_scores = []
     for o in octets:
         heads_here = range(o * OCTET, (o + 1) * OCTET)
@@ -436,8 +445,8 @@
         stacked = jnp.concatenate(stacked, axis=0).astype(BF16)
         told = jnp.concatenate([given[:, o * lanes : (o + 1) * lanes]] * OCTET, axis=0)
         told = jnp.where(given_head == row_head, told, 0.0).T.astype(BF16)
-        some = slice(o * OCTET * 2 * HD, (o + 1) * OCTET * 2 * HD)
-        page = jnp.concatenate([page_ref[:, some], fold_ref[:, some]], axis=0)
+        page_copy(o).wait()
+        page = jnp.concatenate([page_buf[o], fold_ref[:, o * octet_lanes : (o + 1) * octet_lanes]], axis=0)
         all_scores.append(jnp.where(touched, dot(place, told), dot(page, stacked) * SCALE))
     all_weights, extras = [], []
     for scores in all_scores:
@@ -456,9 +465,9 @@
     gathered = []
     for o in octets:
         for i in range(OCTET // QUAD):
-            first = (o * OCTET + i * QUAD) * 2 * HD
-            some = slice(first, first + QUAD * 2 * HD)
-            page = [page_ref[:, some], fold_ref[:, some]]
+            quad_lanes = QUAD * 2 * HD
+            first = o * octet_lanes + i * quad_lanes
+            page = [page_buf[o, :, i * quad_lanes : (i + 1) * quad_lanes], fold_ref[:, first : first + quad_lanes]]
             page.append(jnp.zeros((256 - tokens - rows, QUAD * 2 * HD), BF16))
             mixed = dot(all_weights[o][i * QUAD * rows : (i + 1) * QUAD * rows], jnp.concatenate(page, axis=0))
             for h in range(QUAD):
@@ -525,15 +534,15 @@
     totals = jnp.zeros((group, 128), F32)
     for part in parts_of(weights, 3):
         totals = totals + dot(back, part)
-    inverse = 1.0 / totals
     lanes, heads_of = iota((128, head_lanes), 1), iota((128, head_lanes), 0)
     over = lanes - heads_of * HD
     spread = jnp.where((over >= 0) & (over < HD), 1.0, 0.0).astype(BF16)
     weighted = split_dot(weights, spread, 2) * rows_ref[:, :head_lanes]
+    inverse = split_dot(1.0 / totals, spread, 3)
     mixed = jnp.zeros((group, head_lanes), F32)
     for part in parts_of(weighted, 2):
         mixed = mixed + dot(back, part)
-    attended = (mixed * split_dot(inverse, spread, 3)).astype(BF16)
+    attended = (mixed * inverse).astype(BF16)
     for step in range(steps):
         dense_copy(step).wait()
         some = slice(step * cols, (step + 1) * cols)
@@ -707,7 +716,6 @@
     pages = page_store.reshape(tokens, 2 * D)
     steps = H // STEP_HEADS
     step_lanes = STEP_HEADS * 2 * HD
-    dests = STEP_HEADS // heads
     fold_width = 2 * head_lanes
 
     pack, cosine = lax.optimization_barrier((pack, cosine))
@@ -777,18 +785,15 @@
     all_lanes = lanes + fold_width
     all_wire = all_lanes + wire_split(all_lanes)
     partial = pl.pallas_call(
-        functools.partial(attend_kernel, (n_pages, slots, dests, heads)),
-        grid=(steps,),
-        in_specs=[
-            pl.BlockSpec((n_pages, dests, 2, wire), lambda i: (0, i, 0, 0)),
-            pl.BlockSpec((tokens + ranks, OCTET * ranks), lambda i: (0, 0)),
-            pl.BlockSpec((tokens + ranks, 2 * OCTET * NREC), lambda i: (0, 0)),
-            pl.BlockSpec((tokens, step_lanes), lambda i: (0, i)),
-            pl.BlockSpec((ranks, step_lanes), lambda i: (0, i)),
+        functools.partial(attend_kernel, (n_pages, slots, n_blk, heads)),
+        in_specs=[VMEM, VMEM, VMEM, HBM, VMEM],
+        out_specs=VMEM,
+        out_shape=shape_of((n_pages, n_blk, 2, all_wire)),
+        scratch_shapes=[
+            pltpu.VMEM((H // OCTET, tokens, OCTET * 2 * HD), BF16),
+            pltpu.SemaphoreType.DMA((H // OCTET,)),
         ],
-        out_specs=pl.BlockSpec((n_pages, dests, 2, all_wire), lambda i: (0, i, 0, 0)),
-        out_shape=shape_of((n_pages, n_blk, 2, all_wire)),
-        compiler_params=params_of(16),
+        compiler_params=params_of(32),
         cost_estimate=cost_of(2 * 128 * tokens * 2 * D, tokens * 4 * D),
         name="attend",
     )(asked.reshape(n_pages, n_blk, 2, wire), valid, renew, fixed(pages), folded_rows)

time: 94.7 us -> 95.4 us (level)
  transfers between devices with their start and end apart: 14 -> 14, of which waited for: 6 -> 6; matrix products, arithmetic and copies ran while one was open for 0% -> 0% of each run, Pallas kernels for 35% -> 36%
where the time goes in v5:
time: 95.4 us; the launch traced here: 94.9 us
  Pallas kernels  41.2 us (43%)
  starting transfers between devices  29.8 us (31%)
  waiting for transfers between devices  22.4 us (23%)
    pallas_call x1, Pallas kernels, on_device(): pl.pallas_call(functools.partial(project_kernel, (group, n_blk, held_rows...  11.8 us
    all_to_all x1, waiting for transfers between devices, on_device(): lax.all_to_all(pack, 'blk', 0, 0, axis_index_groups=[list(range(core, n_b...  10.7 us
    ppermute x10, starting transfers between devices, swapped(): return lax.ppermute(array, axis, [(i, i ^ by) for i in range(size)])  10.6 us
    pallas_call x1, Pallas kernels, on_device(): pl.pallas_call(functools.partial(mlp_kernel, (group, n_pages, n_blk)), in...  7.71 us
    pallas_call x1, Pallas kernels, on_device(): pl.pallas_call(functools.partial(attend_kernel, (n_pages, slots, n_blk, h...  7.01 us
    all_to_all x1, starting transfers between devices, on_device(): lax.all_to_all(pack, 'blk', 0, 0, axis_index_groups=[list(range(core, n_b...  6.32 us
    ppermute x10, waiting for transfers between devices, swapped(): return lax.ppermute(array, axis, [(i, i ^ by) for i in range(size)])  5.78 us
    pallas_call x1, Pallas kernels, on_device(): pl.pallas_call(functools.partial(merge_kernel, (group, n_dev, heads, n_pa...  5.26 us
  transfers between devices with their start and end apart: 14, of which 6 were waited for; matrix products, arithmetic and copies ran while one was open for 0% of the time, Pallas kernels for 36%

profile of v5, /device:TPU:0, one launch (start us, length us, event | category | flops | bytes accessed | tf_op | source)
XLA Modules:
  0.0 94.9 jit_solution(37685873212827434)
XLA Ops:
  0.6 2.0 %pack.1 = bf16[4,72,768]{2,1,0:T(8,128)(2,1)} custom-call(bf16[8,6144]{1,0:T(8,128)(2,1)} %bitcast.15, bf16[8,768]{1,0:T(8,128)(2,1)} %new_ref.1, f32[1,6144]{1,0:T(1,128)} %bitcast.13), custom_call_target="tpu_custom_call" | custom-call | tf_op jit(solution)/shard_map/pack/pallas_call | solution.py:663
  2.6 6.3 %all-to-all-start = ((bf16[4,72,768]{2,1,0:T(8,128)(2,1)}), bf16[4,72,768]{2,1,0:T(8,128)(2,1)S(1)}, u32[]{:S(2)}, u32[]{:S(2)}) async-start(bf16[4,72,768]{2,1,0:T(8,128)(2,1)} %pack.1), calls=%async_computation | async-start | bytes 884736 | tf_op jit(solution)/shard_map/all_to_all | solution.py:671
  8.9 2.0 %prep.1 = (f32[2,6144]{1,0:T(2,128)S(1)}, f32[72,1152]{1,0:T(8,128)S(1)}, f32[72,1152]{1,0:T(8,128)S(1)}, f32[72,1152]{1,0:T(8,128)S(1)}, bf16[96,8]{1,0:T(8,128...) custom-call(s32[12,32]{1,0:T(8,128)} %bitcast.16, ...), custom_call_target="tpu_custom_call" | custom-call | tf_op jit(solution)/shard_map/prep/pallas_call | solution.py:685
  10.9 10.7 %all-to-all-done.refs_0_ = bf16[4,72,768]{2,1,0:T(8,128)(2,1)S(1)} async-done(((bf16[4,72,768]{2,1,0:T(8,128)(2,1)}), bf16[4,72,768]{2,1,0:T(8,128)(2,1)S(1)}, u32[]{:S(2)}, u32[]{:S(2)}) %all-to-all-start) | async-done | bytes 442400 | tf_op jit(solution)/shard_map/all_to_all | solution.py:671
  21.7 1.5 %collective-permute-start.1 = (s32[8,26]{1,0:T(8,128)S(1)}, s32[8,26]{1,0:T(8,128)S(1)}, u32[]{:S(2)}, u32[]{:S(2)}) collective-permute-start(s32[8,26]{1,0:T(8,128)S(1)} %get-tuple-element.45.refs_0_), channel_id=1, source_target_pairs={{0,8},{8,0},{16,24},{24,16},{1,9},{9,1},{17,25},{25,17},{2,10},{10... | collective-permute-start | bytes 2504 | tf_op jit(solution)/shard_map/ppermute | solution.py:657
  23.2 1.5 %collective-permute-start.2 = (s32[8,26]{1,0:T(8,128)S(1)}, s32[8,26]{1,0:T(8,128)S(1)}, u32[]{:S(2)}, u32[]{:S(2)}) collective-permute-start(s32[8,26]{1,0:T(8,128)S(1)} %get-tuple-element.45.refs_0_), channel_id=1, source_target_pairs={{0,16},{8,24},{16,0},{24,8},{1,17},{9,25},{17,1},{25,9},{2,18},{10... | collective-permute-start | bytes 2504 | tf_op jit(solution)/shard_map/ppermute | solution.py:657
  24.7 0.5 collective-permute-start.3
  25.2 11.8 %project.1 = (bf16[32,2,1408]{2,1,0:T(2,128)(2,1)}, bf16[8,896]{1,0:T(8,128)(2,1)S(1)}, bf16[64,768]{1,0:T(8,128)(2,1)S(1)}) custom-call(bf16[4,72,768]{2,1,0:T(8,128)(2,1)S(1)} %all-to-all-done.refs_0_, bf16[4,72,768]{2,1,0:T(8,128)(2,1)S(1)} %collective-permute-done.refs_1_, f32[2,6144]{1,0:T(2,128)S(1)} %get-tuple-element.37.refs_2_, ...), custom_call_target="tpu_custom_call" | custom-call | flops 2038431744 | bytes 28311552 | tf_op jit(solution)/shard_map/project/pallas_call | solution.py:725
  37.0 0.0 collective-permute-done.1.refs_1_
  37.0 0.0 collective-permute-done.2.refs_2_
  37.0 3.7 %all-to-all-start.1 = ((bf16[32,2,1408]{2,1,0:T(2,128)(2,1)}), bf16[32,2,1408]{2,1,0:T(2,128)(2,1)S(1)}, u32[]{:S(2)}, u32[]{:S(2)}) async-start(bf16[32,2,1408]{2,1,0:T(2,128)(2,1)} %get-tuple-element.44), calls=%async_computation.1 | async-start | bytes 360448 | tf_op jit(solution)/shard_map/all_to_all | solution.py:753
  40.7 1.4 %facts.1 = (f32[16,192]{1,0:T(8,128)S(1)}, f32[208,128]{1,0:T(8,128)S(1)}, bf16[208,128]{1,0:T(8,128)(2,1)S(1)}) custom-call(s32[8,26]{1,0:T(8,128)S(1)} %get-tuple-element.45.refs_0_, s32[8,26]{1,0:T(8,128)S(1)} %collective-permute-done.1.refs_1_, s32[8,26]{1,0:T(8,128)S(1)} %collective-permute-done.2.refs_2_, s32[8,26]{1,0:T(8,128)S(1)} %collective-permute-done.3.refs_3_, ...), custom_call_target="tpu_custom_call" | custom-call | tf_op jit(solution)/shard_map/facts/pallas_call | solution.py:754
  42.1 1.8 %collective-permute-start.4 = (bf16[64,768]{1,0:T(8,128)(2,1)S(1)}, bf16[64,768]{1,0:T(8,128)(2,1)S(1)}, u32[]{:S(2)}, u32[]{:S(2)}) collective-permute-start(bf16[64,768]{1,0:T(8,128)(2,1)S(1)} %get-tuple-element.59.refs_0_), channel_id=1, source_target_pairs={{0,8},{8,0},{16,24},{24,16},{1,9},{9,1},{17,25},{25,17},{2,10},{10... | collective-permute-start | bytes 294920 | tf_op jit(solution)/shard_map/ppermute | solution.py:657
  44.0 1.5 %collective-permute-start.5 = (bf16[64,768]{1,0:T(8,128)(2,1)S(1)}, bf16[64,768]{1,0:T(8,128)(2,1)S(1)}, u32[]{:S(2)}, u32[]{:S(2)}) collective-permute-start(bf16[64,768]{1,0:T(8,128)(2,1)S(1)} %get-tuple-element.59.refs_0_), channel_id=1, source_target_pairs={{0,16},{8,24},{16,0},{24,8},{1,17},{9,25},{17,1},{25,9},{2,18},{10... | collective-permute-start | bytes 294920 | tf_op jit(solution)/shard_map/ppermute | solution.py:657
  45.4 0.3 collective-permute-start.6
  45.7 2.8 %fold.1.fold_ref = bf16[16,12288]{1,0:T(8,128)(2,1)S(1)} custom-call(f32[16,192]{1,0:T(8,128)S(1)} %get-tuple-element.53.weight_ref, bf16[192,12288]{1,0:T(8,128)(2,1)} %bitcast.10), custom_call_target="tpu_custom_call" | custom-call | tf_op jit(solution)/shard_map/fold/pallas_call | solution.py:771
  48.5 0.8 all-to-all-done.1
  49.3 7.0 %attend.1.refs_6_ = bf16[4,8,2,3712]{3,2,1,0:T(2,128)(2,1)} custom-call(bf16[4,8,2,1408]{3,2,1,0:T(2,128)(2,1)S(1)} %bitcast.9, f32[208,128]{1,0:T(8,128)S(1)} %get-tuple-element.49.valid_ref, bf16[208,128]{1,0:T(8,128)(2,1)S(1)} %get-tuple-element.50.place_ref, bf16[192,12288]{1,0:T(8,128)(2,1)} %bitcast.11, bf16[16,12288]{1,0:T(8,128)(2,1)S(1)} %fold.1.fold_ref), custom_call_target="tpu_custom_call" | custom-call | flops 603979776 | bytes 4718592 | tf_op jit(solution)/shard_map/attend/pallas_call | solution.py:787
  56.4 0.0 collective-permute-done.5.refs_2_
  56.4 5.2 %all-to-all-start.2 = ((bf16[32,2,3712]{2,1,0:T(2,128)(2,1)}), bf16[32,2,3712]{2,1,0:T(2,128)(2,1)S(1)}, u32[]{:S(2)}, u32[]{:S(2)}) async-start(bf16[32,2,3712]{2,1,0:T(2,128)(2,1)} %bitcast.7), calls=%async_computation.2 | async-start | bytes 950272 | tf_op jit(solution)/shard_map/all_to_all | solution.py:801
  61.6 7.7 %mlp.1 = (bf16[8,6144]{1,0:T(8,128)(2,1)S(1)}, bf16[8,6144]{1,0:T(8,128)(2,1)S(1)}, bf16[8,6144]{1,0:T(8,128)(2,1)S(1)}, bf16[8,6144]{1,0:T(8,128)(2,1)S(1)}) custom-call(bf16[64,768]{1,0:T(8,128)(2,1)S(1)} %get-tuple-element.59.refs_0_, bf16[64,768]{1,0:T(8,128)(2,1)S(1)} %collective-permute-done.4.refs_1_, ...), custom_call_target="tpu_custom_call" | custom-call | flops 603979776 | bytes 18874368 | tf_op jit(solution)/shard_map/mlp/pallas_call | solution.py:804
  69.3 1.7 %collective-permute-start.7 = (bf16[8,6144]{1,0:T(8,128)(2,1)S(1)}, bf16[8,6144]{1,0:T(8,128)(2,1)S(1)}, u32[]{:S(2)}, u32[]{:S(2)}) collective-permute-start(bf16[8,6144]{1,0:T(8,128)(2,1)S(1)} %get-tuple-element.64), channel_id=1, source_target_pairs={{0,8},{8,0},{16,24},{24,16},{1,9},{9,1},{17,25},{25,17},{2,10},{10... | collective-permute-start | bytes 294920 | tf_op jit(solution)/shard_map/ppermute | solution.py:657
  71.0 1.5 %collective-permute-start.8 = (bf16[8,6144]{1,0:T(8,128)(2,1)S(1)}, bf16[8,6144]{1,0:T(8,128)(2,1)S(1)}, u32[]{:S(2)}, u32[]{:S(2)}) collective-permute-start(bf16[8,6144]{1,0:T(8,128)(2,1)S(1)} %get-tuple-element.65), channel_id=1, source_target_pairs={{0,16},{8,24},{16,0},{24,8},{1,17},{9,25},{17,1},{25,9},{2,18},{10... | collective-permute-start | bytes 294920 | tf_op jit(solution)/shard_map/ppermute | solution.py:657
  72.5 0.4 collective-permute-start.9
  72.9 2.2 %collective-permute-done.7.refs_1_ = bf16[8,6144]{1,0:T(8,128)(2,1)S(1)} collective-permute-done((bf16[8,6144]{1,0:T(8,128)(2,1)S(1)}, bf16[8,6144]{1,0:T(8,128)(2,1)S(1)}, u32[]{:S(2)}, u32[]{:S(2)}) %collective-permute-start.7) | collective-permute-done | bytes 98336 | tf_op jit(solution)/shard_map/ppermute | solution.py:657
  75.1 2.2 %collective-permute-done.8.refs_2_ = bf16[8,6144]{1,0:T(8,128)(2,1)S(1)} collective-permute-done((bf16[8,6144]{1,0:T(8,128)(2,1)S(1)}, bf16[8,6144]{1,0:T(8,128)(2,1)S(1)}, u32[]{:S(2)}, u32[]{:S(2)}) %collective-permute-start.8) | collective-permute-done | bytes 98336 | tf_op jit(solution)/shard_map/ppermute | solution.py:657
  77.3 1.3 %collective-permute-done.9.refs_3_ = bf16[8,6144]{1,0:T(8,128)(2,1)S(1)} collective-permute-done((bf16[8,6144]{1,0:T(8,128)(2,1)S(1)}, bf16[8,6144]{1,0:T(8,128)(2,1)S(1)}, u32[]{:S(2)}, u32[]{:S(2)}) %collective-permute-start.9) | collective-permute-done | bytes 98336 | tf_op jit(solution)/shard_map/ppermute | solution.py:657
  78.7 5.3 %merge.1 = bf16[8,8,768]{2,1,0:T(8,128)(2,1)} custom-call(bf16[32,2,3712]{2,1,0:T(2,128)(2,1)S(1)} %all-to-all-done.2.got_ref, bf16[8,896]{1,0:T(8,128)(2,1)S(1)} %get-tuple-element.56.own_ref, f32[104,8]{1,0:T(8,128)S(1)} %get-tuple-element.57.sel_ref, bf16[8,104]{1,0:T(8,128)(2,1)S(1)} %get-tuple-element.58.back_ref, ...), custom_call_target="tpu_custom_call" | custom-call | flops 75497472 | bytes 9437184 | tf_op jit(solution)/shard_map/merge/pallas_call | solution.py:821
  83.9 4.0 %all-to-all-start.3 = ((bf16[8,8,768]{2,1,0:T(8,128)(2,1)}), bf16[8,8,768]{2,1,0:T(8,128)(2,1)S(1)}, u32[]{:S(2)}, u32[]{:S(2)}) async-start(bf16[8,8,768]{2,1,0:T(8,128)(2,1)} %merge.1), calls=%async_computation.3 | async-start | bytes 196608 | tf_op jit(solution)/shard_map/all_to_all | solution.py:842
  87.9 1.2 %place.1 = bf16[12,8,1536]{2,1,0:T(8,128)(2,1)} custom-call(bf16[96,96]{1,0:T(8,128)(2,1)S(1)} %get-tuple-element.67.pick_ref, bf16[32,2,3712]{2,1,0:T(2,128)(2,1)S(1)} %all-to-all-done.2.got_ref), custom_call_target="tpu_custom_call" | custom-call | bytes 589824 | tf_op jit(solution)/shard_map/place/pallas_call | solution.py:845
  89.1 5.1 %all-to-all-done.3 = bf16[8,8,768]{2,1,0:T(8,128)(2,1)S(1)} async-done(((bf16[8,8,768]{2,1,0:T(8,128)(2,1)}), bf16[8,8,768]{2,1,0:T(8,128)(2,1)S(1)}, u32[]{:S(2)}, u32[]{:S(2)}) %all-to-all-start.3) | async-done | bytes 98336 | tf_op jit(solution)/shard_map/all_to_all | solution.py:842
  94.2 0.6 reduce_sum.12
  (6 shorter events, 0.0 us)
Async XLA Ops:
  2.6 19.1 %all-to-all-start = ((bf16[4,72,768]{2,1,0:T(8,128)(2,1)}), bf16[4,72,768]{2,1,0:T(8,128)(2,1)S(1)}, u32[]{:S(2)}, u32[]{:S(2)}) async-start(bf16[4,72,768]{2,1,0:T(8,128)(2,1)} %pack.1), calls=%async_computation | async-start | bytes 884736 | tf_op jit(solution)/shard_map/all_to_all | solution.py:671
  21.7 3.5 %collective-permute-start = (bf16[4,72,768]{2,1,0:T(8,128)(2,1)S(1)}, bf16[4,72,768]{2,1,0:T(8,128)(2,1)S(1)}, u32[]{:S(2)}, u32[]{:S(2)}) collective-permute-start(bf16[4,72,768]{2,1,0:T(8,128)(2,1)S(1)} %all-to-all-done.refs_0_), channel_id=1, source_target_pairs={{0,1},{1,0},{2,3},{3,2},{4,5},{5,4},{6,7},{7,6},{8,9},{9,8},{10,11... | collective-permute-start | bytes 1327112 | tf_op jit(solution)/shard_map/ppermute | solution.py:657
  21.7 15.3 %collective-permute-start.1 = (s32[8,26]{1,0:T(8,128)S(1)}, s32[8,26]{1,0:T(8,128)S(1)}, u32[]{:S(2)}, u32[]{:S(2)}) collective-permute-start(s32[8,26]{1,0:T(8,128)S(1)} %get-tuple-element.45.refs_0_), channel_id=1, source_target_pairs={{0,8},{8,0},{16,24},{24,16},{1,9},{9,1},{17,25},{25,17},{2,10},{10... | collective-permute-start | bytes 2504 | tf_op jit(solution)/shard_map/ppermute | solution.py:657
  23.2 13.8 %collective-permute-start.2 = (s32[8,26]{1,0:T(8,128)S(1)}, s32[8,26]{1,0:T(8,128)S(1)}, u32[]{:S(2)}, u32[]{:S(2)}) collective-permute-start(s32[8,26]{1,0:T(8,128)S(1)} %get-tuple-element.45.refs_0_), channel_id=1, source_target_pairs={{0,16},{8,24},{16,0},{24,8},{1,17},{9,25},{17,1},{25,9},{2,18},{10... | collective-permute-start | bytes 2504 | tf_op jit(solution)/shard_map/ppermute | solution.py:657
  24.7 12.3 %collective-permute-start.3 = (s32[8,26]{1,0:T(8,128)S(1)}, s32[8,26]{1,0:T(8,128)S(1)}, u32[]{:S(2)}, u32[]{:S(2)}) collective-permute-start(s32[8,26]{1,0:T(8,128)S(1)} %get-tuple-element.45.refs_0_), channel_id=1, source_target_pairs={{0,24},{8,16},{16,8},{24,0},{1,25},{9,17},{17,9},{25,1},{2,26},{10... | collective-permute-start | bytes 2504 | tf_op jit(solution)/shard_map/ppermute | solution.py:657
  37.0 12.3 %all-to-all-start.1 = ((bf16[32,2,1408]{2,1,0:T(2,128)(2,1)}), bf16[32,2,1408]{2,1,0:T(2,128)(2,1)S(1)}, u32[]{:S(2)}, u32[]{:S(2)}) async-start(bf16[32,2,1408]{2,1,0:T(2,128)(2,1)} %get-tuple-element.44), calls=%async_computation.1 | async-start | bytes 360448 | tf_op jit(solution)/shard_map/all_to_all | solution.py:753
  42.1 14.2 %collective-permute-start.4 = (bf16[64,768]{1,0:T(8,128)(2,1)S(1)}, bf16[64,768]{1,0:T(8,128)(2,1)S(1)}, u32[]{:S(2)}, u32[]{:S(2)}) collective-permute-start(bf16[64,768]{1,0:T(8,128)(2,1)S(1)} %get-tuple-element.59.refs_0_), channel_id=1, source_target_pairs={{0,8},{8,0},{16,24},{24,16},{1,9},{9,1},{17,25},{25,17},{2,10},{10... | collective-permute-start | bytes 294920 | tf_op jit(solution)/shard_map/ppermute | solution.py:657
  44.0 12.4 %collective-permute-start.5 = (bf16[64,768]{1,0:T(8,128)(2,1)S(1)}, bf16[64,768]{1,0:T(8,128)(2,1)S(1)}, u32[]{:S(2)}, u32[]{:S(2)}) collective-permute-start(bf16[64,768]{1,0:T(8,128)(2,1)S(1)} %get-tuple-element.59.refs_0_), channel_id=1, source_target_pairs={{0,16},{8,24},{16,0},{24,8},{1,17},{9,25},{17,1},{25,9},{2,18},{10... | collective-permute-start | bytes 294920 | tf_op jit(solution)/shard_map/ppermute | solution.py:657
  45.4 11.0 %collective-permute-start.6 = (bf16[64,768]{1,0:T(8,128)(2,1)S(1)}, bf16[64,768]{1,0:T(8,128)(2,1)S(1)}, u32[]{:S(2)}, u32[]{:S(2)}) collective-permute-start(bf16[64,768]{1,0:T(8,128)(2,1)S(1)} %get-tuple-element.59.refs_0_), channel_id=1, source_target_pairs={{0,24},{8,16},{16,8},{24,0},{1,25},{9,17},{17,9},{25,1},{2,26},{10... | collective-permute-start | bytes 294920 | tf_op jit(solution)/shard_map/ppermute | solution.py:657
  56.4 22.3 %all-to-all-start.2 = ((bf16[32,2,3712]{2,1,0:T(2,128)(2,1)}), bf16[32,2,3712]{2,1,0:T(2,128)(2,1)S(1)}, u32[]{:S(2)}, u32[]{:S(2)}) async-start(bf16[32,2,3712]{2,1,0:T(2,128)(2,1)} %bitcast.7), calls=%async_computation.2 | async-start | bytes 950272 | tf_op jit(solution)/shard_map/all_to_all | solution.py:801
  69.3 5.7 %collective-permute-start.7 = (bf16[8,6144]{1,0:T(8,128)(2,1)S(1)}, bf16[8,6144]{1,0:T(8,128)(2,1)S(1)}, u32[]{:S(2)}, u32[]{:S(2)}) collective-permute-start(bf16[8,6144]{1,0:T(8,128)(2,1)S(1)} %get-tuple-element.64), channel_id=1, source_target_pairs={{0,8},{8,0},{16,24},{24,16},{1,9},{9,1},{17,25},{25,17},{2,10},{10... | collective-permute-start | bytes 294920 | tf_op jit(solution)/shard_map/ppermute | solution.py:657
  71.0 6.3 %collective-permute-start.8 = (bf16[8,6144]{1,0:T(8,128)(2,1)S(1)}, bf16[8,6144]{1,0:T(8,128)(2,1)S(1)}, u32[]{:S(2)}, u32[]{:S(2)}) collective-permute-start(bf16[8,6144]{1,0:T(8,128)(2,1)S(1)} %get-tuple-element.65), channel_id=1, source_target_pairs={{0,16},{8,24},{16,0},{24,8},{1,17},{9,25},{17,1},{25,9},{2,18},{10... | collective-permute-start | bytes 294920 | tf_op jit(solution)/shard_map/ppermute | solution.py:657
  72.5 6.2 %collective-permute-start.9 = (bf16[8,6144]{1,0:T(8,128)(2,1)S(1)}, bf16[8,6144]{1,0:T(8,128)(2,1)S(1)}, u32[]{:S(2)}, u32[]{:S(2)}) collective-permute-start(bf16[8,6144]{1,0:T(8,128)(2,1)S(1)} %get-tuple-element.66), channel_id=1, source_target_pairs={{0,24},{8,16},{16,8},{24,0},{1,25},{9,17},{17,9},{25,1},{2,26},{10... | collective-permute-start | bytes 294920 | tf_op jit(solution)/shard_map/ppermute | solution.py:657
  83.9 10.3 %all-to-all-start.3 = ((bf16[8,8,768]{2,1,0:T(8,128)(2,1)}), bf16[8,8,768]{2,1,0:T(8,128)(2,1)S(1)}, u32[]{:S(2)}, u32[]{:S(2)}) async-start(bf16[8,8,768]{2,1,0:T(8,128)(2,1)} %merge.1), calls=%async_computation.3 | async-start | bytes 196608 | tf_op jit(solution)/shard_map/all_to_all | solution.py:842

commit v6 on v4

--- a/solution.py
+++ b/solution.py
@@ -325,18 +325,19 @@
         down = jnp.concatenate([block[:, -ROT // 2 :], block[:, : -ROT // 2]], axis=1)
         turned = block * cos_ref[...] + up * low_ref[...] + down * high_ref[...]
         turned = turned.astype(BF16).astype(F32)
+        firsts = [h * 3 * HD for h in range(period_heads)]
+        asked = [turned[:group, first : first + HD] for first in firsts]
+        keys = [turned[:, first + HD : first + 2 * HD] for first in firsts]
+        queries += asked
+        values += [turned[:group, first + 2 * HD : first + 3 * HD] for first in firsts]
+        products = []
+        for query, key in zip(asked, keys):
+            held_product = key[group:].reshape(group, -1, HD) * query[:, None, :]
+            held_product = held_product.reshape(rows - group, HD)
+            products.append(jnp.concatenate([key[:group] * query, held_product], axis=0))
+        sums = [jnp.sum(product, axis=1, keepdims=True) for product in products]
         for h in range(period_heads):
-            first = h * 3 * HD
-            query = turned[:group, first : first + HD]
-            key = turned[:, first + HD : first + 2 * HD]
-            queries.append(query)
-            values.append(turned[:group, first + 2 * HD : first + 3 * HD])
-            own_product = key[:group] * query
-            held_product = key[group:].reshape(group, -1, HD) * query[:, None, :]
-            product = jnp.concatenate([own_product, held_product.reshape(rows - group, HD)], axis=0)
-            score = jnp.where(
-                head_at == j * period_heads + h, jnp.sum(product, axis=1, keepdims=True), score
-            )
+            score = jnp.where(head_at == j * period_heads + h, sums[h], score)
     score = score * SCALE
     sel = sel_ref[...]
     asked = dot(sel, jnp.concatenate(queries, axis=1).astype(BF16))
@@ -499,7 +500,8 @@
             dense_hbm.at[:, pl.ds(step * cols, cols)], dense_buf.at[step], sems.at[step]
         )
 
-    for step in range(steps):
+    flight = min(5, steps)
+    for step in range(flight):
         dense_copy(step).start()
     for d in range(n_dev):
         rows_ref[2 * d : 2 * d + 2, :] = got_ref[d, :, : head_lanes + extra].astype(F32)
@@ -525,17 +527,19 @@
     totals = jnp.zeros((group, 128), F32)
     for part in parts_of(weights, 3):
         totals = totals + dot(back, part)
-    inverse = 1.0 / totals
     lanes, heads_of = iota((128, head_lanes), 1), iota((128, head_lanes), 0)
     over = lanes - heads_of * HD
     spread = jnp.where((over >= 0) & (over < HD), 1.0, 0.0).astype(BF16)
     weighted = split_dot(weights, spread, 2) * rows_ref[:, :head_lanes]
+    inverse = split_dot(1.0 / totals, spread, 3)
     mixed = jnp.zeros((group, head_lanes), F32)
     for part in parts_of(weighted, 2):
         mixed = mixed + dot(back, part)
-    attended = (mixed * split_dot(inverse, spread, 3)).astype(BF16)
+    attended = (mixed * inverse).astype(BF16)
     for step in range(steps):
         dense_copy(step).wait()
+        if step + flight < steps:
+            dense_copy(step + flight).start()
         some = slice(step * cols, (step + 1) * cols)
         result = dot(attended, dense_buf[step])
         for share_ref in share_refs:
@@ -564,7 +568,7 @@
         )
 
     copies = [in_copy(step) for step in range(n_blk)] + [out_copy(step) for step in range(n_steps)]
-    flight = 4
+    flight = 6
     for copy in copies[:flight]:
         copy.start()
 
@@ -710,7 +714,7 @@
     dests = STEP_HEADS // heads
     fold_width = 2 * head_lanes
 
-    pack, cosine = lax.optimization_barrier((pack, cosine))
+    pack, cosine, *numbers = lax.optimization_barrier((pack, cosine, *numbers))
     packs = [pack, swapped(pack, "blk", n_blk, 1)]
 
     wire = lanes + wire_split(lanes)

time: 94.7 us -> 92.9 us (0.981)
  waiting for transfers between devices: 22.6 us -> 20.8 us
    all_to_all x1, waiting for transfers between devices: 10.7 us -> 4.09 us  [on_device(): lax.all_to_all(pack, 'blk', 0, 0, axis_index_groups=[list(range(core, n_b...]
    ppermute x10, waiting for transfers between devices: 5.96 us -> 10.8 us  [swapped(): return lax.ppermute(array, axis, [(i, i ^ by) for i in range(size)])]
  transfers between devices with their start and end apart: 14 -> 14, of which waited for: 6 -> 10; matrix products, arithmetic and copies ran while one was open for 0% -> 0% of each run, Pallas kernels for 35% -> 23%
where the time goes in v6:
time: 92.9 us; the launch traced here: 92.4 us
  Pallas kernels  40.5 us (44%)
  starting transfers between devices  29.7 us (32%)
  waiting for transfers between devices  20.8 us (22%)
    pallas_call x1, Pallas kernels, on_device(): pl.pallas_call(functools.partial(project_kernel, (group, n_blk, held_rows...  11.7 us
    ppermute x10, waiting for transfers between devices, swapped(): return lax.ppermute(array, axis, [(i, i ^ by) for i in range(size)])  10.8 us
    ppermute x10, starting transfers between devices, swapped(): return lax.ppermute(array, axis, [(i, i ^ by) for i in range(size)])  10.7 us
    pallas_call x1, Pallas kernels, on_device(): pl.pallas_call(functools.partial(mlp_kernel, (group, n_pages, n_blk)), in...  7.62 us
    pallas_call x1, Pallas kernels, on_device(): pl.pallas_call(functools.partial(attend_kernel, (n_pages, slots, dests, h...  6.33 us
    all_to_all x1, starting transfers between devices, on_device(): lax.all_to_all(pack, 'blk', 0, 0, axis_index_groups=[list(range(core, n_b...  6.32 us
    pallas_call x1, Pallas kernels, on_device(): pl.pallas_call(functools.partial(merge_kernel, (group, n_dev, heads, n_pa...  5.44 us
    all_to_all x1, waiting for transfers between devices, on_device(): out_got = lax.all_to_all(out_part, 'blk', 0, 0, tiled=True)  5.14 us
  transfers between devices with their start and end apart: 14, of which 10 were waited for; matrix products, arithmetic and copies ran while one was open for 0% of the time, Pallas kernels for 23%

profile of v6, /device:TPU:0, one launch (start us, length us, event | category | flops | bytes accessed | tf_op | source)
XLA Modules:
  0.0 92.4 jit_solution(5172115089887961128)
XLA Ops:
  0.6 2.0 %pack.1 = bf16[4,72,768]{2,1,0:T(8,128)(2,1)} custom-call(bf16[8,6144]{1,0:T(8,128)(2,1)} %bitcast.15, bf16[8,768]{1,0:T(8,128)(2,1)} %new_ref.1, f32[1,6144]{1,0:T(1,128)} %bitcast.13), custom_call_target="tpu_custom_call" | custom-call | tf_op jit(solution)/shard_map/pack/pallas_call | solution.py:658
  2.6 6.3 %all-to-all-start = ((bf16[4,72,768]{2,1,0:T(8,128)(2,1)}), bf16[4,72,768]{2,1,0:T(8,128)(2,1)S(1)}, u32[]{:S(2)}, u32[]{:S(2)}) async-start(bf16[4,72,768]{2,1,0:T(8,128)(2,1)} %pack.1), calls=%async_computation | async-start | bytes 884736 | tf_op jit(solution)/shard_map/all_to_all | solution.py:666
  8.9 2.0 %prep.1 = (f32[2,6144]{1,0:T(2,128)S(1)}, f32[72,1152]{1,0:T(8,128)S(1)}, f32[72,1152]{1,0:T(8,128)S(1)}, f32[72,1152]{1,0:T(8,128)S(1)}, bf16[96,8]{1,0:T(8,128...) custom-call(s32[12,32]{1,0:T(8,128)} %bitcast.16, ...), custom_call_target="tpu_custom_call" | custom-call | tf_op jit(solution)/shard_map/prep/pallas_call | solution.py:680
  10.9 2.5 %collective-permute-start.2 = (s32[8,26]{1,0:T(8,128)S(1)}, s32[8,26]{1,0:T(8,128)S(1)}, u32[]{:S(2)}, u32[]{:S(2)}) collective-permute-start(s32[8,26]{1,0:T(8,128)S(1)} %get-tuple-element.53.refs_0_), channel_id=1, source_target_pairs={{0,24},{8,16},{16,8},{24,0},{1,25},{9,17},{17,9},{25,1},{2,26},{10... | collective-permute-start | bytes 2504 | tf_op jit(solution)/shard_map/ppermute | solution.py:652
  13.5 0.5 collective-permute-start.1
  14.0 0.5 collective-permute-start
  14.5 1.0 %collective-permute-done.2.refs_3_ = s32[8,26]{1,0:T(8,128)S(1)} collective-permute-done((s32[8,26]{1,0:T(8,128)S(1)}, s32[8,26]{1,0:T(8,128)S(1)}, u32[]{:S(2)}, u32[]{:S(2)}) %collective-permute-start.2) | collective-permute-done | bytes 864 | tf_op jit(solution)/shard_map/ppermute | solution.py:652
  15.5 1.5 %collective-permute-done.1.refs_2_ = s32[8,26]{1,0:T(8,128)S(1)} collective-permute-done((s32[8,26]{1,0:T(8,128)S(1)}, s32[8,26]{1,0:T(8,128)S(1)}, u32[]{:S(2)}, u32[]{:S(2)}) %collective-permute-start.1) | collective-permute-done | bytes 864 | tf_op jit(solution)/shard_map/ppermute | solution.py:652
  17.1 0.5 collective-permute-done.refs_1_
  17.6 4.1 %all-to-all-done.refs_0_ = bf16[4,72,768]{2,1,0:T(8,128)(2,1)S(1)} async-done(((bf16[4,72,768]{2,1,0:T(8,128)(2,1)}), bf16[4,72,768]{2,1,0:T(8,128)(2,1)S(1)}, u32[]{:S(2)}, u32[]{:S(2)}) %all-to-all-start) | async-done | bytes 442400 | tf_op jit(solution)/shard_map/all_to_all | solution.py:666
  21.7 1.8 %collective-permute-done.3.refs_1_ = bf16[4,72,768]{2,1,0:T(8,128)(2,1)S(1)} collective-permute-done((bf16[4,72,768]{2,1,0:T(8,128)(2,1)S(1)}, bf16[4,72,768]{2,1,0:T(8,128)(2,1)S(1)}, u32[]{:S(2)}, u32[]{:S(2)}) %collective-permute-start.3) | collective-permute-done | bytes 442400 | tf_op jit(solution)/shard_map/ppermute | solution.py:652
  23.5 11.7 %project.1 = (bf16[32,2,1408]{2,1,0:T(2,128)(2,1)}, bf16[8,896]{1,0:T(8,128)(2,1)S(1)}, bf16[64,768]{1,0:T(8,128)(2,1)S(1)}) custom-call(bf16[4,72,768]{2,1,0:T(8,128)(2,1)S(1)} %all-to-all-done.refs_0_, bf16[4,72,768]{2,1,0:T(8,128)(2,1)S(1)} %collective-permute-done.3.refs_1_, f32[2,6144]{1,0:T(2,128)S(1)} %get-tuple-element.42.refs_2_, ...), custom_call_target="tpu_custom_call" | custom-call | flops 2038431744 | bytes 28311552 | tf_op jit(solution)/shard_map/project/pallas_call | solution.py:721
  35.1 3.7 %all-to-all-start.1 = ((bf16[32,2,1408]{2,1,0:T(2,128)(2,1)}), bf16[32,2,1408]{2,1,0:T(2,128)(2,1)S(1)}, u32[]{:S(2)}, u32[]{:S(2)}) async-start(bf16[32,2,1408]{2,1,0:T(2,128)(2,1)} %get-tuple-element.52), calls=%async_computation.1 | async-start | bytes 360448 | tf_op jit(solution)/shard_map/all_to_all | solution.py:749
  38.9 1.4 %facts.1 = (f32[16,192]{1,0:T(8,128)S(1)}, f32[208,128]{1,0:T(8,128)S(1)}, bf16[208,128]{1,0:T(8,128)(2,1)S(1)}) custom-call(s32[8,26]{1,0:T(8,128)S(1)} %get-tuple-element.53.refs_0_, s32[8,26]{1,0:T(8,128)S(1)} %collective-permute-done.refs_1_, s32[8,26]{1,0:T(8,128)S(1)} %collective-permute-done.1.refs_2_, s32[8,26]{1,0:T(8,128)S(1)} %collective-permute-done.2.refs_3_, ...), custom_call_target="tpu_custom_call" | custom-call | tf_op jit(solution)/shard_map/facts/pallas_call | solution.py:750
  40.3 2.7 %collective-permute-start.6 = (bf16[64,768]{1,0:T(8,128)(2,1)S(1)}, bf16[64,768]{1,0:T(8,128)(2,1)S(1)}, u32[]{:S(2)}, u32[]{:S(2)}) collective-permute-start(bf16[64,768]{1,0:T(8,128)(2,1)S(1)} %get-tuple-element.67.refs_0_), channel_id=1, source_target_pairs={{0,24},{8,16},{16,8},{24,0},{1,25},{9,17},{17,9},{25,1},{2,26},{10... | collective-permute-start | bytes 294920 | tf_op jit(solution)/shard_map/ppermute | solution.py:652
  43.0 0.6 collective-permute-start.5
  43.5 0.3 collective-permute-start.4
  43.8 2.8 %fold.1.fold_ref = bf16[16,12288]{1,0:T(8,128)(2,1)S(1)} custom-call(f32[16,192]{1,0:T(8,128)S(1)} %get-tuple-element.61.weight_ref, bf16[192,12288]{1,0:T(8,128)(2,1)} %bitcast.10), custom_call_target="tpu_custom_call" | custom-call | tf_op jit(solution)/shard_map/fold/pallas_call | solution.py:767
  46.7 0.8 all-to-all-done.1
  47.5 6.3 %attend.1.refs_6_ = bf16[4,8,2,3712]{3,2,1,0:T(2,128)(2,1)} custom-call(bf16[4,8,2,1408]{3,2,1,0:T(2,128)(2,1)S(1)} %bitcast.9, f32[208,128]{1,0:T(8,128)S(1)} %get-tuple-element.57.valid_ref, bf16[208,128]{1,0:T(8,128)(2,1)S(1)} %get-tuple-element.58.place_ref, bf16[192,12288]{1,0:T(8,128)(2,1)} %bitcast.11, bf16[16,12288]{1,0:T(8,128)(2,1)S(1)} %fold.1.fold_ref), custom_call_target="tpu_custom_call" | custom-call | flops 603979776 | bytes 4718592 | tf_op jit(solution)/shard_map/attend/pallas_call | solution.py:783
  53.8 5.1 %all-to-all-start.2 = ((bf16[32,2,3712]{2,1,0:T(2,128)(2,1)}), bf16[32,2,3712]{2,1,0:T(2,128)(2,1)S(1)}, u32[]{:S(2)}, u32[]{:S(2)}) async-start(bf16[32,2,3712]{2,1,0:T(2,128)(2,1)} %bitcast.7), calls=%async_computation.2 | async-start | bytes 950272 | tf_op jit(solution)/shard_map/all_to_all | solution.py:800
  58.9 7.6 %mlp.1 = (bf16[8,6144]{1,0:T(8,128)(2,1)S(1)}, bf16[8,6144]{1,0:T(8,128)(2,1)S(1)}, bf16[8,6144]{1,0:T(8,128)(2,1)S(1)}, bf16[8,6144]{1,0:T(8,128)(2,1)S(1)}) custom-call(bf16[64,768]{1,0:T(8,128)(2,1)S(1)} %get-tuple-element.67.refs_0_, bf16[64,768]{1,0:T(8,128)(2,1)S(1)} %collective-permute-done.4.refs_1_, ...), custom_call_target="tpu_custom_call" | custom-call | flops 603979776 | bytes 18874368 | tf_op jit(solution)/shard_map/mlp/pallas_call | solution.py:803
  66.5 1.8 %collective-permute-start.7 = (bf16[8,6144]{1,0:T(8,128)(2,1)S(1)}, bf16[8,6144]{1,0:T(8,128)(2,1)S(1)}, u32[]{:S(2)}, u32[]{:S(2)}) collective-permute-start(bf16[8,6144]{1,0:T(8,128)(2,1)S(1)} %get-tuple-element.72), channel_id=1, source_target_pairs={{0,8},{8,0},{16,24},{24,16},{1,9},{9,1},{17,25},{25,17},{2,10},{10... | collective-permute-start | bytes 294920 | tf_op jit(solution)/shard_map/ppermute | solution.py:652
  68.3 1.5 %collective-permute-start.8 = (bf16[8,6144]{1,0:T(8,128)(2,1)S(1)}, bf16[8,6144]{1,0:T(8,128)(2,1)S(1)}, u32[]{:S(2)}, u32[]{:S(2)}) collective-permute-start(bf16[8,6144]{1,0:T(8,128)(2,1)S(1)} %get-tuple-element.73), channel_id=1, source_target_pairs={{0,16},{8,24},{16,0},{24,8},{1,17},{9,25},{17,1},{25,9},{2,18},{10... | collective-permute-start | bytes 294920 | tf_op jit(solution)/shard_map/ppermute | solution.py:652
  70.1 2.4 %collective-permute-done.7.refs_1_ = bf16[8,6144]{1,0:T(8,128)(2,1)S(1)} collective-permute-done((bf16[8,6144]{1,0:T(8,128)(2,1)S(1)}, bf16[8,6144]{1,0:T(8,128)(2,1)S(1)}, u32[]{:S(2)}, u32[]{:S(2)}) %collective-permute-start.7) | collective-permute-done | bytes 98336 | tf_op jit(solution)/shard_map/ppermute | solution.py:652
  72.4 2.3 %collective-permute-done.8.refs_2_ = bf16[8,6144]{1,0:T(8,128)(2,1)S(1)} collective-permute-done((bf16[8,6144]{1,0:T(8,128)(2,1)S(1)}, bf16[8,6144]{1,0:T(8,128)(2,1)S(1)}, u32[]{:S(2)}, u32[]{:S(2)}) %collective-permute-start.8) | collective-permute-done | bytes 98336 | tf_op jit(solution)/shard_map/ppermute | solution.py:652
  74.7 1.3 %collective-permute-done.9.refs_3_ = bf16[8,6144]{1,0:T(8,128)(2,1)S(1)} collective-permute-done((bf16[8,6144]{1,0:T(8,128)(2,1)S(1)}, bf16[8,6144]{1,0:T(8,128)(2,1)S(1)}, u32[]{:S(2)}, u32[]{:S(2)}) %collective-permute-start.9) | collective-permute-done | bytes 98336 | tf_op jit(solution)/shard_map/ppermute | solution.py:652
  76.0 5.4 %merge.1 = bf16[8,8,768]{2,1,0:T(8,128)(2,1)} custom-call(bf16[32,2,3712]{2,1,0:T(2,128)(2,1)S(1)} %all-to-all-done.2.got_ref, bf16[8,896]{1,0:T(8,128)(2,1)S(1)} %get-tuple-element.64.own_ref, f32[104,8]{1,0:T(8,128)S(1)} %get-tuple-element.65.sel_ref, bf16[8,104]{1,0:T(8,128)(2,1)S(1)} %get-tuple-element.66.back_ref, ...), custom_call_target="tpu_custom_call" | custom-call | flops 75497472 | bytes 9437184 | tf_op jit(solution)/shard_map/merge/pallas_call | solution.py:820
  81.5 4.0 %all-to-all-start.3 = ((bf16[8,8,768]{2,1,0:T(8,128)(2,1)}), bf16[8,8,768]{2,1,0:T(8,128)(2,1)S(1)}, u32[]{:S(2)}, u32[]{:S(2)}) async-start(bf16[8,8,768]{2,1,0:T(8,128)(2,1)} %merge.1), calls=%async_computation.3 | async-start | bytes 196608 | tf_op jit(solution)/shard_map/all_to_all | solution.py:841
  85.4 1.2 %place.1 = bf16[12,8,1536]{2,1,0:T(8,128)(2,1)} custom-call(bf16[96,96]{1,0:T(8,128)(2,1)S(1)} %get-tuple-element.75.pick_ref, bf16[32,2,3712]{2,1,0:T(2,128)(2,1)S(1)} %all-to-all-done.2.got_ref), custom_call_target="tpu_custom_call" | custom-call | bytes 589824 | tf_op jit(solution)/shard_map/place/pallas_call | solution.py:844
  86.6 5.1 %all-to-all-done.3 = bf16[8,8,768]{2,1,0:T(8,128)(2,1)S(1)} async-done(((bf16[8,8,768]{2,1,0:T(8,128)(2,1)}), bf16[8,8,768]{2,1,0:T(8,128)(2,1)S(1)}, u32[]{:S(2)}, u32[]{:S(2)}) %all-to-all-start.3) | async-done | bytes 98336 | tf_op jit(solution)/shard_map/all_to_all | solution.py:841
  91.8 0.6 reduce_sum.12
  (6 shorter events, 0.3 us)
Async XLA Ops:
  2.6 19.1 %all-to-all-start = ((bf16[4,72,768]{2,1,0:T(8,128)(2,1)}), bf16[4,72,768]{2,1,0:T(8,128)(2,1)S(1)}, u32[]{:S(2)}, u32[]{:S(2)}) async-start(bf16[4,72,768]{2,1,0:T(8,128)(2,1)} %pack.1), calls=%async_computation | async-start | bytes 884736 | tf_op jit(solution)/shard_map/all_to_all | solution.py:666
  10.9 4.6 %collective-permute-start.2 = (s32[8,26]{1,0:T(8,128)S(1)}, s32[8,26]{1,0:T(8,128)S(1)}, u32[]{:S(2)}, u32[]{:S(2)}) collective-permute-start(s32[8,26]{1,0:T(8,128)S(1)} %get-tuple-element.53.refs_0_), channel_id=1, source_target_pairs={{0,24},{8,16},{16,8},{24,0},{1,25},{9,17},{17,9},{25,1},{2,26},{10... | collective-permute-start | bytes 2504 | tf_op jit(solution)/shard_map/ppermute | solution.py:652
  13.5 3.6 %collective-permute-start.1 = (s32[8,26]{1,0:T(8,128)S(1)}, s32[8,26]{1,0:T(8,128)S(1)}, u32[]{:S(2)}, u32[]{:S(2)}) collective-permute-start(s32[8,26]{1,0:T(8,128)S(1)} %get-tuple-element.53.refs_0_), channel_id=1, source_target_pairs={{0,16},{8,24},{16,0},{24,8},{1,17},{9,25},{17,1},{25,9},{2,18},{10... | collective-permute-start | bytes 2504 | tf_op jit(solution)/shard_map/ppermute | solution.py:652
  14.0 3.6 %collective-permute-start = (s32[8,26]{1,0:T(8,128)S(1)}, s32[8,26]{1,0:T(8,128)S(1)}, u32[]{:S(2)}, u32[]{:S(2)}) collective-permute-start(s32[8,26]{1,0:T(8,128)S(1)} %get-tuple-element.53.refs_0_), channel_id=1, source_target_pairs={{0,8},{8,0},{16,24},{24,16},{1,9},{9,1},{17,25},{25,17},{2,10},{10... | collective-permute-start | bytes 2504 | tf_op jit(solution)/shard_map/ppermute | solution.py:652
  21.7 1.8 %collective-permute-start.3 = (bf16[4,72,768]{2,1,0:T(8,128)(2,1)S(1)}, bf16[4,72,768]{2,1,0:T(8,128)(2,1)S(1)}, u32[]{:S(2)}, u32[]{:S(2)}) collective-permute-start(bf16[4,72,768]{2,1,0:T(8,128)(2,1)S(1)} %all-to-all-done.refs_0_), channel_id=1, source_target_pairs={{0,1},{1,0},{2,3},{3,2},{4,5},{5,4},{6,7},{7,6},{8,9},{9,8},{10,11... | collective-permute-start | bytes 1327112 | tf_op jit(solution)/shard_map/ppermute | solution.py:652
  35.1 12.3 %all-to-all-start.1 = ((bf16[32,2,1408]{2,1,0:T(2,128)(2,1)}), bf16[32,2,1408]{2,1,0:T(2,128)(2,1)S(1)}, u32[]{:S(2)}, u32[]{:S(2)}) async-start(bf16[32,2,1408]{2,1,0:T(2,128)(2,1)} %get-tuple-element.52), calls=%async_computation.1 | async-start | bytes 360448 | tf_op jit(solution)/shard_map/all_to_all | solution.py:749
  40.3 13.5 %collective-permute-start.6 = (bf16[64,768]{1,0:T(8,128)(2,1)S(1)}, bf16[64,768]{1,0:T(8,128)(2,1)S(1)}, u32[]{:S(2)}, u32[]{:S(2)}) collective-permute-start(bf16[64,768]{1,0:T(8,128)(2,1)S(1)} %get-tuple-element.67.refs_0_), channel_id=1, source_target_pairs={{0,24},{8,16},{16,8},{24,0},{1,25},{9,17},{17,9},{25,1},{2,26},{10... | collective-permute-start | bytes 294920 | tf_op jit(solution)/shard_map/ppermute | solution.py:652
  43.0 10.8 %collective-permute-start.5 = (bf16[64,768]{1,0:T(8,128)(2,1)S(1)}, bf16[64,768]{1,0:T(8,128)(2,1)S(1)}, u32[]{:S(2)}, u32[]{:S(2)}) collective-permute-start(bf16[64,768]{1,0:T(8,128)(2,1)S(1)} %get-tuple-element.67.refs_0_), channel_id=1, source_target_pairs={{0,16},{8,24},{16,0},{24,8},{1,17},{9,25},{17,1},{25,9},{2,18},{10... | collective-permute-start | bytes 294920 | tf_op jit(solution)/shard_map/ppermute | solution.py:652
  43.5 10.2 %collective-permute-start.4 = (bf16[64,768]{1,0:T(8,128)(2,1)S(1)}, bf16[64,768]{1,0:T(8,128)(2,1)S(1)}, u32[]{:S(2)}, u32[]{:S(2)}) collective-permute-start(bf16[64,768]{1,0:T(8,128)(2,1)S(1)} %get-tuple-element.67.refs_0_), channel_id=1, source_target_pairs={{0,8},{8,0},{16,24},{24,16},{1,9},{9,1},{17,25},{25,17},{2,10},{10... | collective-permute-start | bytes 294920 | tf_op jit(solution)/shard_map/ppermute | solution.py:652
  53.8 22.2 %all-to-all-start.2 = ((bf16[32,2,3712]{2,1,0:T(2,128)(2,1)}), bf16[32,2,3712]{2,1,0:T(2,128)(2,1)S(1)}, u32[]{:S(2)}, u32[]{:S(2)}) async-start(bf16[32,2,3712]{2,1,0:T(2,128)(2,1)} %bitcast.7), calls=%async_computation.2 | async-start | bytes 950272 | tf_op jit(solution)/shard_map/all_to_all | solution.py:800
  66.5 5.9 %collective-permute-start.7 = (bf16[8,6144]{1,0:T(8,128)(2,1)S(1)}, bf16[8,6144]{1,0:T(8,128)(2,1)S(1)}, u32[]{:S(2)}, u32[]{:S(2)}) collective-permute-start(bf16[8,6144]{1,0:T(8,128)(2,1)S(1)} %get-tuple-element.72), channel_id=1, source_target_pairs={{0,8},{8,0},{16,24},{24,16},{1,9},{9,1},{17,25},{25,17},{2,10},{10... | collective-permute-start | bytes 294920 | tf_op jit(solution)/shard_map/ppermute | solution.py:652
  68.3 6.3 %collective-permute-start.8 = (bf16[8,6144]{1,0:T(8,128)(2,1)S(1)}, bf16[8,6144]{1,0:T(8,128)(2,1)S(1)}, u32[]{:S(2)}, u32[]{:S(2)}) collective-permute-start(bf16[8,6144]{1,0:T(8,128)(2,1)S(1)} %get-tuple-element.73), channel_id=1, source_target_pairs={{0,16},{8,24},{16,0},{24,8},{1,17},{9,25},{17,1},{25,9},{2,18},{10... | collective-permute-start | bytes 294920 | tf_op jit(solution)/shard_map/ppermute | solution.py:652
  69.8 6.2 %collective-permute-start.9 = (bf16[8,6144]{1,0:T(8,128)(2,1)S(1)}, bf16[8,6144]{1,0:T(8,128)(2,1)S(1)}, u32[]{:S(2)}, u32[]{:S(2)}) collective-permute-start(bf16[8,6144]{1,0:T(8,128)(2,1)S(1)} %get-tuple-element.74), channel_id=1, source_target_pairs={{0,24},{8,16},{16,8},{24,0},{1,25},{9,17},{17,9},{25,1},{2,26},{10... | collective-permute-start | bytes 294920 | tf_op jit(solution)/shard_map/ppermute | solution.py:652
  81.5 10.3 %all-to-all-start.3 = ((bf16[8,8,768]{2,1,0:T(8,128)(2,1)}), bf16[8,8,768]{2,1,0:T(8,128)(2,1)S(1)}, u32[]{:S(2)}, u32[]{:S(2)}) async-start(bf16[8,8,768]{2,1,0:T(8,128)(2,1)} %merge.1), calls=%async_computation.3 | async-start | bytes 196608 | tf_op jit(solution)/shard_map/all_to_all | solution.py:841
